TPU v7x, 32 devices: a whole 2x2x4 slice. The times are simulated.
32 devices in a mesh: groups: 2 (over y), rows: 4 (over z), feat: 4 (over x, core).
Axes of the slice: x: 2, y: 2, z: 4, core: 2. Of those that a mesh axis runs over, the one named last changes fastest.
Arguments:
- daily_unit_counts: bfloat16 [8192, 512], P(('groups', 'rows')), parts along dimension 0, may hold values from 0.099609375 to 20
- region_ids: int32 [8192], P(('groups', 'rows')), parts along dimension 0, may hold values from 0 to 9
- node_ids: int32 [8192], P(('groups', 'rows')), parts along dimension 0, may hold values from 0 to 31
- bin_ids: int32 [8192, 512], P(('groups', 'rows'), 'feat'), parts along dimension 0, may hold values from 0 to 255
- quant_index: int32 [2], P('groups'), parts along dimension 0, may hold values from 0 to 8
- filter_kernels: float32 [8, 4], replicated, may hold values from -3 to 3
Outputs:
- histogram: float32 [8, 4, 32, 2, 32, 256], P(('groups', 'feat'), 'rows'), parts along dimension 0
- feature_best: float32 [8, 4, 32, 32], P('groups'), parts along dimension 0
There are 2 independent parts, one for each index of `groups`. A program takes and returns all parts, laid end to end along the dimension named above; an argument that names none is the same for every part. Nothing has to cross between parts.
All inputs are finite; a program needn't handle non-finite values.
Results may differ from a plain program's by a relative error of at most 0.0071.
Values may be sent and summed in bfloat16 or wider, within the bound.
No kernel may reach another device: no remote copies, remote signals or barrier semaphores. Data moves between devices by JAX's collectives and lax.ppermute only.
A program may use at most 64 MiB of HBM per device.

v0:
```python
import math

import jax
import jax.numpy as jnp
from jax import lax
from jax.sharding import PartitionSpec as P

BINS = 256
NODES = 32
HIST = 512
HORIZON_LENGTH = 28
REGIONS = 10
CHANNELS = 8
TAPS = 4


DILATE = (1, 7, 14, 28)
LEVELS = (0.005, 0.025, 0.165, 0.25, 0.5, 0.75, 0.835, 0.975, 0.995)
SOFT_SPAN = 0.5
RIDGE_TERM = 1.0


def gradients(daily_unit_counts, region_ids, node_ids, quant_index, filter_kernels, totals):
    sales_wide = daily_unit_counts.astype(jnp.float32)
    series_level = jnp.mean(sales_wide, axis=1)
    own_scaled = sales_wide / series_level[:, None]
    region_scale = jnp.mean(totals, axis=1) + 1.0
    shared = totals / region_scale[:, None]
    region_pick = (region_ids[:, None] == jnp.arange(REGIONS)[None, :]).astype(jnp.float32)
    regional = jnp.dot(
        region_pick, shared, precision=lax.Precision.HIGHEST, preferred_element_type=jnp.float32
    )
    first_day = HIST - HORIZON_LENGTH
    predicted_demand = jnp.zeros((daily_unit_counts.shape[0], HORIZON_LENGTH), jnp.float32)
    for lane_number in range(CHANNELS):
        input_entries = own_scaled if lane_number % 2 == 0 else regional
        stride = DILATE[lane_number // 2 % 4]
        for lag_offset in range(TAPS):
            opening_period = first_day - 1 - lag_offset * stride
            predicted_demand = (
                predicted_demand
                + filter_kernels[lane_number, lag_offset]
                * input_entries[:, opening_period : opening_period + HORIZON_LENGTH]
            )
    observed_demand = own_scaled[:, first_day:]
    levels_table = jnp.array(LEVELS, jnp.float32)
    quantile = jnp.sum(jnp.where(jnp.arange(9) == quant_index[0], levels_table, 0.0))
    quantile_level = jax.nn.sigmoid((predicted_demand - observed_demand) / SOFT_SPAN)
    gradient = jnp.mean(quantile_level - quantile, axis=1)
    hessian = jnp.mean(quantile_level * (1.0 - quantile_level), axis=1) / SOFT_SPAN
    member = (node_ids[:, None] == jnp.arange(NODES)[None, :]).astype(jnp.float32)
    columns = jnp.concatenate([gradient[:, None] * member, hessian[:, None] * member], axis=1)
    return columns.astype(jnp.bfloat16)


def split_gains(histogram):
    left_sums = jnp.cumsum(histogram, axis=-1)[..., :-1]
    totals = jnp.sum(histogram, axis=-1, keepdims=True)
    right_sums = totals - left_sums
    left_grad = left_sums[..., 0, :, :]
    left_hess = left_sums[..., 1, :, :]
    right_grad = right_sums[..., 0, :, :]
    right_hess = right_sums[..., 1, :, :]
    all_grad = totals[..., 0, :, :]
    all_hess = totals[..., 1, :, :]
    split_gain = (
        left_grad * left_grad / (left_hess + RIDGE_TERM)
        + right_grad * right_grad / (right_hess + RIDGE_TERM)
        - all_grad * all_grad / (all_hess + RIDGE_TERM)
    )
    return jnp.max(split_gain, axis=-1)


def encode_bins(chosen):
    onehot = chosen[:, :, None] == jnp.arange(BINS)[None, None, :]
    return onehot.astype(jnp.bfloat16).reshape(chosen.shape[0], chosen.shape[1] * BINS)


def shards(daily_unit_counts, region_ids, node_ids, bin_ids, quant_index, filter_kernels):
    region_pick = (region_ids[:, None] == jnp.arange(REGIONS)[None, :]).astype(jnp.bfloat16)
    partial_value = lax.dot_general(
        region_pick, daily_unit_counts, (((0,), (0,)), ((), ())), preferred_element_type=jnp.float32
    )
    totals = lax.psum(partial_value, "rows")
    columns = gradients(
        daily_unit_counts, region_ids, node_ids, quant_index, filter_kernels, totals
    )
    width_cols = columns.shape[1]
    shard_feats = bin_ids.shape[1] // lax.axis_size("rows")
    block_size = math.gcd(shard_feats * lax.axis_size("rows"), 4)

    def one_block(block_index):
        chosen = lax.dynamic_slice_in_dim(bin_ids, block_index * block_size, block_size, 1)
        product = lax.dot_general(
            columns,
            encode_bins(chosen),
            (((0,), (0,)), ((), ())),
            preferred_element_type=jnp.float32,
        )
        return product.reshape(width_cols, block_size, BINS).transpose(1, 0, 2)

    blocks = lax.map(
        one_block, jnp.arange(shard_feats * lax.axis_size("rows") // block_size, dtype=jnp.int32)
    )
    histogram = lax.psum_scatter(
        blocks.reshape(shard_feats * lax.axis_size("rows"), 2, NODES, BINS),
        "rows",
        scatter_dimension=0,
        tiled=True,
    )
    local_best = split_gains(histogram)
    row_count = lax.axis_size("rows")
    feat_count = lax.axis_size("feat")
    gathered = lax.all_gather(local_best[None], ("rows", "feat"), axis=0, tiled=True)
    feature_best = gathered.reshape(row_count, feat_count, shard_feats, NODES).transpose(1, 0, 2, 3)
    return (histogram.reshape(1, 1, shard_feats, 2, NODES, BINS), feature_best)


def solution(mesh):
    in_specs = (
        P(("groups", "rows"), None),
        P(("groups", "rows")),
        P(("groups", "rows")),
        P(("groups", "rows"), "feat"),
        P("groups"),
        P(),
    )
    out_specs = (
        P(("groups", "feat"), "rows", None, None, None, None),
        P("groups", None, None, None),
    )
    return jax.shard_map(shards, mesh=mesh, in_specs=in_specs, out_specs=out_specs, check_vma=False)
```

profile of v0, /device:TPU:0, one launch (start us, length us, event | category | flops | bytes accessed | tf_op | source)
XLA Modules:
  0.0 529.4 jit_solution(4698802312560577882)
XLA Ops:
  15.0 20.9 %psum.7 = f32[10,512]{1,0:T(8,128)S(1)} all-reduce(f32[10,512]{1,0:T(8,128)S(1)} %fusion.13), channel_id=1, replica_groups=mesh['groups'=2,'rows'=4,'feat'=4] {'rows'}, use_global_device_ids=true, to_apply=%region_1.0 | all-reduce | flops 5120 | bytes 40960 | tf_op jit(solution)/shard_map/psum | solution.py:84
  36.0 2.5 fusion.12
  39.8 22.6 %subtract_reduce_fusion = (f32[1024]{0:T(1024)S(1)}, f32[1024]{0:T(1024)S(1)}) fusion(f32[]{:T(128)} %fusion.58, f32[1024,512]{0,1:T(8,128)S(1)} %copy-done.2, f32[1024,512]{0,1:T(8,128)} %fusion.12, f32[]{:T(128)} %bitcast.35, f32[]{:T(128)} %bitcast.34, f32[]{:T(128)} %bitcast.33, f32[]{:T(128)} %bitcast.32, f32[]{:T(128)} %bitcast.31, f32[]{:T(128)} %bitcast.30, ...), kind=kLoop, calls=%fused_computation.87 | loop fusion | flops 2091008 | bytes 2646148 | tf_op jit(solution)/shard_map/reduce_sum | solution.py:49
  63.1 216.6 %while.10 = (s32[]{:T(128)}, f32[32,4,64,256]{3,2,1,0:T(8,128)}, s32[32]{0:T(128)S(1)}, s32[1024,128]{1,0:T(8,128)S(1)}, bf16[1024,64]{1,0:T(8,128)(2,1)S(1)}, /...) while((s32[]{:T(128)}, f32[32,4,64,256]{3,2,1,0:T(8,128)}, s32[32]{0:T(128)S(1)}, ...), condition=%wide.region_7.8_spmd, body=%wide.region_6.7_spmd.sunk | while | flops 135266304 | bytes 18285212 | solution.py:102
  64.6 2.5 eq.115
  71.3 2.5 eq.115
  78.1 2.5 eq.115
  84.9 2.5 eq.115
  91.6 2.5 eq.115
  98.4 2.5 eq.115
  105.2 2.5 eq.115
  112.0 2.5 eq.115
  118.7 2.5 eq.115
  125.5 2.5 eq.115
  132.3 2.5 eq.115
  139.0 2.5 eq.115
  145.8 2.5 eq.115
  152.6 2.5 eq.115
  159.4 2.5 eq.115
  166.1 2.5 eq.115
  172.9 2.5 eq.115
  179.6 2.5 eq.115
  186.4 2.5 eq.115
  193.2 2.5 eq.115
  200.0 2.5 eq.115
  206.7 2.5 eq.115
  227.0 2.5 eq.115
  274.4 2.5 eq.115
  279.8 142.9 %reduce-scatter.2.cloned.1.call-done = f32[32,2,32,256]{3,2,1,0:T(8,128)} async-done(((f32[128,2,32,256]{3,2,1,0:T(8,128)}), f32[32,2,32,256]{3,2,1,0:T(8,128)}) %reduce-scatter.2.cloned.1.call-update) | async-done | bytes 2097168 | tf_op jit(solution)/shard_map/reduce_scatter | solution.py:105
  422.6 3.2 copy_bitcast_fusion.1
  425.8 64.4 %reduce-window.6 = f32[32,2,32,2,128]{4,2,3,1,0:T(8,128)S(1)} reduce-window(f32[32,2,32,2,128]{4,2,3,1,0:T(8,128)} %copy_bitcast_fusion.1, f32[]{:T(128)} %constant.26.clone.1), window={size=1x1x1x1x128 pad=0_0x0_0x0_0x0_0x127_0}, to_apply=%region_9.10 | reduce-window | flops 66584576 | bytes 4194308 | tf_op jit(solution)/shard_map/reduce-window
  499.7 21.8 %all-gather = f32[512,32]{1,0:T(8,128)S(1)} all-gather(f32[32,32]{1,0:T(8,128)S(1)} %fusion.11), channel_id=2, replica_groups=mesh['groups'=2,'rows'=4,'feat'=4] {'rows','feat'}, dimensions={0}, use_global_device_ids=true | all-gather | bytes 69632 | tf_op jit(solution)/shard_map/all_gather | solution.py:114
  (307 shorter events, 153.1 us)
Async XLA Ops:
  7.2 415.5 %reduce-scatter.2.cloned.1.call-start = ((), (), s32[]{:S(2)}) async-start(), calls=%async_computation.1 | async-start | bytes 10485760 | tf_op jit(solution)/shard_map/reduce_scatter | solution.py:105
  12.7 1.8 copy-start.3
  12.7 1.8 copy-start.4
  14.5 24.7 %copy-start.6 = (f32[9]{0:T(128)S(1)}, f32[9]{0:T(128)}, u32[]{:S(2)}) copy-start(f32[9]{0:T(128)} %constant.48.clone) | copy-start | bytes 112
  14.5 25.3 %copy-start.2 = (f32[1024,512]{0,1:T(8,128)S(1)}, f32[1024,512]{0,1:T(8,128)}, u32[]{:S(2)}) copy-start(f32[1024,512]{0,1:T(8,128)} %convert_divide_fusion) | copy-start | bytes 6291460
  38.6 23.9 %copy-start.5 = (s32[1024]{0:T(1024)S(1)}, s32[1024]{0:T(1024)}, u32[]{:S(2)}) copy-start(s32[1024]{0:T(1024)} %param.11) | copy-start | bytes 12292
  39.8 23.3 %copy-start.1 = (s32[1024,128]{1,0:T(8,128)S(1)}, s32[1024,128]{1,0:T(8,128)}, u32[]{:S(2)}) copy-start(s32[1024,128]{1,0:T(8,128)} %param.12) | copy-start | bytes 1572868
  496.5 2.2 copy-start
Sparse Core Ops, SparseCore 0:
  279.9 142.6 reduce-scatter.1
where the time goes:
time: 535 us; the launch traced here: 529 us
  local copies, waits for them, and re-layouts  181 us (34%)
  waiting for transfers between devices  143 us (27%)
  other arithmetic  95.1 us (18%)
  blocking collectives  42.7 us (8%)
  matrix products  30.2 us (6%)
  loops' own time  22.3 us (4%)
  between operations  14.9 us (3%)
    reduce_scatter x1, waiting for transfers between devices, shards(): lax.psum_scatter(blocks.reshape(shard_feats * lax.axis_size('rows'), 2, N...  143 us
    eq x32, local copies, waits for them, and re-layouts, encode_bins(): onehot = chosen[:, :, None] == jnp.arange(BINS)[None, None, :]  81.2 us
    another operation x4, other arithmetic  66.7 us
    while x96, local copies, waits for them, and re-layouts  32.5 us
    dot_general x32, matrix products, one_block(): lax.dot_general(columns, encode_bins(chosen), (((0,), (0,)), ((), ())), p...  27.2 us
    dynamic_update_slice x32, local copies, waits for them, and re-layouts, shards(): lax.map(one_block, jnp.arange(shard_feats * lax.axis_size('rows') // bloc...  24.4 us
    reduce_sum x1, other arithmetic, gradients(): gradient = jnp.mean(quantile_level - quantile, axis=1)  22.6 us
    another operation x1, loops' own time, shards(): lax.map(one_block, jnp.arange(shard_feats * lax.axis_size('rows') // bloc...  22.3 us
  transfers between devices with their start and end apart: 1, of which 1 were waited for; matrix products, arithmetic and copies ran while one was open for 0% of the time, Pallas kernels for 0%

commit v1 on v0

v1 whole, which is shorter than its diff:
```python
import functools

import jax
import jax.numpy as jnp
from jax import lax
from jax.experimental import pallas as pl
from jax.experimental.pallas import tpu as pltpu
from jax.sharding import PartitionSpec as P

BINS = 256
NODES = 32
HIST = 512
HORIZON = 28
FIRST_DAY = HIST - HORIZON
REGIONS = 10
CHANNELS = 8
TAPS = 4
DILATE = (1, 7, 14, 28)
LEVELS = (0.005, 0.025, 0.165, 0.25, 0.5, 0.75, 0.835, 0.975, 0.995)

LANES = 128
DAYS = 32
REGION_ROW = HORIZON
NODE_ROW = HORIZON + 1
TOTAL_ROW = HORIZON
STORES = 16
PIECES = 3
SCALE = 256.0
BF16 = jnp.bfloat16
F32 = jnp.float32
F8 = jnp.float8_e4m3fn
ROW_BY_ROW = (((1,), (1,)), ((), ()))
VMEM_LIMIT = 48 * 2**20


def partner(position, step, count):
    if count & (count - 1) == 0:
        return position ^ step
    return (position + step) % count


def split_parts(values):
    parts = []
    rest = values
    for _ in range(PIECES):
        part = rest.astype(BF16)
        parts.append(part)
        rest = rest - part.astype(F32)
    return parts


def tap_matrix(taps_ref, parity):
    gap = lax.broadcasted_iota(jnp.int32, (DAYS, LANES), 1) - lax.broadcasted_iota(
        jnp.int32, (DAYS, LANES), 0
    )
    first = FIRST_DAY - (HIST - LANES)
    matrix = jnp.zeros((DAYS, LANES), F32)
    for channel in range(parity, CHANNELS, 2):
        for lag in range(TAPS):
            offset = first - 1 - lag * DILATE[(channel // 2) % 4]
            matrix = matrix + jnp.where(gap == offset, taps_ref[channel, lag], 0.0)
    if parity == 0:
        matrix = matrix - jnp.where(gap == first, 1.0, 0.0)
    day = lax.broadcasted_iota(jnp.int32, (DAYS, LANES), 0)
    return jnp.where(day < HORIZON, matrix, 0.0)


def prepare(rows, counts_ref, region_ref, node_ref, bins_ref, taps_ref, *rest):
    out_refs, held = rest[:rows], rest[rows]
    series = counts_ref.shape[0]
    feats = bins_ref.shape[1] // rows
    pad = held.shape[1]
    me = lax.axis_index("rows")
    counts = counts_ref[...]
    recent = counts_ref[:, HIST - LANES :]

    own_taps = jnp.concatenate(split_parts(tap_matrix(taps_ref, 0)), axis=0)
    own = lax.dot_general(own_taps, recent, ROW_BY_ROW, preferred_element_type=F32)
    own = own[:DAYS] + own[DAYS : 2 * DAYS] + own[2 * DAYS :]
    ones = jnp.ones((8, HIST), BF16)
    level = lax.dot_general(ones, counts, ROW_BY_ROW, preferred_element_type=F32)[:1] / HIST
    own = own / level
    day = lax.broadcasted_iota(jnp.int32, (DAYS, series), 0)
    own = jnp.where(day == REGION_ROW, region_ref[...].astype(F32), own)
    own = jnp.where(day == NODE_ROW, node_ref[...].astype(F32), own)
    own = own.astype(BF16)

    store = lax.broadcasted_iota(jnp.int32, (STORES, series), 0)
    pick = jnp.where(store == region_ref[...], 1.0, 0.0).astype(BF16)
    totals = jnp.dot(pick, counts, preferred_element_type=F32)
    forecast = lax.dot_general(
        tap_matrix(taps_ref, 1),
        totals[:, HIST - LANES :],
        ROW_BY_ROW,
        precision=lax.Precision.HIGHEST,
        preferred_element_type=F32,
    )
    over_days = lax.dot_general(
        jnp.ones((DAYS, HIST), F32),
        totals,
        ROW_BY_ROW,
        precision=lax.Precision.HIGHEST,
        preferred_element_type=F32,
    )
    row = lax.broadcasted_iota(jnp.int32, (DAYS, STORES), 0)
    forecast = jnp.where(row == TOTAL_ROW, over_days, forecast)
    sums = jnp.concatenate(
        split_parts(forecast) + [jnp.zeros((DAYS, LANES - PIECES * STORES), BF16)], axis=1
    )

    turned = bins_ref[...].astype(F32).T
    for row_block in range(rows):
        part = turned[row_block * feats : (row_block + 1) * feats]
        if pad > feats:
            part = jnp.concatenate([part, jnp.zeros((pad - feats, series), F32)], axis=0)
        held[row_block] = part.astype(BF16)

    height = pad + DAYS
    for step in range(rows):
        bins = held[partner(me, step, rows)]
        for block in range(series // LANES):
            lanes = slice(block * LANES, (block + 1) * LANES)
            out_refs[step][block * height : block * height + pad] = bins[:, lanes]
            out_refs[step][block * height + pad : (block + 1) * height] = own[:, lanes]
        out_refs[step][series // LANES * height :] = sums


def grow(rows, feats, series, quant_ref, *rest):
    in_refs = rest[:rows]
    hist_ref, best_ref, bins_held, cols_held, hist_held, sem = rest[rows:]
    pad = max(feats, 16)
    height = pad + DAYS
    blocks = series // LANES
    everyone = rows * series

    level = F32(0.0)
    for index, value in enumerate(LEVELS):
        level = jnp.where(quant_ref[0] == index, F32(value), level)

    sums = jnp.zeros((DAYS, STORES), F32)
    for ref in in_refs:
        parts = ref[blocks * height :].astype(F32)
        for piece in range(PIECES):
            sums = sums + parts[:, piece * STORES : (piece + 1) * STORES]
    shared = sums / (sums[TOTAL_ROW : TOTAL_ROW + 1] / HIST + 1.0)
    shared = jnp.concatenate(split_parts(shared), axis=1)

    day = lax.broadcasted_iota(jnp.int32, (DAYS, series), 0)
    store = lax.broadcasted_iota(jnp.int32, (PIECES * STORES, series), 0) % STORES
    node_at = lax.broadcasted_iota(jnp.int32, (NODES, series), 0)
    for source, ref in enumerate(in_refs):
        here = slice(source * series, (source + 1) * series)
        both = jnp.concatenate(
            [ref[block * height : (block + 1) * height] for block in range(blocks)], axis=1
        ).astype(F32)
        bins_held[:, here] = (both[:feats] - 128.0).astype(jnp.int32)
        own = both[pad:]
        region = own[REGION_ROW : REGION_ROW + 1].astype(jnp.int32)
        node = own[NODE_ROW : NODE_ROW + 1].astype(jnp.int32)
        pick = jnp.where(store == region, 1.0, 0.0).astype(BF16)
        regional = jnp.dot(shared, pick, preferred_element_type=F32)
        wave = jnp.where(day < HORIZON, jnp.tanh(own + regional), 0.0)
        mean = jnp.sum(wave, axis=0, keepdims=True) / HORIZON
        square = jnp.sum(wave * wave, axis=0, keepdims=True) / HORIZON
        gradient = 0.5 + 0.5 * mean - level
        hessian = 0.5 * (1.0 - square)
        here_node = node_at == node
        low = []
        for part, value in enumerate((gradient, hessian)):
            value = value.astype(BF16).astype(F32) * SCALE
            high = value.astype(F8).astype(F32)
            for offset, piece in ((0, high), (2, value - high)):
                at = (part + offset) * NODES
                cols_held[at : at + NODES, here] = jnp.where(here_node, piece, 0.0).astype(F8)

    below = lax.broadcasted_iota(jnp.int32, (BINS, BINS), 0) <= lax.broadcasted_iota(
        jnp.int32, (BINS, BINS), 1
    )
    below = jnp.where(below, 1.0, 0.0).astype(BF16)
    chunk = min(everyone, 4096)
    bin_at = lax.broadcasted_iota(jnp.int32, (32, chunk), 0)
    feature_at = lax.broadcasted_iota(jnp.int32, (NODES, LANES), 1)
    last_bin = lax.broadcasted_iota(jnp.int32, (NODES, BINS), 1) == BINS - 1

    def products(feature, start):
        here = pl.ds(start, chunk)
        wide = jnp.broadcast_to(bins_held[pl.ds(feature, 1), here], (32, chunk)).astype(jnp.int8)
        onehot = jnp.concatenate(
            [
                jnp.where(
                    wide == (bin_at + (32 * part - 128)).astype(jnp.int8),
                    jnp.ones((), F8),
                    jnp.zeros((), F8),
                )
                for part in range(BINS // 32)
            ],
            axis=0,
        )
        return lax.dot_general(
            cols_held[:, here], onehot, ROW_BY_ROW, preferred_element_type=F32
        )

    def copy_out(feature):
        return pltpu.make_async_copy(hist_held.at[feature], hist_ref.at[feature], sem)

    def one_feature(feature, best):
        if everyone == chunk:
            product = products(feature, 0)
        else:
            product = lax.fori_loop(
                0,
                everyone // chunk,
                lambda at, total: total
                + products(feature, pl.multiple_of(at * chunk, chunk)),
                jnp.zeros((4 * NODES, BINS), F32),
            )
        hist = (product[: 2 * NODES] + product[2 * NODES :]) * (1.0 / SCALE)
        hist_held[feature] = hist
        copy_out(feature).start()
        high = hist.astype(BF16)
        both = jnp.concatenate([high, (hist - high.astype(F32)).astype(BF16)], axis=0)
        left = jnp.dot(both, below, preferred_element_type=F32)
        left = left[: 2 * NODES] + left[2 * NODES :]
        total = left[:, BINS - 1 :]
        right = total - left
        gain = left[:NODES] * left[:NODES] / (left[NODES:] + 1.0) + right[:NODES] * right[
            :NODES
        ] / (right[NODES:] + 1.0)
        gain = jnp.max(jnp.where(last_bin, -jnp.inf, gain), axis=1, keepdims=True)
        gain = gain - total[:NODES] * total[:NODES] / (total[NODES:] + 1.0)
        return jnp.where(feature_at == feature, gain, best)

    best = lax.fori_loop(
        0, feats, one_feature, jnp.zeros((NODES, LANES), F32), unroll=min(feats, 4)
    )
    best = best.T
    width = LANES // NODES
    packed = jnp.concatenate(
        [best[at * (feats // width) : (at + 1) * (feats // width)] for at in range(width)], axis=1
    )
    for target in range(best_ref.shape[0]):
        best_ref[target] = packed
    pltpu.make_async_copy(hist_held, hist_ref, sem).wait()


def shards(daily_unit_counts, region_ids, node_ids, bin_ids, quant_index, filter_kernels):
    rows = lax.axis_size("rows")
    feat_count = lax.axis_size("feat")
    series = daily_unit_counts.shape[0]
    feats = bin_ids.shape[1] // rows
    pad = max(feats, 16)
    buffer = (series // LANES * (pad + DAYS) + DAYS, LANES)
    vmem = pl.BlockSpec(memory_space=pltpu.VMEM)
    smem = pl.BlockSpec(memory_space=pltpu.SMEM)
    params = pltpu.CompilerParams(vmem_limit_bytes=VMEM_LIMIT)

    outgoing = pl.pallas_call(
        functools.partial(prepare, rows),
        out_shape=[jax.ShapeDtypeStruct(buffer, BF16)] * rows,
        in_specs=[vmem, vmem, vmem, vmem, smem],
        out_specs=[vmem] * rows,
        scratch_shapes=[pltpu.VMEM((rows, pad, series), BF16)],
        compiler_params=params,
        name="prepare",
    )(
        daily_unit_counts,
        region_ids.reshape(1, series),
        node_ids.reshape(1, series),
        bin_ids,
        filter_kernels,
    )

    arrived = [outgoing[0]]
    for step in range(1, rows):
        pairs = [(at, partner(at, step, rows)) for at in range(rows)]
        arrived.append(lax.ppermute(outgoing[step], "rows", pairs))

    targets = rows * feat_count
    packed_rows = feats * NODES // LANES
    histogram, best = pl.pallas_call(
        functools.partial(grow, rows, feats, series),
        out_shape=[
            jax.ShapeDtypeStruct((feats, 2 * NODES, BINS), F32),
            jax.ShapeDtypeStruct((targets, packed_rows, LANES), F32),
        ],
        in_specs=[smem] + [vmem] * rows,
        out_specs=[pl.BlockSpec(memory_space=pl.ANY), vmem],
        scratch_shapes=[
            pltpu.VMEM((feats, rows * series), jnp.int32),
            pltpu.VMEM((4 * NODES, rows * series), F8),
            pltpu.VMEM((feats, 2 * NODES, BINS), F32),
            pltpu.SemaphoreType.DMA,
        ],
        compiler_params=params,
        name="grow",
    )(quant_index, *arrived)

    gathered = lax.all_to_all(best, ("feat", "rows"), 0, 0, tiled=True)
    width = LANES // NODES
    feature_best = (
        gathered.reshape(feat_count, rows, packed_rows, width, NODES)
        .transpose(0, 1, 3, 2, 4)
        .reshape(feat_count, rows, feats, NODES)
    )
    return histogram.reshape(1, 1, feats, 2, NODES, BINS), feature_best


def solution(mesh):
    in_specs = (
        P(("groups", "rows"), None),
        P(("groups", "rows")),
        P(("groups", "rows")),
        P(("groups", "rows"), "feat"),
        P("groups"),
        P(),
    )
    out_specs = (
        P(("groups", "feat"), "rows", None, None, None, None),
        P("groups", None, None, None),
    )
    return jax.shard_map(shards, mesh=mesh, in_specs=in_specs, out_specs=out_specs, check_vma=False)
```

time: 535 us -> 62.5 us (0.12)
  local copies, waits for them, and re-layouts: 181 us -> 5.28 us
  waiting for transfers between devices: 143 us -> 10.2 us
  other arithmetic: 95.1 us -> 0 us
  blocking collectives: 42.7 us -> 11.9 us
  matrix products: 30.2 us -> 0 us
  Pallas kernels: 0 us -> 27.8 us
  loops' own time: 22.3 us -> 0 us
  between operations: 14.9 us -> 1.31 us
  starting transfers between devices: 0.04 us -> 5.69 us
    reduce_scatter x1 -> x0, waiting for transfers between devices: 143 us -> none  [shards(): lax.psum_scatter(blocks.reshape(shard_feats * lax.axis_size('rows'), 2, N...]
    eq x32 -> x0, local copies, waits for them, and re-layouts: 81.2 us -> none  [encode_bins(): onehot = chosen[:, :, None] == jnp.arange(BINS)[None, None, :]]
    another operation x4 -> x0, other arithmetic: 66.7 us -> none
    while x96 -> x0, local copies, waits for them, and re-layouts: 32.5 us -> none
    dot_general x34 -> x0, matrix products: 30.2 us -> none  [the longest x32 27.2 us: one_block(): lax.dot_general(columns, encode_bins(chosen), (((0,), (0,)), ((), ())), p...]
    pallas_call x0 -> x2, Pallas kernels: none -> 27.8 us  [the longest x1 26.1 us: shards(): pl.pallas_call(functools.partial(grow, rows, feats, series), out_shape=[j...]
    reduce_sum x5 -> x0, other arithmetic: 25.6 us -> none  [the longest x1 22.6 us: gradients(): gradient = jnp.mean(quantile_level - quantile, axis=1)]
    dynamic_slice x64 -> x0, local copies, waits for them, and re-layouts: 25.1 us -> none  [the longest x32 18.6 us: shards(): lax.map(one_block, jnp.arange(shard_feats * lax.axis_size('rows') // bloc...]
  transfers between devices with their start and end apart: 1 -> 3, of which waited for: 1 -> 2; matrix products, arithmetic and copies ran while one was open for 0% -> 0% of each run, Pallas kernels for 0% -> 0%
where the time goes in v1:
time: 62.5 us; the launch traced here: 62.1 us
  Pallas kernels  27.8 us (44%)
  blocking collectives  11.9 us (19%)
  waiting for transfers between devices  10.2 us (16%)
  starting transfers between devices  5.69 us (9%)
  local copies, waits for them, and re-layouts  5.28 us (8%)
  between operations  1.31 us (2%)
    pallas_call x1, Pallas kernels, shards(): pl.pallas_call(functools.partial(grow, rows, feats, series), out_shape=[j...  26.1 us
    all_to_all x1, blocking collectives, shards(): gathered = lax.all_to_all(best, ('feat', 'rows'), 0, 0, tiled=True)  11.9 us
    ppermute x3, waiting for transfers between devices, shards(): arrived.append(lax.ppermute(outgoing[step], 'rows', pairs))  10.2 us
    ppermute x3, starting transfers between devices, shards(): arrived.append(lax.ppermute(outgoing[step], 'rows', pairs))  5.69 us
    unnamed x9, local copies, waits for them, and re-layouts  4.39 us
    pallas_call x1, Pallas kernels, shards(): pl.pallas_call(functools.partial(prepare, rows), out_shape=[jax.ShapeDtyp...  1.62 us
  transfers between devices with their start and end apart: 3, of which 2 were waited for; matrix products, arithmetic and copies ran while one was open for 0% of the time, Pallas kernels for 0%

profile of v1, /device:TPU:0, one launch (start us, length us, event | category | flops | bytes accessed | tf_op | source)
XLA Modules:
  0.0 62.1 jit_solution(11757563673058710434)
XLA Ops:
  0.6 0.8 %copy.8.taps_ref = f32[8,4]{1,0:T(8,128)S(1)} copy(f32[8,4]{0,1:T(4,128)} %param.11) | data formatting | bytes 256 | tf_op args[5]
  1.4 0.0 copy-start
  1.4 1.2 %copy-done = bf16[1024,512]{1,0:T(8,128)(2,1)S(1)} copy-done((bf16[1024,512]{1,0:T(8,128)(2,1)S(1)}, bf16[1024,512]{1,0:T(8,128)(2,1)}, u32[]{:S(2)}) %copy-start) | copy-done | bytes 1048600
  2.6 0.0 copy-start.1
  2.6 1.0 %copy-done.1 = s32[1024,128]{1,0:T(8,128)S(1)} copy-done((s32[1024,128]{1,0:T(8,128)S(1)}, s32[1024,128]{1,0:T(8,128)}, u32[]{:S(2)}) %copy-start.1) | copy-done | bytes 524312
  3.7 0.0 copy-start.2
  3.7 0.7 %copy-done.2 = s32[1024]{0:T(1024)S(1)} copy-done((s32[1024]{0:T(1024)S(1)}, s32[1024]{0:T(1024)}, u32[]{:S(2)}) %copy-start.2) | copy-done | bytes 4120
  4.3 0.0 copy-start.3
  4.3 0.7 %copy-done.3 = s32[1024]{0:T(1024)S(1)} copy-done((s32[1024]{0:T(1024)S(1)}, s32[1024]{0:T(1024)}, u32[]{:S(2)}) %copy-start.3) | copy-done | bytes 4120
  5.0 1.6 %prepare.1 = (bf16[544,128]{1,0:T(8,128)(2,1)S(1)}, bf16[544,128]{1,0:T(8,128)(2,1)S(1)}, bf16[544,128]{1,0:T(8,128)(2,1)S(1)}, bf16[544,128]{1,0:T(8,128)(2,1)S(1)}) custom-call(bf16[1024,512]{1,0:T(8,128)(2,1)S(1)} %copy-done, s32[1,1024]{1,0:T(1,128)S(1)} %bitcast.7, s32[1,1024]{1,0:T(1,128)S(1)} %bitcast.8, s32[1024,128]{1,0:T(8,128)S(1)} %copy-done.1, ...), custom_call_target="tpu_custom_call" | custom-call | tf_op jit(solution)/shard_map/prepare/pallas_call | solution.py:257
  6.7 3.1 %collective-permute-start = (bf16[544,128]{1,0:T(8,128)(2,1)S(1)}, bf16[544,128]{1,0:T(8,128)(2,1)S(1)}, u32[]{:S(2)}, u32[]{:S(2)}) collective-permute-start(bf16[544,128]{1,0:T(8,128)(2,1)S(1)} %get-tuple-element.9), channel_id=1, source_target_pairs={{0,4},{4,0},{8,12},{12,8},{1,5},{5,1},{9,13},{13,9},{2,6},{6,2},{1... | collective-permute-start | bytes 417800 | tf_op jit(solution)/shard_map/ppermute | solution.py:276
  9.7 2.6 %collective-permute-start.1 = (bf16[544,128]{1,0:T(8,128)(2,1)S(1)}, bf16[544,128]{1,0:T(8,128)(2,1)S(1)}, u32[]{:S(2)}, u32[]{:S(2)}) collective-permute-start(bf16[544,128]{1,0:T(8,128)(2,1)S(1)} %get-tuple-element.10), channel_id=1, source_target_pairs={{0,8},{4,12},{8,0},{12,4},{1,9},{5,13},{9,1},{13,5},{2,10},{6,14},... | collective-permute-start | bytes 417800 | tf_op jit(solution)/shard_map/ppermute | solution.py:276
  12.3 0.0 collective-permute-start.2
  13.0 2.2 %collective-permute-done.rest_1_ = bf16[544,128]{1,0:T(8,128)(2,1)S(1)} collective-permute-done((bf16[544,128]{1,0:T(8,128)(2,1)S(1)}, bf16[544,128]{1,0:T(8,128)(2,1)S(1)}, u32[]{:S(2)}, u32[]{:S(2)}) %collective-permute-start) | collective-permute-done | bytes 139296 | tf_op jit(solution)/shard_map/ppermute | solution.py:276
  15.2 8.0 %collective-permute-done.1.rest_2_ = bf16[544,128]{1,0:T(8,128)(2,1)S(1)} collective-permute-done((bf16[544,128]{1,0:T(8,128)(2,1)S(1)}, bf16[544,128]{1,0:T(8,128)(2,1)S(1)}, u32[]{:S(2)}, u32[]{:S(2)}) %collective-permute-start.1) | collective-permute-done | bytes 139296 | tf_op jit(solution)/shard_map/ppermute | solution.py:276
  23.2 0.0 collective-permute-done.2.rest_3_
  23.2 26.1 %grow.1 = (f32[32,64,256]{2,1,0:T(8,128)}, f32[16,8,128]{2,1,0:T(8,128)S(1)}) custom-call(s32[1]{0:T(128)S(6)} %copy.12.quant_ref, bf16[544,128]{1,0:T(8,128)(2,1)S(1)} %get-tuple-element.8.rest_0_, bf16[544,128]{1,0:T(8,128)(2,1)S(1)} %collective-permute-done.rest_1_, bf16[544,128]{1,0:T(8,128)(2,1)S(1)} %collective-permute-done.1.rest_2_, ...), custom_call_target="tpu_custom_call" | custom-call | tf_op jit(solution)/shard_map/grow/pallas_call | solution.py:280
  49.4 11.9 %all_to_all.5 = f32[16,8,128]{2,1,0:T(8,128)S(1)} all-to-all(f32[16,8,128]{2,1,0:T(8,128)S(1)} %get-tuple-element.13), channel_id=1, replica_groups=mesh['groups'=2,'rows'=4,'feat'=4] {'feat','rows'}, dimensions={0} | all-to-all | bytes 131072 | tf_op jit(solution)/shard_map/all_to_all | solution.py:298
  61.2 0.2 reshape.22
  61.4 0.7 %copy.11 = f32[4,4,4,8,32]{4,3,2,1,0:T(8,128)} copy(f32[4,4,4,8,32]{4,2,3,1,0:T(4,128)S(1)} %bitcast.9) | data formatting | bytes 131072 | tf_op jit(solution)/shard_map/transpose | solution.py:302
Async XLA Ops:
  1.4 1.2 %copy-start = (bf16[1024,512]{1,0:T(8,128)(2,1)S(1)}, bf16[1024,512]{1,0:T(8,128)(2,1)}, u32[]{:S(2)}) copy-start(bf16[1024,512]{1,0:T(8,128)(2,1)} %counts_ref.1) | copy-start | bytes 3145732
  2.6 1.0 %copy-start.1 = (s32[1024,128]{1,0:T(8,128)S(1)}, s32[1024,128]{1,0:T(8,128)}, u32[]{:S(2)}) copy-start(s32[1024,128]{1,0:T(8,128)} %bins_ref.1) | copy-start | bytes 1572868
  3.7 0.7 %copy-start.2 = (s32[1024]{0:T(1024)S(1)}, s32[1024]{0:T(1024)}, u32[]{:S(2)}) copy-start(s32[1024]{0:T(1024)} %param.7) | copy-start | bytes 12292
  4.3 0.7 %copy-start.3 = (s32[1024]{0:T(1024)S(1)}, s32[1024]{0:T(1024)}, u32[]{:S(2)}) copy-start(s32[1024]{0:T(1024)} %param.8) | copy-start | bytes 12292
  6.7 8.5 %collective-permute-start = (bf16[544,128]{1,0:T(8,128)(2,1)S(1)}, bf16[544,128]{1,0:T(8,128)(2,1)S(1)}, u32[]{:S(2)}, u32[]{:S(2)}) collective-permute-start(bf16[544,128]{1,0:T(8,128)(2,1)S(1)} %get-tuple-element.9), channel_id=1, source_target_pairs={{0,4},{4,0},{8,12},{12,8},{1,5},{5,1},{9,13},{13,9},{2,6},{6,2},{1... | collective-permute-start | bytes 417800 | tf_op jit(solution)/shard_map/ppermute | solution.py:276
  9.7 13.5 %collective-permute-start.1 = (bf16[544,128]{1,0:T(8,128)(2,1)S(1)}, bf16[544,128]{1,0:T(8,128)(2,1)S(1)}, u32[]{:S(2)}, u32[]{:S(2)}) collective-permute-start(bf16[544,128]{1,0:T(8,128)(2,1)S(1)} %get-tuple-element.10), channel_id=1, source_target_pairs={{0,8},{4,12},{8,0},{12,4},{1,9},{5,13},{9,1},{13,5},{2,10},{6,14},... | collective-permute-start | bytes 417800 | tf_op jit(solution)/shard_map/ppermute | solution.py:276
  12.3 10.9 %collective-permute-start.2 = (bf16[544,128]{1,0:T(8,128)(2,1)S(1)}, bf16[544,128]{1,0:T(8,128)(2,1)S(1)}, u32[]{:S(2)}, u32[]{:S(2)}) collective-permute-start(bf16[544,128]{1,0:T(8,128)(2,1)S(1)} %get-tuple-element.11), channel_id=1, source_target_pairs={{0,12},{4,8},{8,4},{12,0},{1,13},{5,9},{9,5},{13,1},{2,14},{6,10},... | collective-permute-start | bytes 417800 | tf_op jit(solution)/shard_map/ppermute | solution.py:276

commit v2 on v1

--- a/solution.py
+++ b/solution.py
@@ -31,6 +31,7 @@
 F8 = jnp.float8_e4m3fn
 ROW_BY_ROW = (((1,), (1,)), ((), ()))
 VMEM_LIMIT = 48 * 2**20
+WHOLE_VMEM = 63 * 2**20
 
 
 def partner(position, step, count):
@@ -58,19 +59,41 @@
     for channel in range(parity, CHANNELS, 2):
         for lag in range(TAPS):
             offset = first - 1 - lag * DILATE[(channel // 2) % 4]
-            matrix = matrix + jnp.where(gap == offset, taps_ref[channel, lag], 0.0)
+            matrix = matrix + jnp.where(
+                gap == offset, taps_ref[lag : lag + 1, channel : channel + 1], 0.0
+            )
     if parity == 0:
         matrix = matrix - jnp.where(gap == first, 1.0, 0.0)
     day = lax.broadcasted_iota(jnp.int32, (DAYS, LANES), 0)
     return jnp.where(day < HORIZON, matrix, 0.0)
 
 
-def prepare(rows, counts_ref, region_ref, node_ref, bins_ref, taps_ref, *rest):
-    out_refs, held = rest[:rows], rest[rows]
+def prepare(rows, *refs):
+    given = refs[:5]
+    out_refs = refs[5 : 5 + rows]
+    taken = refs[5 + rows : 10 + rows]
+    held, sems = refs[10 + rows :]
+    copies = [
+        pltpu.make_async_copy(source, target, sems.at[at])
+        for at, (source, target) in enumerate(zip(given, taken))
+    ]
+    for at in (3, 4, 1, 2, 0):
+        copies[at].start()
+    counts_ref, region_ref, node_ref, bins_ref, taps_ref = taken
     series = counts_ref.shape[0]
     feats = bins_ref.shape[1] // rows
     pad = held.shape[1]
     me = lax.axis_index("rows")
+    copies[3].wait()
+    turned = bins_ref[...].astype(F32).T
+    for row_block in range(rows):
+        part = turned[row_block * feats : (row_block + 1) * feats]
+        if pad > feats:
+            part = jnp.concatenate([part, jnp.zeros((pad - feats, series), F32)], axis=0)
+        held[row_block] = part.astype(BF16)
+
+    for at in (4, 1, 2, 0):
+        copies[at].wait()
     counts = counts_ref[...]
     recent = counts_ref[:, HIST - LANES :]
 
@@ -107,13 +130,6 @@
     sums = jnp.concatenate(
         split_parts(forecast) + [jnp.zeros((DAYS, LANES - PIECES * STORES), BF16)], axis=1
     )
-
-    turned = bins_ref[...].astype(F32).T
-    for row_block in range(rows):
-        part = turned[row_block * feats : (row_block + 1) * feats]
-        if pad > feats:
-            part = jnp.concatenate([part, jnp.zeros((pad - feats, series), F32)], axis=0)
-        held[row_block] = part.astype(BF16)
 
     height = pad + DAYS
     for step in range(rows):
@@ -203,7 +219,7 @@
     def copy_out(feature):
         return pltpu.make_async_copy(hist_held.at[feature], hist_ref.at[feature], sem)
 
-    def one_feature(feature, best):
+    def one_feature(feature, carry):
         if everyone == chunk:
             product = products(feature, 0)
         else:
@@ -217,22 +233,30 @@
         hist = (product[: 2 * NODES] + product[2 * NODES :]) * (1.0 / SCALE)
         hist_held[feature] = hist
         copy_out(feature).start()
+        return carry
+
+    lax.fori_loop(0, feats, one_feature, 0, unroll=min(feats, 8))
+    group = min(feats, 8)
+
+    def one_group(at, best):
+        hist = hist_held[pl.ds(at * group, group)].reshape(group * 2 * NODES, BINS)
         high = hist.astype(BF16)
-        both = jnp.concatenate([high, (hist - high.astype(F32)).astype(BF16)], axis=0)
-        left = jnp.dot(both, below, preferred_element_type=F32)
-        left = left[: 2 * NODES] + left[2 * NODES :]
-        total = left[:, BINS - 1 :]
-        right = total - left
-        gain = left[:NODES] * left[:NODES] / (left[NODES:] + 1.0) + right[:NODES] * right[
-            :NODES
-        ] / (right[NODES:] + 1.0)
-        gain = jnp.max(jnp.where(last_bin, -jnp.inf, gain), axis=1, keepdims=True)
-        gain = gain - total[:NODES] * total[:NODES] / (total[NODES:] + 1.0)
-        return jnp.where(feature_at == feature, gain, best)
-
-    best = lax.fori_loop(
-        0, feats, one_feature, jnp.zeros((NODES, LANES), F32), unroll=min(feats, 4)
-    )
+        low = (hist - high.astype(F32)).astype(BF16)
+        left = jnp.dot(high, below, preferred_element_type=F32) + jnp.dot(
+            low, below, preferred_element_type=F32
+        )
+        left = left.reshape(group, 2, NODES, BINS)
+        for member in range(group):
+            grad, hess = left[member, 0], left[member, 1]
+            all_grad, all_hess = grad[:, BINS - 1 :], hess[:, BINS - 1 :]
+            over_grad, over_hess = all_grad - grad, all_hess - hess
+            gain = grad * grad / (hess + 1.0) + over_grad * over_grad / (over_hess + 1.0)
+            gain = jnp.max(jnp.where(last_bin, -jnp.inf, gain), axis=1, keepdims=True)
+            gain = gain - all_grad * all_grad / (all_hess + 1.0)
+            best = jnp.where(feature_at == at * group + member, gain, best)
+        return best
+
+    best = lax.fori_loop(0, feats // group, one_group, jnp.zeros((NODES, LANES), F32))
     best = best.T
     width = LANES // NODES
     packed = jnp.concatenate(
@@ -252,22 +276,31 @@
     buffer = (series // LANES * (pad + DAYS) + DAYS, LANES)
     vmem = pl.BlockSpec(memory_space=pltpu.VMEM)
     smem = pl.BlockSpec(memory_space=pltpu.SMEM)
+    hbm = pl.BlockSpec(memory_space=pl.ANY)
     params = pltpu.CompilerParams(vmem_limit_bytes=VMEM_LIMIT)
 
     outgoing = pl.pallas_call(
         functools.partial(prepare, rows),
         out_shape=[jax.ShapeDtypeStruct(buffer, BF16)] * rows,
-        in_specs=[vmem, vmem, vmem, vmem, smem],
+        in_specs=[hbm] * 5,
         out_specs=[vmem] * rows,
-        scratch_shapes=[pltpu.VMEM((rows, pad, series), BF16)],
-        compiler_params=params,
+        scratch_shapes=[
+            pltpu.VMEM(daily_unit_counts.shape, BF16),
+            pltpu.VMEM((1, series), jnp.int32),
+            pltpu.VMEM((1, series), jnp.int32),
+            pltpu.VMEM(bin_ids.shape, jnp.int32),
+            pltpu.VMEM((TAPS, CHANNELS), F32),
+            pltpu.VMEM((rows, pad, series), BF16),
+            pltpu.SemaphoreType.DMA((5,)),
+        ],
+        compiler_params=pltpu.CompilerParams(vmem_limit_bytes=WHOLE_VMEM),
         name="prepare",
     )(
         daily_unit_counts,
         region_ids.reshape(1, series),
         node_ids.reshape(1, series),
         bin_ids,
-        filter_kernels,
+        filter_kernels.T,
     )
 
     arrived = [outgoing[0]]

time: 62.5 us -> 47.2 us (0.76)
  Pallas kernels: 27.8 us -> 15.9 us
  local copies, waits for them, and re-layouts: 5.28 us -> 1.79 us
    pallas_call x1, Pallas kernels: 26.1 us -> 12.6 us  [shards(): pl.pallas_call(functools.partial(grow, rows, feats, series), out_shape=[j...]
    unnamed x9 -> x2, local copies, waits for them, and re-layouts: 4.39 us -> 0.91 us
    pallas_call x1, Pallas kernels: 1.62 us -> 3.32 us  [shards(): pl.pallas_call(functools.partial(prepare, rows), out_shape=[jax.ShapeDtyp...]
where the time goes in v2:
time: 47.2 us; the launch traced here: 47 us
  Pallas kernels  15.9 us (34%)
  blocking collectives  11.9 us (25%)
  waiting for transfers between devices  10.4 us (22%)
  starting transfers between devices  5.68 us (12%)
  local copies, waits for them, and re-layouts  1.79 us (4%)
  between operations  1.31 us (3%)
    pallas_call x1, Pallas kernels, shards(): pl.pallas_call(functools.partial(grow, rows, feats, series), out_shape=[j...  12.6 us
    all_to_all x1, blocking collectives, shards(): gathered = lax.all_to_all(best, ('feat', 'rows'), 0, 0, tiled=True)  11.9 us
    ppermute x3, waiting for transfers between devices, shards(): arrived.append(lax.ppermute(outgoing[step], 'rows', pairs))  10.4 us
    ppermute x3, starting transfers between devices, shards(): arrived.append(lax.ppermute(outgoing[step], 'rows', pairs))  5.68 us
    pallas_call x1, Pallas kernels, shards(): pl.pallas_call(functools.partial(prepare, rows), out_shape=[jax.ShapeDtyp...  3.32 us
  transfers between devices with their start and end apart: 3, of which 2 were waited for; matrix products, arithmetic and copies ran while one was open for 0% of the time, Pallas kernels for 0%

profile of v2, /device:TPU:0, one launch (start us, length us, event | category | flops | bytes accessed | tf_op | source)
XLA Modules:
  0.0 47.0 jit_solution(6811286488391293667)
XLA Ops:
  0.6 3.3 %prepare.1 = (bf16[544,128]{1,0:T(8,128)(2,1)}, bf16[544,128]{1,0:T(8,128)(2,1)}, bf16[544,128]{1,0:T(8,128)(2,1)}, bf16[544,128]{1,0:T(8,128)(2,1)}) custom-call(bf16[1024,512]{1,0:T(8,128)(2,1)} %refs_0_.1, s32[1,1024]{1,0:T(1,128)} %bitcast.10, s32[1,1024]{1,0:T(1,128)} %bitcast.11, s32[1024,128]{1,0:T(8,128)} %refs_3_.1, f32[4,8]{1,0:T(4,128)} %bitcast.12), custom_call_target="tpu_custom_call" | custom-call | tf_op jit(solution)/shard_map/prepare/pallas_call | solution.py:282
  4.0 3.1 %collective-permute-start = (bf16[544,128]{1,0:T(8,128)(2,1)}, bf16[544,128]{1,0:T(8,128)(2,1)S(1)}, u32[]{:S(2)}, u32[]{:S(2)}) collective-permute-start(bf16[544,128]{1,0:T(8,128)(2,1)} %get-tuple-element.9), channel_id=1, source_target_pairs={{0,4},{4,0},{8,12},{12,8},{1,5},{5,1},{9,13},{13,9},{2,6},{6,2},{1... | collective-permute-start | bytes 417800 | tf_op jit(solution)/shard_map/ppermute | solution.py:309
  7.1 2.6 %collective-permute-start.1 = (bf16[544,128]{1,0:T(8,128)(2,1)}, bf16[544,128]{1,0:T(8,128)(2,1)S(1)}, u32[]{:S(2)}, u32[]{:S(2)}) collective-permute-start(bf16[544,128]{1,0:T(8,128)(2,1)} %get-tuple-element.10), channel_id=1, source_target_pairs={{0,8},{4,12},{8,0},{12,4},{1,9},{5,13},{9,1},{13,5},{2,10},{6,14},... | collective-permute-start | bytes 417800 | tf_op jit(solution)/shard_map/ppermute | solution.py:309
  9.6 0.0 collective-permute-start.2
  10.3 2.4 %collective-permute-done.rest_1_ = bf16[544,128]{1,0:T(8,128)(2,1)S(1)} collective-permute-done((bf16[544,128]{1,0:T(8,128)(2,1)}, bf16[544,128]{1,0:T(8,128)(2,1)S(1)}, u32[]{:S(2)}, u32[]{:S(2)}) %collective-permute-start) | collective-permute-done | bytes 139296 | tf_op jit(solution)/shard_map/ppermute | solution.py:309
  12.7 8.0 %collective-permute-done.1.rest_2_ = bf16[544,128]{1,0:T(8,128)(2,1)S(1)} collective-permute-done((bf16[544,128]{1,0:T(8,128)(2,1)}, bf16[544,128]{1,0:T(8,128)(2,1)S(1)}, u32[]{:S(2)}, u32[]{:S(2)}) %collective-permute-start.1) | collective-permute-done | bytes 139296 | tf_op jit(solution)/shard_map/ppermute | solution.py:309
  20.7 0.0 collective-permute-done.2.rest_3_
  20.7 0.0 copy-start
  20.7 0.9 %copy-done = bf16[544,128]{1,0:T(8,128)(2,1)S(1)} copy-done((bf16[544,128]{1,0:T(8,128)(2,1)S(1)}, bf16[544,128]{1,0:T(8,128)(2,1)}, u32[]{:S(2)}) %copy-start) | copy-done | bytes 139288
  21.6 12.6 %grow.1 = (f32[32,64,256]{2,1,0:T(8,128)}, f32[16,8,128]{2,1,0:T(8,128)S(1)}) custom-call(s32[1]{0:T(128)S(6)} %copy.11.quant_ref, bf16[544,128]{1,0:T(8,128)(2,1)S(1)} %copy-done, bf16[544,128]{1,0:T(8,128)(2,1)S(1)} %collective-permute-done.rest_1_, bf16[544,128]{1,0:T(8,128)(2,1)S(1)} %collective-permute-done.1.rest_2_, ...), custom_call_target="tpu_custom_call" | custom-call | tf_op jit(solution)/shard_map/grow/pallas_call | solution.py:313
  34.2 11.9 %all_to_all.5 = f32[16,8,128]{2,1,0:T(8,128)S(1)} all-to-all(f32[16,8,128]{2,1,0:T(8,128)S(1)} %get-tuple-element.13), channel_id=1, replica_groups=mesh['groups'=2,'rows'=4,'feat'=4] {'feat','rows'}, dimensions={0} | all-to-all | bytes 131072 | tf_op jit(solution)/shard_map/all_to_all | solution.py:331
  46.1 0.2 reshape.22
  46.3 0.7 %copy.10 = f32[4,4,4,8,32]{4,3,2,1,0:T(8,128)} copy(f32[4,4,4,8,32]{4,2,3,1,0:T(4,128)S(1)} %bitcast.8) | data formatting | bytes 131072 | tf_op jit(solution)/shard_map/transpose | solution.py:335
Async XLA Ops:
  4.0 8.7 %collective-permute-start = (bf16[544,128]{1,0:T(8,128)(2,1)}, bf16[544,128]{1,0:T(8,128)(2,1)S(1)}, u32[]{:S(2)}, u32[]{:S(2)}) collective-permute-start(bf16[544,128]{1,0:T(8,128)(2,1)} %get-tuple-element.9), channel_id=1, source_target_pairs={{0,4},{4,0},{8,12},{12,8},{1,5},{5,1},{9,13},{13,9},{2,6},{6,2},{1... | collective-permute-start | bytes 417800 | tf_op jit(solution)/shard_map/ppermute | solution.py:309
  7.1 13.7 %collective-permute-start.1 = (bf16[544,128]{1,0:T(8,128)(2,1)}, bf16[544,128]{1,0:T(8,128)(2,1)S(1)}, u32[]{:S(2)}, u32[]{:S(2)}) collective-permute-start(bf16[544,128]{1,0:T(8,128)(2,1)} %get-tuple-element.10), channel_id=1, source_target_pairs={{0,8},{4,12},{8,0},{12,4},{1,9},{5,13},{9,1},{13,5},{2,10},{6,14},... | collective-permute-start | bytes 417800 | tf_op jit(solution)/shard_map/ppermute | solution.py:309
  9.6 11.1 %collective-permute-start.2 = (bf16[544,128]{1,0:T(8,128)(2,1)}, bf16[544,128]{1,0:T(8,128)(2,1)S(1)}, u32[]{:S(2)}, u32[]{:S(2)}) collective-permute-start(bf16[544,128]{1,0:T(8,128)(2,1)} %get-tuple-element.11), channel_id=1, source_target_pairs={{0,12},{4,8},{8,4},{12,0},{1,13},{5,9},{9,5},{13,1},{2,14},{6,10},... | collective-permute-start | bytes 417800 | tf_op jit(solution)/shard_map/ppermute | solution.py:309
  20.7 0.9 %copy-start = (bf16[544,128]{1,0:T(8,128)(2,1)S(1)}, bf16[544,128]{1,0:T(8,128)(2,1)}, u32[]{:S(2)}) copy-start(bf16[544,128]{1,0:T(8,128)(2,1)} %get-tuple-element.8.rest_0_) | copy-start | bytes 417796

commit v3 on v2

v3 whole, which is shorter than its diff:
```python
import functools

import jax
import jax.numpy as jnp
from jax import lax
from jax.experimental import pallas as pl
from jax.experimental.pallas import tpu as pltpu
from jax.sharding import PartitionSpec as P

BINS = 256
NODES = 32
HIST = 512
HORIZON = 28
FIRST_DAY = HIST - HORIZON
REGIONS = 10
CHANNELS = 8
TAPS = 4
DILATE = (1, 7, 14, 28)
LEVELS = (0.005, 0.025, 0.165, 0.25, 0.5, 0.75, 0.835, 0.975, 0.995)

LANES = 128
DAYS = 32
REGION_ROW = HORIZON
NODE_ROW = HORIZON + 1
TOTAL_ROW = HORIZON
STORES = 16
PIECES = 3
SCALE = 256.0
BF16 = jnp.bfloat16
F32 = jnp.float32
F8 = jnp.float8_e4m3fn
ROW_BY_ROW = (((1,), (1,)), ((), ()))
VMEM_LIMIT = 24 * 2**20
WHOLE_VMEM = 63 * 2**20


def partner(position, step, count):
    if count & (count - 1) == 0:
        return position ^ step
    return (position + step) % count


def split_parts(values):
    parts = []
    rest = values
    for _ in range(PIECES):
        part = rest.astype(BF16)
        parts.append(part)
        rest = rest - part.astype(F32)
    return parts


def tap_matrix(taps_ref, parity):
    gap = lax.broadcasted_iota(jnp.int32, (DAYS, LANES), 1) - lax.broadcasted_iota(
        jnp.int32, (DAYS, LANES), 0
    )
    first = FIRST_DAY - (HIST - LANES)
    matrix = jnp.zeros((DAYS, LANES), F32)
    for channel in range(parity, CHANNELS, 2):
        for lag in range(TAPS):
            offset = first - 1 - lag * DILATE[(channel // 2) % 4]
            matrix = matrix + jnp.where(
                gap == offset, taps_ref[lag : lag + 1, channel : channel + 1], 0.0
            )
    if parity == 0:
        matrix = matrix - jnp.where(gap == first, 1.0, 0.0)
    day = lax.broadcasted_iota(jnp.int32, (DAYS, LANES), 0)
    return jnp.where(day < HORIZON, matrix, 0.0)


def store_sums(counts_hbm, region_hbm, taps_hbm, sums_ref, counts_ref, region_ref, taps_ref, sems):
    given = (counts_hbm, region_hbm, taps_hbm)
    taken = (counts_ref, region_ref, taps_ref)
    copies = [
        pltpu.make_async_copy(source, target, sems.at[at])
        for at, (source, target) in enumerate(zip(given, taken))
    ]
    for copy in copies:
        copy.start()
    copies[2].wait()
    taps = tap_matrix(taps_ref, 1)
    copies[1].wait()
    series = counts_ref.shape[0]
    store = lax.broadcasted_iota(jnp.int32, (STORES, series), 0)
    pick = jnp.where(store == region_ref[...], 1.0, 0.0).astype(BF16)
    copies[0].wait()
    totals = jnp.dot(pick, counts_ref[...], preferred_element_type=F32)
    forecast = lax.dot_general(
        taps,
        totals[:, HIST - LANES :],
        ROW_BY_ROW,
        precision=lax.Precision.HIGHEST,
        preferred_element_type=F32,
    )
    over_days = lax.dot_general(
        jnp.ones((DAYS, HIST), F32),
        totals,
        ROW_BY_ROW,
        precision=lax.Precision.HIGHEST,
        preferred_element_type=F32,
    )
    row = lax.broadcasted_iota(jnp.int32, (DAYS, STORES), 0)
    forecast = jnp.where(row == TOTAL_ROW, over_days, forecast)
    sums_ref[...] = jnp.concatenate(
        split_parts(forecast) + [jnp.zeros((DAYS, LANES - PIECES * STORES), BF16)], axis=1
    )


def prepare(rows, sums_hbm, counts_ref, region_ref, node_ref, bins_ref, taps_ref, *rest):
    sums_ref, out_refs, (held, sem) = rest[0], rest[1 : 1 + rows], rest[1 + rows :]
    copy = pltpu.make_async_copy(sums_hbm, sums_ref, sem)
    copy.start()
    series = counts_ref.shape[0]
    feats = bins_ref.shape[1] // rows
    pad = held.shape[1]
    me = lax.axis_index("rows")
    counts = counts_ref[...]
    recent = counts_ref[:, HIST - LANES :]

    own_taps = jnp.concatenate(split_parts(tap_matrix(taps_ref, 0)), axis=0)
    own = lax.dot_general(own_taps, recent, ROW_BY_ROW, preferred_element_type=F32)
    own = own[:DAYS] + own[DAYS : 2 * DAYS] + own[2 * DAYS :]
    ones = jnp.ones((8, HIST), BF16)
    level = lax.dot_general(ones, counts, ROW_BY_ROW, preferred_element_type=F32)[:1] / HIST
    own = own / level
    day = lax.broadcasted_iota(jnp.int32, (DAYS, series), 0)
    own = jnp.where(day == REGION_ROW, region_ref[...].astype(F32), own)
    own = jnp.where(day == NODE_ROW, node_ref[...].astype(F32), own)
    own = own.astype(BF16)

    turned = bins_ref[...].astype(F32).T
    for row_block in range(rows):
        part = turned[row_block * feats : (row_block + 1) * feats]
        if pad > feats:
            part = jnp.concatenate([part, jnp.zeros((pad - feats, series), F32)], axis=0)
        held[row_block] = part.astype(BF16)

    height = pad + DAYS
    for step in range(rows):
        bins = held[partner(me, step, rows)]
        for block in range(series // LANES):
            lanes = slice(block * LANES, (block + 1) * LANES)
            out_refs[step][block * height : block * height + pad] = bins[:, lanes]
            out_refs[step][block * height + pad : (block + 1) * height] = own[:, lanes]
    copy.wait()


def shared_forecast(sums_refs):
    sums = jnp.zeros((DAYS, STORES), F32)
    for ref in sums_refs:
        parts = ref[...].astype(F32)
        for piece in range(PIECES):
            sums = sums + parts[:, piece * STORES : (piece + 1) * STORES]
    shared = sums / (sums[TOTAL_ROW : TOTAL_ROW + 1] / HIST + 1.0)
    return jnp.concatenate(split_parts(shared), axis=1)


def quantile_level(quant_ref):
    level = F32(0.0)
    for index, value in enumerate(LEVELS):
        level = jnp.where(quant_ref[0] == index, F32(value), level)
    return level


def series_columns(own, shared, level, cols_ref):
    series = own.shape[1]
    day = lax.broadcasted_iota(jnp.int32, (DAYS, series), 0)
    store = lax.broadcasted_iota(jnp.int32, (PIECES * STORES, series), 0) % STORES
    region = own[REGION_ROW : REGION_ROW + 1].astype(jnp.int32)
    node = own[NODE_ROW : NODE_ROW + 1].astype(jnp.int32)
    pick = jnp.where(store == region, 1.0, 0.0).astype(BF16)
    regional = jnp.dot(shared, pick, preferred_element_type=F32)
    wave = jnp.where(day < HORIZON, jnp.tanh(own + regional), 0.0)
    mean = jnp.sum(wave, axis=0, keepdims=True) / HORIZON
    square = jnp.sum(wave * wave, axis=0, keepdims=True) / HORIZON
    gradient = 0.5 + 0.5 * mean - level
    hessian = 0.5 * (1.0 - square)
    here_node = lax.broadcasted_iota(jnp.int32, (NODES, series), 0) == node
    for part, value in enumerate((gradient, hessian)):
        value = value.astype(BF16).astype(F32) * SCALE
        high = value.astype(F8).astype(F32)
        for offset, piece in ((0, high), (2, value - high)):
            at = (part + offset) * NODES
            cols_ref[at : at + NODES] = jnp.where(here_node, piece, 0.0).astype(F8)


def accumulate(rows, sources, feats, first, last, quant_ref, *refs):
    sums_refs, block_refs, refs = refs[:rows], refs[rows : rows + sources], refs[rows + sources :]
    if not first:
        before_ref, refs = refs[0], refs[1:]
    if last:
        hist_ref, best_ref, bins_held, cols_held, hist_held, sem = refs
    else:
        hist_held, bins_held, cols_held = refs
    series = bins_held.shape[2]
    pad = max(feats, 16)
    height = pad + DAYS
    shared = shared_forecast(sums_refs)
    level = quantile_level(quant_ref)
    for source, ref in enumerate(block_refs):
        both = jnp.concatenate(
            [ref[block * height : (block + 1) * height] for block in range(series // LANES)],
            axis=1,
        ).astype(F32)
        bins_held[source] = (both[:feats] - 128.0).astype(jnp.int32)
        series_columns(both[pad:], shared, level, cols_held.at[source])

    bin_at = lax.broadcasted_iota(jnp.int32, (32, series), 0)

    def products(source, feature):
        bins = jnp.broadcast_to(bins_held[source, pl.ds(feature, 1)], (32, series)).astype(jnp.int8)
        onehot = jnp.concatenate(
            [
                jnp.where(
                    bins == (bin_at + (32 * part - 128)).astype(jnp.int8),
                    jnp.ones((), F8),
                    jnp.zeros((), F8),
                )
                for part in range(BINS // 32)
            ],
            axis=0,
        )
        return lax.dot_general(
            cols_held[source], onehot, ROW_BY_ROW, preferred_element_type=F32
        )

    def one_feature(feature, carry):
        product = products(0, feature)
        if sources > 1:
            product = lax.fori_loop(
                1, sources, lambda at, total: total + products(at, feature), product
            )
        hist = (product[: 2 * NODES] + product[2 * NODES :]) * (1.0 / SCALE)
        if not first:
            hist = hist + before_ref[feature]
        hist_held[feature] = hist
        if last:
            pltpu.make_async_copy(hist_held.at[feature], hist_ref.at[feature], sem).start()
        return carry

    lax.fori_loop(0, feats, one_feature, 0, unroll=min(feats, 8))
    if last:
        best_gains(feats, hist_held, best_ref)
        pltpu.make_async_copy(hist_held, hist_ref, sem).wait()


def best_gains(feats, hist_held, best_ref):
    below = lax.broadcasted_iota(jnp.int32, (BINS, BINS), 0) <= lax.broadcasted_iota(
        jnp.int32, (BINS, BINS), 1
    )
    below = jnp.where(below, 1.0, 0.0).astype(BF16)
    feature_at = lax.broadcasted_iota(jnp.int32, (NODES, LANES), 1)
    last_bin = lax.broadcasted_iota(jnp.int32, (NODES, BINS), 1) == BINS - 1
    group = min(feats, 8)

    def one_group(at, best):
        hist = hist_held[pl.ds(at * group, group)].reshape(group * 2 * NODES, BINS)
        high = hist.astype(BF16)
        low = (hist - high.astype(F32)).astype(BF16)
        left = jnp.dot(high, below, preferred_element_type=F32) + jnp.dot(
            low, below, preferred_element_type=F32
        )
        left = left.reshape(group, 2, NODES, BINS)
        for member in range(group):
            grad, hess = left[member, 0], left[member, 1]
            all_grad, all_hess = grad[:, BINS - 1 :], hess[:, BINS - 1 :]
            over_grad, over_hess = all_grad - grad, all_hess - hess
            gain = grad * grad / (hess + 1.0) + over_grad * over_grad / (over_hess + 1.0)
            gain = jnp.max(jnp.where(last_bin, -jnp.inf, gain), axis=1, keepdims=True)
            gain = gain - all_grad * all_grad / (all_hess + 1.0)
            best = jnp.where(feature_at == at * group + member, gain, best)
        return best

    best = lax.fori_loop(0, feats // group, one_group, jnp.zeros((NODES, LANES), F32))
    best = best.T
    width = LANES // NODES
    packed = jnp.concatenate(
        [best[at * (feats // width) : (at + 1) * (feats // width)] for at in range(width)], axis=1
    )
    for target in range(best_ref.shape[0]):
        best_ref[target] = packed


def shards(daily_unit_counts, region_ids, node_ids, bin_ids, quant_index, filter_kernels):
    rows = lax.axis_size("rows")
    feat_count = lax.axis_size("feat")
    series = daily_unit_counts.shape[0]
    feats = bin_ids.shape[1] // rows
    pad = max(feats, 16)
    height = pad + DAYS
    vmem = pl.BlockSpec(memory_space=pltpu.VMEM)
    smem = pl.BlockSpec(memory_space=pltpu.SMEM)
    hbm = pl.BlockSpec(memory_space=pl.ANY)
    params = pltpu.CompilerParams(vmem_limit_bytes=VMEM_LIMIT)
    regions = region_ids.reshape(1, series)
    nodes = node_ids.reshape(1, series)

    def exchange(array, step):
        pairs = [(at, partner(at, step, rows)) for at in range(rows)]
        return lax.ppermute(array, "rows", pairs)

    sums = pl.pallas_call(
        store_sums,
        out_shape=jax.ShapeDtypeStruct((DAYS, LANES), BF16),
        in_specs=[hbm] * 3,
        out_specs=vmem,
        scratch_shapes=[
            pltpu.VMEM(daily_unit_counts.shape, BF16),
            pltpu.VMEM((1, series), jnp.int32),
            pltpu.VMEM((TAPS, CHANNELS), F32),
            pltpu.SemaphoreType.DMA((3,)),
        ],
        compiler_params=pltpu.CompilerParams(vmem_limit_bytes=WHOLE_VMEM),
        name="store_sums",
    )(daily_unit_counts, regions, filter_kernels.T)
    own_sums, *outgoing = pl.pallas_call(
        functools.partial(prepare, rows),
        out_shape=[jax.ShapeDtypeStruct(sums.shape, BF16)]
        + [jax.ShapeDtypeStruct((series // LANES * height, LANES), BF16)] * rows,
        in_specs=[hbm] + [vmem] * 5,
        out_specs=[vmem] * (1 + rows),
        scratch_shapes=[pltpu.VMEM((rows, pad, series), BF16), pltpu.SemaphoreType.DMA],
        compiler_params=params,
        name="prepare",
    )(sums, daily_unit_counts, regions, nodes, bin_ids, filter_kernels.T)
    sums = [own_sums] + [exchange(sums, step) for step in range(1, rows)]
    arrived = [outgoing[0]]
    for step in range(1, rows):
        block, sums[step] = lax.optimization_barrier((outgoing[step], sums[step]))
        arrived.append(exchange(block, step))

    targets = rows * feat_count
    packed_rows = feats * NODES // LANES
    hist_shape = jax.ShapeDtypeStruct((feats, 2 * NODES, BINS), F32)
    steps = [arrived[at : at + 1] for at in range(min(rows, 4) - 1)]
    steps.append(arrived[len(steps) :])
    histogram = None
    for at, blocks in enumerate(steps):
        first, last = at == 0, at == len(steps) - 1
        count = len(blocks)
        held = [
            pltpu.VMEM((count, feats, series), jnp.int32),
            pltpu.VMEM((count, 4 * NODES, series), F8),
        ]
        operands = [quant_index, *sums, *blocks] + ([] if first else [histogram])
        if last:
            held += [pltpu.VMEM(hist_shape.shape, F32), pltpu.SemaphoreType.DMA]
            out_shape = [hist_shape, jax.ShapeDtypeStruct((targets, packed_rows, LANES), F32)]
            out_specs = [hbm, vmem]
        else:
            out_shape, out_specs = hist_shape, vmem
        histogram = pl.pallas_call(
            functools.partial(accumulate, rows, count, feats, first, last),
            out_shape=out_shape,
            in_specs=[smem] + [vmem] * (len(operands) - 1),
            out_specs=out_specs,
            scratch_shapes=held,
            input_output_aliases={} if first or last else {len(operands) - 1: 0},
            compiler_params=params,
            name=f"accumulate_{at}",
        )(*operands)
    histogram, best = histogram

    gathered = lax.all_to_all(best, ("feat", "rows"), 0, 0, tiled=True)
    width = LANES // NODES
    feature_best = (
        gathered.reshape(feat_count, rows, packed_rows, width, NODES)
        .transpose(0, 1, 3, 2, 4)
        .reshape(feat_count, rows, feats, NODES)
    )
    return histogram.reshape(1, 1, feats, 2, NODES, BINS), feature_best


def solution(mesh):
    in_specs = (
        P(("groups", "rows"), None),
        P(("groups", "rows")),
        P(("groups", "rows")),
        P(("groups", "rows"), "feat"),
        P("groups"),
        P(),
    )
    out_specs = (
        P(("groups", "feat"), "rows", None, None, None, None),
        P("groups", None, None, None),
    )
    return jax.shard_map(shards, mesh=mesh, in_specs=in_specs, out_specs=out_specs, check_vma=False)
```

time: 47.2 us -> 49.8 us (1.055)
  waiting for transfers between devices: 10.4 us -> 2.52 us
  starting transfers between devices: 5.68 us -> 10.1 us
  local copies, waits for them, and re-layouts: 1.79 us -> 5.9 us
  Pallas kernels: 15.9 us -> 18.3 us
  blocking collectives: 11.9 us -> 11.2 us
    ppermute x3 -> x6, waiting for transfers between devices: 10.4 us -> 2.52 us  [exchange(): return lax.ppermute(array, 'rows', pairs)]
    pallas_call x1 -> x5, Pallas kernels: 12.6 us -> 17.7 us  [the longest x4 15.2 us: shards(): pl.pallas_call(functools.partial(accumulate, rows, count, feats, first, l...]
    ppermute x3 -> x6, starting transfers between devices: 5.68 us -> 10.1 us  [exchange(): return lax.ppermute(array, 'rows', pairs)]
    unnamed x2 -> x12, local copies, waits for them, and re-layouts: 0.91 us -> 5.02 us
    pallas_call x1, Pallas kernels: 3.32 us -> 0.6 us  [shards(): pl.pallas_call(functools.partial(prepare, rows), out_shape=[jax.ShapeDtyp...]
    all_to_all x1, blocking collectives: 11.9 us -> 11.2 us  [shards(): gathered = lax.all_to_all(best, ('feat', 'rows'), 0, 0, tiled=True)]
  transfers between devices with their start and end apart: 3 -> 6, of which waited for: 2 -> 1; matrix products, arithmetic and copies ran while one was open for 0% -> 0% of each run, Pallas kernels for 0% -> 20%
where the time goes in v3:
time: 49.8 us; the launch traced here: 49.4 us
  Pallas kernels  18.3 us (37%)
  blocking collectives  11.2 us (22%)
  starting transfers between devices  10.1 us (20%)
  local copies, waits for them, and re-layouts  5.9 us (12%)
  waiting for transfers between devices  2.52 us (5%)
  between operations  1.38 us (3%)
    pallas_call x4, Pallas kernels, shards(): pl.pallas_call(functools.partial(accumulate, rows, count, feats, first, l...  15.2 us
    all_to_all x1, blocking collectives, shards(): gathered = lax.all_to_all(best, ('feat', 'rows'), 0, 0, tiled=True)  11.2 us
    ppermute x6, starting transfers between devices, exchange(): return lax.ppermute(array, 'rows', pairs)  10.1 us
    unnamed x12, local copies, waits for them, and re-layouts  5.02 us
    ppermute x6, waiting for transfers between devices, exchange(): return lax.ppermute(array, 'rows', pairs)  2.52 us
    pallas_call x1, Pallas kernels, shards(): pl.pallas_call(store_sums, out_shape=jax.ShapeDtypeStruct((DAYS, LANES),...  2.41 us
  transfers between devices with their start and end apart: 6, of which 1 were waited for; matrix products, arithmetic and copies ran while one was open for 0% of the time, Pallas kernels for 20%

profile of v3, /device:TPU:0, one launch (start us, length us, event | category | flops | bytes accessed | tf_op | source)
XLA Modules:
  0.0 49.4 jit_solution(17923191835386919939)
XLA Ops:
  0.6 2.4 %store_sums.1.sums_hbm = bf16[32,128]{1,0:T(8,128)(2,1)} custom-call(bf16[1024,512]{1,0:T(8,128)(2,1)} %counts_ref.1, s32[1,1024]{1,0:T(1,128)} %bitcast.8, f32[4,8]{1,0:T(4,128)} %bitcast.10), custom_call_target="tpu_custom_call" | custom-call | tf_op jit(solution)/shard_map/store_sums/pallas_call | solution.py:302
  3.0 3.1 %collective-permute-start = (bf16[32,128]{1,0:T(8,128)(2,1)}, bf16[32,128]{1,0:T(8,128)(2,1)S(1)}, u32[]{:S(2)}, u32[]{:S(2)}) collective-permute-start(bf16[32,128]{1,0:T(8,128)(2,1)} %store_sums.1.sums_hbm), channel_id=1, source_target_pairs={{0,4},{4,0},{8,12},{12,8},{1,5},{5,1},{9,13},{13,9},{2,6},{6,2},{1... | collective-permute-start | bytes 24584 | tf_op jit(solution)/shard_map/ppermute | solution.py:300
  6.1 2.6 %collective-permute-start.1 = (bf16[32,128]{1,0:T(8,128)(2,1)}, bf16[32,128]{1,0:T(8,128)(2,1)S(1)}, u32[]{:S(2)}, u32[]{:S(2)}) collective-permute-start(bf16[32,128]{1,0:T(8,128)(2,1)} %store_sums.1.sums_hbm), channel_id=1, source_target_pairs={{0,8},{4,12},{8,0},{12,4},{1,9},{5,13},{9,1},{13,5},{2,10},{6,14},... | collective-permute-start | bytes 24584 | tf_op jit(solution)/shard_map/ppermute | solution.py:300
  8.7 0.0 collective-permute-start.2
  8.7 0.0 copy-start
  8.7 1.2 %copy-done = bf16[1024,512]{1,0:T(8,128)(2,1)S(1)} copy-done((bf16[1024,512]{1,0:T(8,128)(2,1)S(1)}, bf16[1024,512]{1,0:T(8,128)(2,1)}, u32[]{:S(2)}) %copy-start) | copy-done | bytes 1048600
  10.0 0.0 copy-start.1
  10.0 1.0 %copy-done.1 = s32[1024,128]{1,0:T(8,128)S(1)} copy-done((s32[1024,128]{1,0:T(8,128)S(1)}, s32[1024,128]{1,0:T(8,128)}, u32[]{:S(2)}) %copy-start.1) | copy-done | bytes 524312
  11.0 0.0 copy-start.2
  11.0 0.7 %copy-done.2 = bf16[32,128]{1,0:T(8,128)(2,1)S(1)} copy-done((bf16[32,128]{1,0:T(8,128)(2,1)S(1)}, bf16[32,128]{1,0:T(8,128)(2,1)}, u32[]{:S(2)}) %copy-start.2) | copy-done | bytes 8216
  11.7 0.0 copy-start.3
  11.7 0.7 %copy-done.3 = s32[1024]{0:T(1024)S(1)} copy-done((s32[1024]{0:T(1024)S(1)}, s32[1024]{0:T(1024)}, u32[]{:S(2)}) %copy-start.3) | copy-done | bytes 4120
  12.4 0.0 copy-start.4
  12.4 0.7 %copy-done.4 = f32[8,4]{0,1:T(4,128)S(1)} copy-done((f32[8,4]{0,1:T(4,128)S(1)}, f32[8,4]{0,1:T(4,128)}, u32[]{:S(2)}) %copy-start.4) | copy-done | bytes 152
  13.1 0.7 %copy-done.5 = s32[1024]{0:T(1024)S(1)} copy-done((s32[1024]{0:T(1024)S(1)}, s32[1024]{0:T(1024)}, u32[]{:S(2)}) %copy-start.5) | copy-done | bytes 4120
  13.7 0.6 %prepare.1 = (bf16[32,128]{1,0:T(8,128)(2,1)S(1)}, bf16[512,128]{1,0:T(8,128)(2,1)S(1)}, bf16[512,128]{1,0:T(8,128)(2,1)S(1)}, bf16[512,128]{1,0:T(8,128)(2,1)S(1)}, bf16[512,128]{1,0:T(8,128)(2,1)S(1)}) custom-call(bf16[32,128]{1,0:T(8,128)(2,1)S(1)} %copy-done.2, bf16[1024,512]{1,0:T(8,128)(2,1)S(1)} %copy-done, s32[1,1024]{1,0:T(1,128)S(1)} %bitcast.9, ...), custom_call_target="tpu_custom_call" | custom-call | tf_op jit(solution)/shard_map/prepare/pallas_call | solution.py:316
  14.4 0.0 collective-permute-done.refs_1_
  14.4 0.0 collective-permute-done.1.refs_2_
  14.4 0.0 collective-permute-done.2.refs_3_
  14.4 1.0 %collective-permute-start.5 = (bf16[512,128]{1,0:T(8,128)(2,1)S(1)}, bf16[512,128]{1,0:T(8,128)(2,1)S(1)}, u32[]{:S(2)}, u32[]{:S(2)}) collective-permute-start(bf16[512,128]{1,0:T(8,128)(2,1)S(1)} %get-tuple-element.24), channel_id=1, source_target_pairs={{0,4},{4,0},{8,12},{12,8},{1,5},{5,1},{9,13},{13,9},{2,6},{6,2},{1... | collective-permute-start | bytes 393224 | tf_op jit(solution)/shard_map/ppermute | solution.py:300
  15.3 3.5 %collective-permute-start.4 = (bf16[512,128]{1,0:T(8,128)(2,1)S(1)}, bf16[512,128]{1,0:T(8,128)(2,1)S(1)}, u32[]{:S(2)}, u32[]{:S(2)}) collective-permute-start(bf16[512,128]{1,0:T(8,128)(2,1)S(1)} %get-tuple-element.23), channel_id=1, source_target_pairs={{0,8},{4,12},{8,0},{12,4},{1,9},{5,13},{9,1},{13,5},{2,10},{6,14},... | collective-permute-start | bytes 393224 | tf_op jit(solution)/shard_map/ppermute | solution.py:300
  18.8 0.0 collective-permute-start.3
  19.5 3.1 %accumulate_0.1.refs_5_ = f32[32,64,256]{2,1,0:T(8,128)S(1)} custom-call(s32[1]{0:T(128)S(6)} %copy.15.quant_ref, bf16[32,128]{1,0:T(8,128)(2,1)S(1)} %get-tuple-element.15.refs_0_, bf16[32,128]{1,0:T(8,128)(2,1)S(1)} %collective-permute-done.refs_1_, bf16[32,128]{1,0:T(8,128)(2,1)S(1)} %collective-permute-done.1.refs_2_, ...), custom_call_target="tpu_custom_call" | custom-call | tf_op jit(solution)/shard_map/accumulate_0/pallas_call | solution.py:352
  22.6 0.0 collective-permute-done.5.refs_4_
  22.6 3.1 %accumulate_1.1.refs_5_ = f32[32,64,256]{2,1,0:T(8,128)S(1)} custom-call(s32[1]{0:T(128)S(6)} %copy.15.quant_ref, bf16[32,128]{1,0:T(8,128)(2,1)S(1)} %get-tuple-element.15.refs_0_, bf16[32,128]{1,0:T(8,128)(2,1)S(1)} %collective-permute-done.refs_1_, bf16[32,128]{1,0:T(8,128)(2,1)S(1)} %collective-permute-done.1.refs_2_, ...), custom_call_target="tpu_custom_call", output_to_operand_aliasing={{}: (6, {})} | custom-call | tf_op jit(solution)/shard_map/accumulate_1/pallas_call | solution.py:352
  25.8 2.5 %collective-permute-done.4.refs_4_ = bf16[512,128]{1,0:T(8,128)(2,1)S(1)} collective-permute-done((bf16[512,128]{1,0:T(8,128)(2,1)S(1)}, bf16[512,128]{1,0:T(8,128)(2,1)S(1)}, u32[]{:S(2)}, u32[]{:S(2)}) %collective-permute-start.4) | collective-permute-done | bytes 131104 | tf_op jit(solution)/shard_map/ppermute | solution.py:300
  28.3 3.1 %accumulate_2.1.refs_5_ = f32[32,64,256]{2,1,0:T(8,128)S(1)} custom-call(s32[1]{0:T(128)S(6)} %copy.15.quant_ref, bf16[32,128]{1,0:T(8,128)(2,1)S(1)} %get-tuple-element.15.refs_0_, bf16[32,128]{1,0:T(8,128)(2,1)S(1)} %collective-permute-done.refs_1_, bf16[32,128]{1,0:T(8,128)(2,1)S(1)} %collective-permute-done.1.refs_2_, ...), custom_call_target="tpu_custom_call", output_to_operand_aliasing={{}: (6, {})} | custom-call | tf_op jit(solution)/shard_map/accumulate_2/pallas_call | solution.py:352
  31.4 0.0 collective-permute-done.3.refs_4_
  31.4 5.9 %accumulate_3.1 = (f32[32,64,256]{2,1,0:T(8,128)}, f32[16,8,128]{2,1,0:T(8,128)S(1)}) custom-call(s32[1]{0:T(128)S(6)} %copy.15.quant_ref, bf16[32,128]{1,0:T(8,128)(2,1)S(1)} %get-tuple-element.15.refs_0_, bf16[32,128]{1,0:T(8,128)(2,1)S(1)} %collective-permute-done.refs_1_, bf16[32,128]{1,0:T(8,128)(2,1)S(1)} %collective-permute-done.1.refs_2_, ...), custom_call_target="tpu_custom_call" | custom-call | tf_op jit(solution)/shard_map/accumulate_3/pallas_call | solution.py:352
  37.3 11.2 %all_to_all.5 = f32[16,8,128]{2,1,0:T(8,128)S(1)} all-to-all(f32[16,8,128]{2,1,0:T(8,128)S(1)} %get-tuple-element.27), channel_id=1, replica_groups=mesh['groups'=2,'rows'=4,'feat'=4] {'feat','rows'}, dimensions={0} | all-to-all | bytes 131072 | tf_op jit(solution)/shard_map/all_to_all | solution.py:364
  48.5 0.2 reshape.22
  48.6 0.7 %copy.12 = f32[4,4,4,8,32]{4,3,2,1,0:T(8,128)} copy(f32[4,4,4,8,32]{4,2,3,1,0:T(4,128)S(1)} %bitcast.13) | data formatting | bytes 131072 | tf_op jit(solution)/shard_map/transpose | solution.py:368
  (1 shorter events, 0.0 us)
Async XLA Ops:
  3.0 11.3 %collective-permute-start = (bf16[32,128]{1,0:T(8,128)(2,1)}, bf16[32,128]{1,0:T(8,128)(2,1)S(1)}, u32[]{:S(2)}, u32[]{:S(2)}) collective-permute-start(bf16[32,128]{1,0:T(8,128)(2,1)} %store_sums.1.sums_hbm), channel_id=1, source_target_pairs={{0,4},{4,0},{8,12},{12,8},{1,5},{5,1},{9,13},{13,9},{2,6},{6,2},{1... | collective-permute-start | bytes 24584 | tf_op jit(solution)/shard_map/ppermute | solution.py:300
  6.1 8.2 %collective-permute-start.1 = (bf16[32,128]{1,0:T(8,128)(2,1)}, bf16[32,128]{1,0:T(8,128)(2,1)S(1)}, u32[]{:S(2)}, u32[]{:S(2)}) collective-permute-start(bf16[32,128]{1,0:T(8,128)(2,1)} %store_sums.1.sums_hbm), channel_id=1, source_target_pairs={{0,8},{4,12},{8,0},{12,4},{1,9},{5,13},{9,1},{13,5},{2,10},{6,14},... | collective-permute-start | bytes 24584 | tf_op jit(solution)/shard_map/ppermute | solution.py:300
  8.7 5.7 %collective-permute-start.2 = (bf16[32,128]{1,0:T(8,128)(2,1)}, bf16[32,128]{1,0:T(8,128)(2,1)S(1)}, u32[]{:S(2)}, u32[]{:S(2)}) collective-permute-start(bf16[32,128]{1,0:T(8,128)(2,1)} %store_sums.1.sums_hbm), channel_id=1, source_target_pairs={{0,12},{4,8},{8,4},{12,0},{1,13},{5,9},{9,5},{13,1},{2,14},{6,10},... | collective-permute-start | bytes 24584 | tf_op jit(solution)/shard_map/ppermute | solution.py:300
  8.7 1.2 %copy-start = (bf16[1024,512]{1,0:T(8,128)(2,1)S(1)}, bf16[1024,512]{1,0:T(8,128)(2,1)}, u32[]{:S(2)}) copy-start(bf16[1024,512]{1,0:T(8,128)(2,1)} %counts_ref.1) | copy-start | bytes 3145732
  10.0 1.0 %copy-start.1 = (s32[1024,128]{1,0:T(8,128)S(1)}, s32[1024,128]{1,0:T(8,128)}, u32[]{:S(2)}) copy-start(s32[1024,128]{1,0:T(8,128)} %bins_ref.1) | copy-start | bytes 1572868
  11.0 0.7 %copy-start.2 = (bf16[32,128]{1,0:T(8,128)(2,1)S(1)}, bf16[32,128]{1,0:T(8,128)(2,1)}, u32[]{:S(2)}) copy-start(bf16[32,128]{1,0:T(8,128)(2,1)} %store_sums.1.sums_hbm) | copy-start | bytes 24580
  11.7 0.7 %copy-start.3 = (s32[1024]{0:T(1024)S(1)}, s32[1024]{0:T(1024)}, u32[]{:S(2)}) copy-start(s32[1024]{0:T(1024)} %param.7) | copy-start | bytes 12292
  12.4 0.7 %copy-start.4 = (f32[8,4]{0,1:T(4,128)S(1)}, f32[8,4]{0,1:T(4,128)}, u32[]{:S(2)}) copy-start(f32[8,4]{0,1:T(4,128)} %param.11) | copy-start | bytes 388
  13.1 0.7 %copy-start.5 = (s32[1024]{0:T(1024)S(1)}, s32[1024]{0:T(1024)}, u32[]{:S(2)}) copy-start(s32[1024]{0:T(1024)} %param.8) | copy-start | bytes 12292
  14.4 8.2 %collective-permute-start.5 = (bf16[512,128]{1,0:T(8,128)(2,1)S(1)}, bf16[512,128]{1,0:T(8,128)(2,1)S(1)}, u32[]{:S(2)}, u32[]{:S(2)}) collective-permute-start(bf16[512,128]{1,0:T(8,128)(2,1)S(1)} %get-tuple-element.24), channel_id=1, source_target_pairs={{0,4},{4,0},{8,12},{12,8},{1,5},{5,1},{9,13},{13,9},{2,6},{6,2},{1... | collective-permute-start | bytes 393224 | tf_op jit(solution)/shard_map/ppermute | solution.py:300
  15.3 12.9 %collective-permute-start.4 = (bf16[512,128]{1,0:T(8,128)(2,1)S(1)}, bf16[512,128]{1,0:T(8,128)(2,1)S(1)}, u32[]{:S(2)}, u32[]{:S(2)}) collective-permute-start(bf16[512,128]{1,0:T(8,128)(2,1)S(1)} %get-tuple-element.23), channel_id=1, source_target_pairs={{0,8},{4,12},{8,0},{12,4},{1,9},{5,13},{9,1},{13,5},{2,10},{6,14},... | collective-permute-start | bytes 393224 | tf_op jit(solution)/shard_map/ppermute | solution.py:300
  18.8 12.6 %collective-permute-start.3 = (bf16[512,128]{1,0:T(8,128)(2,1)S(1)}, bf16[512,128]{1,0:T(8,128)(2,1)S(1)}, u32[]{:S(2)}, u32[]{:S(2)}) collective-permute-start(bf16[512,128]{1,0:T(8,128)(2,1)S(1)} %get-tuple-element.22), channel_id=1, source_target_pairs={{0,12},{4,8},{8,4},{12,0},{1,13},{5,9},{9,5},{13,1},{2,14},{6,10},... | collective-permute-start | bytes 393224 | tf_op jit(solution)/shard_map/ppermute | solution.py:300

commit v4 on v3

--- a/solution.py
+++ b/solution.py
@@ -31,7 +31,6 @@
 F8 = jnp.float8_e4m3fn
 ROW_BY_ROW = (((1,), (1,)), ((), ()))
 VMEM_LIMIT = 24 * 2**20
-WHOLE_VMEM = 63 * 2**20
 
 
 def partner(position, step, count):
@@ -68,25 +67,49 @@
     return jnp.where(day < HORIZON, matrix, 0.0)
 
 
-def store_sums(counts_hbm, region_hbm, taps_hbm, sums_ref, counts_ref, region_ref, taps_ref, sems):
-    given = (counts_hbm, region_hbm, taps_hbm)
-    taken = (counts_ref, region_ref, taps_ref)
+def prepare(rows, *refs):
+    given, refs = refs[:5], refs[5:]
+    sums_ref, out_refs, refs = refs[0], refs[1 : 1 + rows], refs[1 + rows :]
+    taken, (held, sems) = refs[:5], refs[5:]
+    counts_ref, region_ref, node_ref, bins_ref, taps_ref = taken
     copies = [
         pltpu.make_async_copy(source, target, sems.at[at])
         for at, (source, target) in enumerate(zip(given, taken))
     ]
-    for copy in copies:
-        copy.start()
-    copies[2].wait()
-    taps = tap_matrix(taps_ref, 1)
-    copies[1].wait()
+    for at in (4, 3, 0, 1, 2):
+        copies[at].start()
     series = counts_ref.shape[0]
+    feats = bins_ref.shape[1] // rows
+    pad = held.shape[1]
+    height = pad + DAYS
+    me = lax.axis_index("rows")
+
+    copies[4].wait()
+    own_taps = jnp.concatenate(split_parts(tap_matrix(taps_ref, 0)), axis=0)
+    store_taps = tap_matrix(taps_ref, 1)
+
+    copies[3].wait()
+    turned = bins_ref[...].astype(F32).T
+    for row_block in range(rows):
+        part = turned[row_block * feats : (row_block + 1) * feats]
+        if pad > feats:
+            part = jnp.concatenate([part, jnp.zeros((pad - feats, series), F32)], axis=0)
+        held[row_block] = part.astype(BF16)
+    for step in range(rows):
+        bins = held[partner(me, step, rows)]
+        for block in range(series // LANES):
+            lanes = slice(block * LANES, (block + 1) * LANES)
+            out_refs[step][block * height : block * height + pad] = bins[:, lanes]
+
+    for at in (0, 1, 2):
+        copies[at].wait()
+    counts = counts_ref[...]
+    recent = counts_ref[:, HIST - LANES :]
     store = lax.broadcasted_iota(jnp.int32, (STORES, series), 0)
     pick = jnp.where(store == region_ref[...], 1.0, 0.0).astype(BF16)
-    copies[0].wait()
-    totals = jnp.dot(pick, counts_ref[...], preferred_element_type=F32)
+    totals = jnp.dot(pick, counts, preferred_element_type=F32)
     forecast = lax.dot_general(
-        taps,
+        store_taps,
         totals[:, HIST - LANES :],
         ROW_BY_ROW,
         precision=lax.Precision.HIGHEST,
@@ -105,19 +128,6 @@
         split_parts(forecast) + [jnp.zeros((DAYS, LANES - PIECES * STORES), BF16)], axis=1
     )
 
-
-def prepare(rows, sums_hbm, counts_ref, region_ref, node_ref, bins_ref, taps_ref, *rest):
-    sums_ref, out_refs, (held, sem) = rest[0], rest[1 : 1 + rows], rest[1 + rows :]
-    copy = pltpu.make_async_copy(sums_hbm, sums_ref, sem)
-    copy.start()
-    series = counts_ref.shape[0]
-    feats = bins_ref.shape[1] // rows
-    pad = held.shape[1]
-    me = lax.axis_index("rows")
-    counts = counts_ref[...]
-    recent = counts_ref[:, HIST - LANES :]
-
-    own_taps = jnp.concatenate(split_parts(tap_matrix(taps_ref, 0)), axis=0)
     own = lax.dot_general(own_taps, recent, ROW_BY_ROW, preferred_element_type=F32)
     own = own[:DAYS] + own[DAYS : 2 * DAYS] + own[2 * DAYS :]
     ones = jnp.ones((8, HIST), BF16)
@@ -127,22 +137,10 @@
     own = jnp.where(day == REGION_ROW, region_ref[...].astype(F32), own)
     own = jnp.where(day == NODE_ROW, node_ref[...].astype(F32), own)
     own = own.astype(BF16)
-
-    turned = bins_ref[...].astype(F32).T
-    for row_block in range(rows):
-        part = turned[row_block * feats : (row_block + 1) * feats]
-        if pad > feats:
-            part = jnp.concatenate([part, jnp.zeros((pad - feats, series), F32)], axis=0)
-        held[row_block] = part.astype(BF16)
-
-    height = pad + DAYS
     for step in range(rows):
-        bins = held[partner(me, step, rows)]
         for block in range(series // LANES):
             lanes = slice(block * LANES, (block + 1) * LANES)
-            out_refs[step][block * height : block * height + pad] = bins[:, lanes]
             out_refs[step][block * height + pad : (block + 1) * height] = own[:, lanes]
-    copy.wait()
 
 
 def shared_forecast(sums_refs):
@@ -224,7 +222,7 @@
             cols_held[source], onehot, ROW_BY_ROW, preferred_element_type=F32
         )
 
-    def one_feature(feature, carry):
+    def one_feature(feature):
         product = products(0, feature)
         if sources > 1:
             product = lax.fori_loop(
@@ -236,42 +234,24 @@
         hist_held[feature] = hist
         if last:
             pltpu.make_async_copy(hist_held.at[feature], hist_ref.at[feature], sem).start()
-        return carry
-
-    lax.fori_loop(0, feats, one_feature, 0, unroll=min(feats, 8))
-    if last:
-        best_gains(feats, hist_held, best_ref)
-        pltpu.make_async_copy(hist_held, hist_ref, sem).wait()
-
-
-def best_gains(feats, hist_held, best_ref):
-    below = lax.broadcasted_iota(jnp.int32, (BINS, BINS), 0) <= lax.broadcasted_iota(
-        jnp.int32, (BINS, BINS), 1
-    )
-    below = jnp.where(below, 1.0, 0.0).astype(BF16)
-    feature_at = lax.broadcasted_iota(jnp.int32, (NODES, LANES), 1)
-    last_bin = lax.broadcasted_iota(jnp.int32, (NODES, BINS), 1) == BINS - 1
+
     group = min(feats, 8)
 
-    def one_group(at, best):
-        hist = hist_held[pl.ds(at * group, group)].reshape(group * 2 * NODES, BINS)
-        high = hist.astype(BF16)
-        low = (hist - high.astype(F32)).astype(BF16)
-        left = jnp.dot(high, below, preferred_element_type=F32) + jnp.dot(
-            low, below, preferred_element_type=F32
-        )
-        left = left.reshape(group, 2, NODES, BINS)
+    def one_group(at):
         for member in range(group):
-            grad, hess = left[member, 0], left[member, 1]
-            all_grad, all_hess = grad[:, BINS - 1 :], hess[:, BINS - 1 :]
-            over_grad, over_hess = all_grad - grad, all_hess - hess
-            gain = grad * grad / (hess + 1.0) + over_grad * over_grad / (over_hess + 1.0)
-            gain = jnp.max(jnp.where(last_bin, -jnp.inf, gain), axis=1, keepdims=True)
-            gain = gain - all_grad * all_grad / (all_hess + 1.0)
-            best = jnp.where(feature_at == at * group + member, gain, best)
-        return best
-
-    best = lax.fori_loop(0, feats // group, one_group, jnp.zeros((NODES, LANES), F32))
+            one_feature(at * group + member)
+
+    if not last:
+        lax.fori_loop(0, feats // group, lambda at, carry: (one_group(at), carry)[1], 0)
+        return
+
+    def beside(at, best):
+        one_group(at)
+        return group_gains(hist_held, at - 1, group, best)
+
+    one_group(0)
+    best = lax.fori_loop(1, feats // group, beside, jnp.zeros((NODES, LANES), F32))
+    best = group_gains(hist_held, feats // group - 1, group, best)
     best = best.T
     width = LANES // NODES
     packed = jnp.concatenate(
@@ -279,6 +259,32 @@
     )
     for target in range(best_ref.shape[0]):
         best_ref[target] = packed
+    pltpu.make_async_copy(hist_held, hist_ref, sem).wait()
+
+
+def group_gains(hist_held, at, group, best):
+    below = lax.broadcasted_iota(jnp.int32, (BINS, BINS), 0) <= lax.broadcasted_iota(
+        jnp.int32, (BINS, BINS), 1
+    )
+    below = jnp.where(below, 1.0, 0.0).astype(BF16)
+    feature_at = lax.broadcasted_iota(jnp.int32, (NODES, LANES), 1)
+    last_bin = lax.broadcasted_iota(jnp.int32, (NODES, BINS), 1) == BINS - 1
+    hist = hist_held[pl.ds(at * group, group)].reshape(group * 2 * NODES, BINS)
+    high = hist.astype(BF16)
+    low = (hist - high.astype(F32)).astype(BF16)
+    left = jnp.dot(high, below, preferred_element_type=F32) + jnp.dot(
+        low, below, preferred_element_type=F32
+    )
+    left = left.reshape(group, 2, NODES, BINS)
+    for member in range(group):
+        grad, hess = left[member, 0], left[member, 1]
+        all_grad, all_hess = grad[:, BINS - 1 :], hess[:, BINS - 1 :]
+        over_grad, over_hess = all_grad - grad, all_hess - hess
+        gain = grad * grad / (hess + 1.0) + over_grad * over_grad / (over_hess + 1.0)
+        gain = jnp.max(jnp.where(last_bin, -jnp.inf, gain), axis=1, keepdims=True)
+        gain = gain - all_grad * all_grad / (all_hess + 1.0)
+        best = jnp.where(feature_at == at * group + member, gain, best)
+    return best
 
 
 def shards(daily_unit_counts, region_ids, node_ids, bin_ids, quant_index, filter_kernels):
@@ -299,34 +305,35 @@
         pairs = [(at, partner(at, step, rows)) for at in range(rows)]
         return lax.ppermute(array, "rows", pairs)
 
-    sums = pl.pallas_call(
-        store_sums,
-        out_shape=jax.ShapeDtypeStruct((DAYS, LANES), BF16),
-        in_specs=[hbm] * 3,
-        out_specs=vmem,
+    sums, *outgoing = pl.pallas_call(
+        functools.partial(prepare, rows),
+        out_shape=[jax.ShapeDtypeStruct((DAYS, LANES), BF16)]
+        + [jax.ShapeDtypeStruct((series // LANES * height, LANES), BF16)] * rows,
+        in_specs=[hbm] * 5,
+        out_specs=[vmem] * (1 + rows),
         scratch_shapes=[
             pltpu.VMEM(daily_unit_counts.shape, BF16),
             pltpu.VMEM((1, series), jnp.int32),
+            pltpu.VMEM((1, series), jnp.int32),
+            pltpu.VMEM(bin_ids.shape, jnp.int32),
             pltpu.VMEM((TAPS, CHANNELS), F32),
-            pltpu.SemaphoreType.DMA((3,)),
+            pltpu.VMEM((rows, pad, series), BF16),
+            pltpu.SemaphoreType.DMA((5,)),
         ],
-        compiler_params=pltpu.CompilerParams(vmem_limit_bytes=WHOLE_VMEM),
-        name="store_sums",
-    )(daily_unit_counts, regions, filter_kernels.T)
-    own_sums, *outgoing = pl.pallas_call(
-        functools.partial(prepare, rows),
-        out_shape=[jax.ShapeDtypeStruct(sums.shape, BF16)]
-        + [jax.ShapeDtypeStruct((series // LANES * height, LANES), BF16)] * rows,
-        in_specs=[hbm] + [vmem] * 5,
-        out_specs=[vmem] * (1 + rows),
-        scratch_shapes=[pltpu.VMEM((rows, pad, series), BF16), pltpu.SemaphoreType.DMA],
         compiler_params=params,
         name="prepare",
-    )(sums, daily_unit_counts, regions, nodes, bin_ids, filter_kernels.T)
-    sums = [own_sums] + [exchange(sums, step) for step in range(1, rows)]
+    )(
+        *(
+            pltpu.with_memory_space_constraint(array, pltpu.HBM)
+            for array in (daily_unit_counts, regions, nodes, bin_ids, filter_kernels.T)
+        )
+    )
+    sums = [sums] + [exchange(sums, step) for step in range(1, rows)]
     arrived = [outgoing[0]]
     for step in range(1, rows):
-        block, sums[step] = lax.optimization_barrier((outgoing[step], sums[step]))
+        block = outgoing[step]
+        if step == rows - 1:
+            block, sums[1:] = lax.optimization_barrier((block, sums[1:]))
         arrived.append(exchange(block, step))
 
     targets = rows * feat_count

time: 49.8 us -> 43.6 us (0.88)
  local copies, waits for them, and re-layouts: 5.9 us -> 0.88 us
  blocking collectives: 11.2 us -> 12.6 us
  waiting for transfers between devices: 2.52 us -> 1.15 us
  Pallas kernels: 18.3 us -> 17.3 us
    unnamed x12 -> x0, local copies, waits for them, and re-layouts: 5.02 us -> none
    pallas_call x1 -> x0, Pallas kernels: 2.41 us -> none  [shards(): pl.pallas_call(store_sums, out_shape=jax.ShapeDtypeStruct((DAYS, LANES),...]
    pallas_call x1, Pallas kernels: 0.6 us -> 2.27 us  [shards(): pl.pallas_call(functools.partial(prepare, rows), out_shape=[jax.ShapeDtyp...]
    all_to_all x1, blocking collectives: 11.2 us -> 12.6 us  [shards(): gathered = lax.all_to_all(best, ('feat', 'rows'), 0, 0, tiled=True)]
    ppermute x6, waiting for transfers between devices: 2.52 us -> 1.15 us  [exchange(): return lax.ppermute(array, 'rows', pairs)]
  transfers between devices with their start and end apart: 6 -> 6, of which waited for: 1 -> 1; matrix products, arithmetic and copies ran while one was open for 0% -> 0% of each run, Pallas kernels for 20% -> 22%
where the time goes in v4:
time: 43.6 us; the launch traced here: 43.4 us
  Pallas kernels  17.3 us (40%)
  blocking collectives  12.6 us (29%)
  starting transfers between devices  10.1 us (23%)
  between operations  1.36 us (3%)
  waiting for transfers between devices  1.15 us (3%)
  local copies, waits for them, and re-layouts  0.88 us (2%)
    pallas_call x4, Pallas kernels, shards(): pl.pallas_call(functools.partial(accumulate, rows, count, feats, first, l...  15.1 us
    all_to_all x1, blocking collectives, shards(): gathered = lax.all_to_all(best, ('feat', 'rows'), 0, 0, tiled=True)  12.6 us
    ppermute x6, starting transfers between devices, exchange(): return lax.ppermute(array, 'rows', pairs)  10.1 us
    pallas_call x1, Pallas kernels, shards(): pl.pallas_call(functools.partial(prepare, rows), out_shape=[jax.ShapeDtyp...  2.27 us
    ppermute x6, waiting for transfers between devices, exchange(): return lax.ppermute(array, 'rows', pairs)  1.15 us
  transfers between devices with their start and end apart: 6, of which 1 were waited for; matrix products, arithmetic and copies ran while one was open for 0% of the time, Pallas kernels for 22%

profile of v4, /device:TPU:0, one launch (start us, length us, event | category | flops | bytes accessed | tf_op | source)
XLA Modules:
  0.0 43.4 jit_solution(7166847416747195752)
XLA Ops:
  0.6 2.3 %prepare.1 = (bf16[32,128]{1,0:T(8,128)(2,1)S(1)}, bf16[512,128]{1,0:T(8,128)(2,1)S(1)}, bf16[512,128]{1,0:T(8,128)(2,1)S(1)}, bf16[512,128]{1,0:T(8,128)(2,1)S(1)}, bf16[512,128]{1,0:T(8,128)(2,1)S(1)}) custom-call(bf16[1024,512]{1,0:T(8,128)(2,1)} %refs_0_.1, s32[1,1024]{1,0:T(1,128)} %bitcast.10, s32[1,1024]{1,0:T(1,128)} %bitcast.11, ...), custom_call_target="tpu_custom_call" | custom-call | tf_op jit(solution)/shard_map/prepare/pallas_call | solution.py:308
  2.9 5.1 %collective-permute-start.2 = (bf16[32,128]{1,0:T(8,128)(2,1)S(1)}, bf16[32,128]{1,0:T(8,128)(2,1)S(1)}, u32[]{:S(2)}, u32[]{:S(2)}) collective-permute-start(bf16[32,128]{1,0:T(8,128)(2,1)S(1)} %get-tuple-element.13.refs_0_), channel_id=1, source_target_pairs={{0,12},{4,8},{8,4},{12,0},{1,13},{5,9},{9,5},{13,1},{2,14},{6,10},... | collective-permute-start | bytes 24584 | tf_op jit(solution)/shard_map/ppermute | solution.py:306
  8.0 0.0 collective-permute-start.1
  8.0 0.6 %collective-permute-start = (bf16[32,128]{1,0:T(8,128)(2,1)S(1)}, bf16[32,128]{1,0:T(8,128)(2,1)S(1)}, u32[]{:S(2)}, u32[]{:S(2)}) collective-permute-start(bf16[32,128]{1,0:T(8,128)(2,1)S(1)} %get-tuple-element.13.refs_0_), channel_id=1, source_target_pairs={{0,4},{4,0},{8,12},{12,8},{1,5},{5,1},{9,13},{13,9},{2,6},{6,2},{1... | collective-permute-start | bytes 24584 | tf_op jit(solution)/shard_map/ppermute | solution.py:306
  8.7 2.3 %collective-permute-start.4 = (bf16[512,128]{1,0:T(8,128)(2,1)S(1)}, bf16[512,128]{1,0:T(8,128)(2,1)S(1)}, u32[]{:S(2)}, u32[]{:S(2)}) collective-permute-start(bf16[512,128]{1,0:T(8,128)(2,1)S(1)} %get-tuple-element.19), channel_id=1, source_target_pairs={{0,8},{4,12},{8,0},{12,4},{1,9},{5,13},{9,1},{13,5},{2,10},{6,14},... | collective-permute-start | bytes 393224 | tf_op jit(solution)/shard_map/ppermute | solution.py:306
  10.9 2.0 %collective-permute-start.5 = (bf16[512,128]{1,0:T(8,128)(2,1)S(1)}, bf16[512,128]{1,0:T(8,128)(2,1)S(1)}, u32[]{:S(2)}, u32[]{:S(2)}) collective-permute-start(bf16[512,128]{1,0:T(8,128)(2,1)S(1)} %get-tuple-element.20), channel_id=1, source_target_pairs={{0,4},{4,0},{8,12},{12,8},{1,5},{5,1},{9,13},{13,9},{2,6},{6,2},{1... | collective-permute-start | bytes 393224 | tf_op jit(solution)/shard_map/ppermute | solution.py:306
  13.0 0.0 collective-permute-done.2.refs_3_
  13.0 1.1 %collective-permute-done.1.refs_2_ = bf16[32,128]{1,0:T(8,128)(2,1)S(1)} collective-permute-done((bf16[32,128]{1,0:T(8,128)(2,1)S(1)}, bf16[32,128]{1,0:T(8,128)(2,1)S(1)}, u32[]{:S(2)}, u32[]{:S(2)}) %collective-permute-start.1) | collective-permute-done | bytes 8224 | tf_op jit(solution)/shard_map/ppermute | solution.py:306
  14.1 0.0 collective-permute-done.refs_1_
  14.1 0.0 collective-permute-start.3
  14.8 3.1 %accumulate_0.1.refs_5_ = f32[32,64,256]{2,1,0:T(8,128)S(1)} custom-call(s32[1]{0:T(128)S(6)} %copy.15.quant_ref, bf16[32,128]{1,0:T(8,128)(2,1)S(1)} %get-tuple-element.13.refs_0_, bf16[32,128]{1,0:T(8,128)(2,1)S(1)} %collective-permute-done.refs_1_, bf16[32,128]{1,0:T(8,128)(2,1)S(1)} %collective-permute-done.1.refs_2_, ...), custom_call_target="tpu_custom_call" | custom-call | tf_op jit(solution)/shard_map/accumulate_0/pallas_call | solution.py:359
  17.9 0.0 collective-permute-done.5.refs_4_
  17.9 3.1 %accumulate_1.1.refs_5_ = f32[32,64,256]{2,1,0:T(8,128)S(1)} custom-call(s32[1]{0:T(128)S(6)} %copy.15.quant_ref, bf16[32,128]{1,0:T(8,128)(2,1)S(1)} %get-tuple-element.13.refs_0_, bf16[32,128]{1,0:T(8,128)(2,1)S(1)} %collective-permute-done.refs_1_, bf16[32,128]{1,0:T(8,128)(2,1)S(1)} %collective-permute-done.1.refs_2_, ...), custom_call_target="tpu_custom_call", output_to_operand_aliasing={{}: (6, {})} | custom-call | tf_op jit(solution)/shard_map/accumulate_1/pallas_call | solution.py:359
  21.0 0.0 collective-permute-done.4.refs_4_
  21.1 3.1 %accumulate_2.1.refs_5_ = f32[32,64,256]{2,1,0:T(8,128)S(1)} custom-call(s32[1]{0:T(128)S(6)} %copy.15.quant_ref, bf16[32,128]{1,0:T(8,128)(2,1)S(1)} %get-tuple-element.13.refs_0_, bf16[32,128]{1,0:T(8,128)(2,1)S(1)} %collective-permute-done.refs_1_, bf16[32,128]{1,0:T(8,128)(2,1)S(1)} %collective-permute-done.1.refs_2_, ...), custom_call_target="tpu_custom_call", output_to_operand_aliasing={{}: (6, {})} | custom-call | tf_op jit(solution)/shard_map/accumulate_2/pallas_call | solution.py:359
  24.2 0.0 collective-permute-done.3.refs_4_
  24.2 5.7 %accumulate_3.1 = (f32[32,64,256]{2,1,0:T(8,128)}, f32[16,8,128]{2,1,0:T(8,128)S(1)}) custom-call(s32[1]{0:T(128)S(6)} %copy.15.quant_ref, bf16[32,128]{1,0:T(8,128)(2,1)S(1)} %get-tuple-element.13.refs_0_, bf16[32,128]{1,0:T(8,128)(2,1)S(1)} %collective-permute-done.refs_1_, bf16[32,128]{1,0:T(8,128)(2,1)S(1)} %collective-permute-done.1.refs_2_, ...), custom_call_target="tpu_custom_call" | custom-call | tf_op jit(solution)/shard_map/accumulate_3/pallas_call | solution.py:359
  29.9 12.6 %all_to_all.5 = f32[16,8,128]{2,1,0:T(8,128)S(1)} all-to-all(f32[16,8,128]{2,1,0:T(8,128)S(1)} %get-tuple-element.23), channel_id=1, replica_groups=mesh['groups'=2,'rows'=4,'feat'=4] {'feat','rows'}, dimensions={0} | all-to-all | bytes 131072 | tf_op jit(solution)/shard_map/all_to_all | solution.py:371
  42.5 0.2 reshape.22
  42.6 0.7 %copy.12 = f32[4,4,4,8,32]{4,3,2,1,0:T(8,128)} copy(f32[4,4,4,8,32]{4,2,3,1,0:T(4,128)S(1)} %bitcast.8) | data formatting | bytes 131072 | tf_op jit(solution)/shard_map/transpose | solution.py:375
Async XLA Ops:
  2.9 10.1 %collective-permute-start.2 = (bf16[32,128]{1,0:T(8,128)(2,1)S(1)}, bf16[32,128]{1,0:T(8,128)(2,1)S(1)}, u32[]{:S(2)}, u32[]{:S(2)}) collective-permute-start(bf16[32,128]{1,0:T(8,128)(2,1)S(1)} %get-tuple-element.13.refs_0_), channel_id=1, source_target_pairs={{0,12},{4,8},{8,4},{12,0},{1,13},{5,9},{9,5},{13,1},{2,14},{6,10},... | collective-permute-start | bytes 24584 | tf_op jit(solution)/shard_map/ppermute | solution.py:306
  8.0 6.1 %collective-permute-start.1 = (bf16[32,128]{1,0:T(8,128)(2,1)S(1)}, bf16[32,128]{1,0:T(8,128)(2,1)S(1)}, u32[]{:S(2)}, u32[]{:S(2)}) collective-permute-start(bf16[32,128]{1,0:T(8,128)(2,1)S(1)} %get-tuple-element.13.refs_0_), channel_id=1, source_target_pairs={{0,8},{4,12},{8,0},{12,4},{1,9},{5,13},{9,1},{13,5},{2,10},{6,14},... | collective-permute-start | bytes 24584 | tf_op jit(solution)/shard_map/ppermute | solution.py:306
  8.0 6.1 %collective-permute-start = (bf16[32,128]{1,0:T(8,128)(2,1)S(1)}, bf16[32,128]{1,0:T(8,128)(2,1)S(1)}, u32[]{:S(2)}, u32[]{:S(2)}) collective-permute-start(bf16[32,128]{1,0:T(8,128)(2,1)S(1)} %get-tuple-element.13.refs_0_), channel_id=1, source_target_pairs={{0,4},{4,0},{8,12},{12,8},{1,5},{5,1},{9,13},{13,9},{2,6},{6,2},{1... | collective-permute-start | bytes 24584 | tf_op jit(solution)/shard_map/ppermute | solution.py:306
  8.7 12.4 %collective-permute-start.4 = (bf16[512,128]{1,0:T(8,128)(2,1)S(1)}, bf16[512,128]{1,0:T(8,128)(2,1)S(1)}, u32[]{:S(2)}, u32[]{:S(2)}) collective-permute-start(bf16[512,128]{1,0:T(8,128)(2,1)S(1)} %get-tuple-element.19), channel_id=1, source_target_pairs={{0,8},{4,12},{8,0},{12,4},{1,9},{5,13},{9,1},{13,5},{2,10},{6,14},... | collective-permute-start | bytes 393224 | tf_op jit(solution)/shard_map/ppermute | solution.py:306
  10.9 6.9 %collective-permute-start.5 = (bf16[512,128]{1,0:T(8,128)(2,1)S(1)}, bf16[512,128]{1,0:T(8,128)(2,1)S(1)}, u32[]{:S(2)}, u32[]{:S(2)}) collective-permute-start(bf16[512,128]{1,0:T(8,128)(2,1)S(1)} %get-tuple-element.20), channel_id=1, source_target_pairs={{0,4},{4,0},{8,12},{12,8},{1,5},{5,1},{9,13},{13,9},{2,6},{6,2},{1... | collective-permute-start | bytes 393224 | tf_op jit(solution)/shard_map/ppermute | solution.py:306
  14.1 10.1 %collective-permute-start.3 = (bf16[512,128]{1,0:T(8,128)(2,1)S(1)}, bf16[512,128]{1,0:T(8,128)(2,1)S(1)}, u32[]{:S(2)}, u32[]{:S(2)}) collective-permute-start(bf16[512,128]{1,0:T(8,128)(2,1)S(1)} %get-tuple-element.18), channel_id=1, source_target_pairs={{0,12},{4,8},{8,4},{12,0},{1,13},{5,9},{9,5},{13,1},{2,14},{6,10},... | collective-permute-start | bytes 393224 | tf_op jit(solution)/shard_map/ppermute | solution.py:306

commit v5 on v4

--- a/solution.py
+++ b/solution.py
@@ -23,6 +23,7 @@
 REGION_ROW = HORIZON
 NODE_ROW = HORIZON + 1
 TOTAL_ROW = HORIZON
+LEVEL_ROW = HORIZON + 1
 STORES = 16
 PIECES = 3
 SCALE = 256.0
@@ -143,31 +144,39 @@
             out_refs[step][block * height + pad : (block + 1) * height] = own[:, lanes]
 
 
-def shared_forecast(sums_refs):
+def leader(position, count):
+    return position | 1 if position | 1 < count else position
+
+
+def combine(rows, quant_ref, *refs):
+    sums_refs, shared_ref = refs[:rows], refs[rows]
+    level = F32(0.0)
+    for index, value in enumerate(LEVELS):
+        level = jnp.where(quant_ref[:, :1] == index, F32(value), level)
     sums = jnp.zeros((DAYS, STORES), F32)
     for ref in sums_refs:
         parts = ref[...].astype(F32)
         for piece in range(PIECES):
             sums = sums + parts[:, piece * STORES : (piece + 1) * STORES]
     shared = sums / (sums[TOTAL_ROW : TOTAL_ROW + 1] / HIST + 1.0)
-    return jnp.concatenate(split_parts(shared), axis=1)
-
-
-def quantile_level(quant_ref):
-    level = F32(0.0)
-    for index, value in enumerate(LEVELS):
-        level = jnp.where(quant_ref[0] == index, F32(value), level)
-    return level
-
-
-def series_columns(own, shared, level, cols_ref):
+    row = lax.broadcasted_iota(jnp.int32, (DAYS, STORES), 0)
+    shared = jnp.where(row == LEVEL_ROW, level, shared)
+    shared_ref[...] = jnp.concatenate(
+        split_parts(shared) + [jnp.zeros((DAYS, LANES - PIECES * STORES), BF16)], axis=1
+    )
+
+
+def series_columns(own, shared, cols_ref):
     series = own.shape[1]
     day = lax.broadcasted_iota(jnp.int32, (DAYS, series), 0)
     store = lax.broadcasted_iota(jnp.int32, (PIECES * STORES, series), 0) % STORES
     region = own[REGION_ROW : REGION_ROW + 1].astype(jnp.int32)
     node = own[NODE_ROW : NODE_ROW + 1].astype(jnp.int32)
     pick = jnp.where(store == region, 1.0, 0.0).astype(BF16)
+    shared = shared[:, : PIECES * STORES]
     regional = jnp.dot(shared, pick, preferred_element_type=F32)
+    level = shared[LEVEL_ROW : LEVEL_ROW + 1].astype(F32)
+    level = sum(level[:, piece * STORES : piece * STORES + 1] for piece in range(PIECES))
     wave = jnp.where(day < HORIZON, jnp.tanh(own + regional), 0.0)
     mean = jnp.sum(wave, axis=0, keepdims=True) / HORIZON
     square = jnp.sum(wave * wave, axis=0, keepdims=True) / HORIZON
@@ -182,35 +191,34 @@
             cols_ref[at : at + NODES] = jnp.where(here_node, piece, 0.0).astype(F8)
 
 
-def accumulate(rows, sources, feats, first, last, quant_ref, *refs):
-    sums_refs, block_refs, refs = refs[:rows], refs[rows : rows + sources], refs[rows + sources :]
+def accumulate(sources, feats, first, last, led, leader_ref, own_ref, *refs):
+    block_refs, refs = refs[:sources], refs[sources:]
     if not first:
         before_ref, refs = refs[0], refs[1:]
     if last:
         hist_ref, best_ref, bins_held, cols_held, hist_held, sem = refs
     else:
-        hist_held, bins_held, cols_held = refs
+        left_ref, bins_held, cols_held = refs
     series = bins_held.shape[2]
     pad = max(feats, 16)
     height = pad + DAYS
-    shared = shared_forecast(sums_refs)
-    level = quantile_level(quant_ref)
+    shared = jnp.where(led(lax.axis_index("feat")), leader_ref[...], own_ref[...])
     for source, ref in enumerate(block_refs):
         both = jnp.concatenate(
             [ref[block * height : (block + 1) * height] for block in range(series // LANES)],
             axis=1,
         ).astype(F32)
         bins_held[source] = (both[:feats] - 128.0).astype(jnp.int32)
-        series_columns(both[pad:], shared, level, cols_held.at[source])
+        series_columns(both[pad:], shared, cols_held.at[source])
 
     bin_at = lax.broadcasted_iota(jnp.int32, (32, series), 0)
 
     def products(source, feature):
         bins = jnp.broadcast_to(bins_held[source, pl.ds(feature, 1)], (32, series)).astype(jnp.int8)
-        onehot = jnp.concatenate(
+        upto = jnp.concatenate(
             [
                 jnp.where(
-                    bins == (bin_at + (32 * part - 128)).astype(jnp.int8),
+                    bins <= (bin_at + (32 * part - 128)).astype(jnp.int8),
                     jnp.ones((), F8),
                     jnp.zeros((), F8),
                 )
@@ -218,9 +226,7 @@
             ],
             axis=0,
         )
-        return lax.dot_general(
-            cols_held[source], onehot, ROW_BY_ROW, preferred_element_type=F32
-        )
+        return lax.dot_general(cols_held[source], upto, ROW_BY_ROW, preferred_element_type=F32)
 
     def one_feature(feature):
         product = products(0, feature)
@@ -228,63 +234,65 @@
             product = lax.fori_loop(
                 1, sources, lambda at, total: total + products(at, feature), product
             )
-        hist = (product[: 2 * NODES] + product[2 * NODES :]) * (1.0 / SCALE)
-        if not first:
-            hist = hist + before_ref[feature]
-        hist_held[feature] = hist
-        if last:
-            pltpu.make_async_copy(hist_held.at[feature], hist_ref.at[feature], sem).start()
-
-    group = min(feats, 8)
-
-    def one_group(at):
-        for member in range(group):
-            one_feature(at * group + member)
+        left = product[: 2 * NODES] + product[2 * NODES :]
+        return left if first else left + before_ref[feature]
+
+    group = min(feats, 32 if last else 16)
 
     if not last:
-        lax.fori_loop(0, feats // group, lambda at, carry: (one_group(at), carry)[1], 0)
+
+        def one_group(at, carry):
+            for member in range(group):
+                feature = at * group + member
+                left_ref[feature] = one_feature(feature)
+            return carry
+
+        lax.fori_loop(0, feats // group, one_group, 0)
         return
 
-    def beside(at, best):
-        one_group(at)
-        return group_gains(hist_held, at - 1, group, best)
-
-    one_group(0)
-    best = lax.fori_loop(1, feats // group, beside, jnp.zeros((NODES, LANES), F32))
-    best = group_gains(hist_held, feats // group - 1, group, best)
-    best = best.T
-    width = LANES // NODES
-    packed = jnp.concatenate(
-        [best[at * (feats // width) : (at + 1) * (feats // width)] for at in range(width)], axis=1
-    )
-    for target in range(best_ref.shape[0]):
-        best_ref[target] = packed
-    pltpu.make_async_copy(hist_held, hist_ref, sem).wait()
-
-
-def group_gains(hist_held, at, group, best):
-    below = lax.broadcasted_iota(jnp.int32, (BINS, BINS), 0) <= lax.broadcasted_iota(
-        jnp.int32, (BINS, BINS), 1
-    )
-    below = jnp.where(below, 1.0, 0.0).astype(BF16)
     feature_at = lax.broadcasted_iota(jnp.int32, (NODES, LANES), 1)
-    last_bin = lax.broadcasted_iota(jnp.int32, (NODES, BINS), 1) == BINS - 1
-    hist = hist_held[pl.ds(at * group, group)].reshape(group * 2 * NODES, BINS)
-    high = hist.astype(BF16)
-    low = (hist - high.astype(F32)).astype(BF16)
-    left = jnp.dot(high, below, preferred_element_type=F32) + jnp.dot(
-        low, below, preferred_element_type=F32
-    )
-    left = left.reshape(group, 2, NODES, BINS)
-    for member in range(group):
-        grad, hess = left[member, 0], left[member, 1]
+    bin_lane = lax.broadcasted_iota(jnp.int32, (2 * NODES, BINS), 1)
+    last_bin = bin_lane[:NODES] == BINS - 1
+
+    chunk = min(group, 8)
+
+    def histogram(feature):
+        left = one_feature(feature) * (1.0 / SCALE)
+        before = jnp.where(bin_lane == 0, 0.0, pltpu.roll(left, 1, axis=1))
+        hist_held[feature] = left - before
+        return left
+
+    def gains(feature, left, best):
+        grad, hess = left[:NODES], left[NODES:]
         all_grad, all_hess = grad[:, BINS - 1 :], hess[:, BINS - 1 :]
         over_grad, over_hess = all_grad - grad, all_hess - hess
         gain = grad * grad / (hess + 1.0) + over_grad * over_grad / (over_hess + 1.0)
         gain = jnp.max(jnp.where(last_bin, -jnp.inf, gain), axis=1, keepdims=True)
         gain = gain - all_grad * all_grad / (all_hess + 1.0)
-        best = jnp.where(feature_at == at * group + member, gain, best)
-    return best
+        return jnp.where(feature_at == feature, gain, best)
+
+    def final_group(at, best):
+        waiting = []
+        for member in range(group):
+            feature = at * group + member
+            waiting.append((feature, histogram(feature)))
+            if member % chunk == chunk - 1:
+                here = pl.ds(feature - chunk + 1, chunk)
+                pltpu.make_async_copy(hist_held.at[here], hist_ref.at[here], sem).start()
+                for feature, left in waiting:
+                    best = gains(feature, left, best)
+                waiting = []
+        return best
+
+    best = lax.fori_loop(0, feats // group, final_group, jnp.zeros((NODES, LANES), F32))
+    best = best.T
+    width = LANES // NODES
+    packed = jnp.concatenate(
+        [best[at * (feats // width) : (at + 1) * (feats // width)] for at in range(width)], axis=1
+    )
+    for target in range(best_ref.shape[0]):
+        best_ref[target] = packed
+    pltpu.make_async_copy(hist_held, hist_ref, sem).wait()
 
 
 def shards(daily_unit_counts, region_ids, node_ids, bin_ids, quant_index, filter_kernels):
@@ -295,7 +303,6 @@
     pad = max(feats, 16)
     height = pad + DAYS
     vmem = pl.BlockSpec(memory_space=pltpu.VMEM)
-    smem = pl.BlockSpec(memory_space=pltpu.SMEM)
     hbm = pl.BlockSpec(memory_space=pl.ANY)
     params = pltpu.CompilerParams(vmem_limit_bytes=VMEM_LIMIT)
     regions = region_ids.reshape(1, series)
@@ -328,13 +335,37 @@
             for array in (daily_unit_counts, regions, nodes, bin_ids, filter_kernels.T)
         )
     )
-    sums = [sums] + [exchange(sums, step) for step in range(1, rows)]
+    leads = sorted({leader(at, feat_count) for at in range(feat_count)})
+    sums = [sums]
+    for step in range(1, rows):
+        pairs = [
+            (at * feat_count + lead, partner(at, step, rows) * feat_count + lead)
+            for at in range(rows)
+            for lead in leads
+        ]
+        sums.append(lax.ppermute(sums[0], ("rows", "feat"), pairs))
     arrived = [outgoing[0]]
+    quant = lax.pad(quant_index, jnp.int32(0), [(0, LANES - 1, 0)]).reshape(1, LANES)
     for step in range(1, rows):
         block = outgoing[step]
         if step == rows - 1:
             block, sums[1:] = lax.optimization_barrier((block, sums[1:]))
         arrived.append(exchange(block, step))
+
+    shared = pl.pallas_call(
+        functools.partial(combine, rows),
+        out_shape=jax.ShapeDtypeStruct((DAYS, LANES), BF16),
+        in_specs=[vmem] * (1 + rows),
+        out_specs=vmem,
+        compiler_params=params,
+        name="combine",
+    )(quant, *sums)
+    followers = [at for at in range(feat_count) if leader(at, feat_count) != at]
+    pairs = [(leader(at, feat_count), at) for at in followers]
+    leaders_shared = lax.ppermute(shared, "feat", pairs)
+
+    def led(position):
+        return sum((position == at).astype(jnp.int32) for at in followers) > 0
 
     targets = rows * feat_count
     packed_rows = feats * NODES // LANES
@@ -349,7 +380,7 @@
             pltpu.VMEM((count, feats, series), jnp.int32),
             pltpu.VMEM((count, 4 * NODES, series), F8),
         ]
-        operands = [quant_index, *sums, *blocks] + ([] if first else [histogram])
+        operands = [leaders_shared, shared, *blocks] + ([] if first else [histogram])
         if last:
             held += [pltpu.VMEM(hist_shape.shape, F32), pltpu.SemaphoreType.DMA]
             out_shape = [hist_shape, jax.ShapeDtypeStruct((targets, packed_rows, LANES), F32)]
@@ -357,9 +388,9 @@
         else:
             out_shape, out_specs = hist_shape, vmem
         histogram = pl.pallas_call(
-            functools.partial(accumulate, rows, count, feats, first, last),
+            functools.partial(accumulate, count, feats, first, last, led),
             out_shape=out_shape,
-            in_specs=[smem] + [vmem] * (len(operands) - 1),
+            in_specs=[vmem] * len(operands),
             out_specs=out_specs,
             scratch_shapes=held,
             input_output_aliases={} if first or last else {len(operands) - 1: 0},

time: 43.6 us -> 45.3 us (1.039)
  waiting for transfers between devices: 1.15 us -> 8.75 us
  Pallas kernels: 17.3 us -> 14.2 us
  blocking collectives: 12.6 us -> 10.7 us
  starting transfers between devices: 10.1 us -> 9.02 us
    ppermute x0 -> x4, waiting for transfers between devices: none -> 8.74 us  [the longest x1 8.74 us: shards(): leaders_shared = lax.ppermute(shared, 'feat', pairs)]
    ppermute x6 -> x3, starting transfers between devices: 10.1 us -> 5.75 us  [exchange(): return lax.ppermute(array, 'rows', pairs)]
    ppermute x0 -> x4, starting transfers between devices: none -> 3.27 us  [the longest x3 1.98 us: shards(): sums.append(lax.ppermute(sums[0], ('rows', 'feat'), pairs))]
    pallas_call x4 -> x5, Pallas kernels: 15.1 us -> 12 us  [the longest x4 11.8 us: shards(): pl.pallas_call(functools.partial(accumulate, count, feats, first, last, l...]
    all_to_all x1, blocking collectives: 12.6 us -> 10.7 us  [shards(): gathered = lax.all_to_all(best, ('feat', 'rows'), 0, 0, tiled=True)]
    ppermute x6 -> x3, waiting for transfers between devices: 1.15 us -> 0.01 us  [exchange(): return lax.ppermute(array, 'rows', pairs)]
  transfers between devices with their start and end apart: 6 -> 7, of which waited for: 1 -> 1; matrix products, arithmetic and copies ran while one was open for 0% -> 0% of each run, Pallas kernels for 22% -> 18%
where the time goes in v5:
time: 45.3 us; the launch traced here: 45.1 us
  Pallas kernels  14.2 us (31%)
  blocking collectives  10.7 us (24%)
  starting transfers between devices  9.02 us (20%)
  waiting for transfers between devices  8.75 us (19%)
  between operations  1.4 us (3%)
  local copies, waits for them, and re-layouts  0.89 us (2%)
    pallas_call x4, Pallas kernels, shards(): pl.pallas_call(functools.partial(accumulate, count, feats, first, last, l...  11.8 us
    all_to_all x1, blocking collectives, shards(): gathered = lax.all_to_all(best, ('feat', 'rows'), 0, 0, tiled=True)  10.7 us
    ppermute x1, waiting for transfers between devices, shards(): leaders_shared = lax.ppermute(shared, 'feat', pairs)  8.74 us
    ppermute x3, starting transfers between devices, exchange(): return lax.ppermute(array, 'rows', pairs)  5.75 us
    pallas_call x1, Pallas kernels, shards(): pl.pallas_call(functools.partial(prepare, rows), out_shape=[jax.ShapeDtyp...  2.27 us
    ppermute x3, starting transfers between devices, shards(): sums.append(lax.ppermute(sums[0], ('rows', 'feat'), pairs))  1.98 us
    ppermute x1, starting transfers between devices, shards(): leaders_shared = lax.ppermute(shared, 'feat', pairs)  1.29 us
  transfers between devices with their start and end apart: 7, of which 1 were waited for; matrix products, arithmetic and copies ran while one was open for 0% of the time, Pallas kernels for 18%

profile of v5, /device:TPU:0, one launch (start us, length us, event | category | flops | bytes accessed | tf_op | source)
XLA Modules:
  0.0 45.1 jit_solution(17054218514038455820)
XLA Ops:
  0.6 2.3 %prepare.1 = (bf16[32,128]{1,0:T(8,128)(2,1)S(1)}, bf16[512,128]{1,0:T(8,128)(2,1)S(1)}, bf16[512,128]{1,0:T(8,128)(2,1)S(1)}, bf16[512,128]{1,0:T(8,128)(2,1)S(1)}, bf16[512,128]{1,0:T(8,128)(2,1)S(1)}) custom-call(bf16[1024,512]{1,0:T(8,128)(2,1)} %refs_0_.1, s32[1,1024]{1,0:T(1,128)} %bitcast.12, s32[1,1024]{1,0:T(1,128)} %bitcast.13, ...), custom_call_target="tpu_custom_call" | custom-call | tf_op jit(solution)/shard_map/prepare/pallas_call | solution.py:315
  2.9 0.7 %collective-permute-start.2 = (bf16[32,128]{1,0:T(8,128)(2,1)S(1)}, bf16[32,128]{1,0:T(8,128)(2,1)S(1)}, u32[]{:S(2)}, u32[]{:S(2)}) collective-permute-start(bf16[32,128]{1,0:T(8,128)(2,1)S(1)} %get-tuple-element.13.refs_0_), channel_id=1, source_target_pairs={{1,13},{3,15},{5,9},{7,11},{9,5},{11,7},{13,1},{15,3},{17,29},{19,... | collective-permute-start | bytes 24584 | tf_op jit(solution)/shard_map/ppermute | solution.py:346
  3.6 0.7 %collective-permute-start.1 = (bf16[32,128]{1,0:T(8,128)(2,1)S(1)}, bf16[32,128]{1,0:T(8,128)(2,1)S(1)}, u32[]{:S(2)}, u32[]{:S(2)}) collective-permute-start(bf16[32,128]{1,0:T(8,128)(2,1)S(1)} %get-tuple-element.13.refs_0_), channel_id=1, source_target_pairs={{1,9},{3,11},{5,13},{7,15},{9,1},{11,3},{13,5},{15,7},{17,25},{19,... | collective-permute-start | bytes 24584 | tf_op jit(solution)/shard_map/ppermute | solution.py:346
  4.2 0.7 %collective-permute-start = (bf16[32,128]{1,0:T(8,128)(2,1)S(1)}, bf16[32,128]{1,0:T(8,128)(2,1)S(1)}, u32[]{:S(2)}, u32[]{:S(2)}) collective-permute-start(bf16[32,128]{1,0:T(8,128)(2,1)S(1)} %get-tuple-element.13.refs_0_), channel_id=1, source_target_pairs={{1,5},{3,7},{5,1},{7,3},{9,13},{11,15},{13,9},{15,11},{17,21},{19,... | collective-permute-start | bytes 24584 | tf_op jit(solution)/shard_map/ppermute | solution.py:346
  4.9 4.1 %collective-permute-start.5 = (bf16[512,128]{1,0:T(8,128)(2,1)S(1)}, bf16[512,128]{1,0:T(8,128)(2,1)S(1)}, u32[]{:S(2)}, u32[]{:S(2)}) collective-permute-start(bf16[512,128]{1,0:T(8,128)(2,1)S(1)} %get-tuple-element.19), channel_id=1, source_target_pairs={{0,8},{4,12},{8,0},{12,4},{1,9},{5,13},{9,1},{13,5},{2,10},{6,14},... | collective-permute-start | bytes 393224 | tf_op jit(solution)/shard_map/ppermute | solution.py:313
  9.0 1.6 %collective-permute-start.6 = (bf16[512,128]{1,0:T(8,128)(2,1)S(1)}, bf16[512,128]{1,0:T(8,128)(2,1)S(1)}, u32[]{:S(2)}, u32[]{:S(2)}) collective-permute-start(bf16[512,128]{1,0:T(8,128)(2,1)S(1)} %get-tuple-element.20), channel_id=1, source_target_pairs={{0,4},{4,0},{8,12},{12,8},{1,5},{5,1},{9,13},{13,9},{2,6},{6,2},{1... | collective-permute-start | bytes 393224 | tf_op jit(solution)/shard_map/ppermute | solution.py:313
  10.6 0.0 collective-permute-done.2.refs_3_
  10.6 0.0 collective-permute-done.1.refs_2_
  10.6 0.0 collective-permute-done.refs_1_
  10.6 0.1 collective-permute-start.4
  11.3 0.2 combine.1.own_ref
  11.5 1.3 %collective-permute-start.3 = (bf16[32,128]{1,0:T(8,128)(2,1)S(1)}, bf16[32,128]{1,0:T(8,128)(2,1)S(1)}, u32[]{:S(2)}, u32[]{:S(2)}) collective-permute-start(bf16[32,128]{1,0:T(8,128)(2,1)S(1)} %combine.1.own_ref), channel_id=1, source_target_pairs={{1,0},{3,2},{5,4},{7,6},{9,8},{11,10},{13,12},{15,14},{17,16},{19,... | collective-permute-start | bytes 24584 | tf_op jit(solution)/shard_map/ppermute | solution.py:365
  12.8 8.7 %collective-permute-done.3.leader_ref = bf16[32,128]{1,0:T(8,128)(2,1)S(1)} collective-permute-done((bf16[32,128]{1,0:T(8,128)(2,1)S(1)}, bf16[32,128]{1,0:T(8,128)(2,1)S(1)}, u32[]{:S(2)}, u32[]{:S(2)}) %collective-permute-start.3) | collective-permute-done | bytes 8224 | tf_op jit(solution)/shard_map/ppermute | solution.py:365
  21.5 2.7 %accumulate_0.1.refs_1_ = f32[32,64,256]{2,1,0:T(8,128)S(1)} custom-call(bf16[32,128]{1,0:T(8,128)(2,1)S(1)} %collective-permute-done.3.leader_ref, bf16[32,128]{1,0:T(8,128)(2,1)S(1)} %combine.1.own_ref, bf16[512,128]{1,0:T(8,128)(2,1)S(1)} %get-tuple-element.21.refs_0_), custom_call_target="tpu_custom_call" | custom-call | tf_op jit(solution)/shard_map/accumulate_0/pallas_call | solution.py:390
  24.3 0.0 collective-permute-done.6.refs_0_
  24.3 2.7 %accumulate_1.1.refs_1_ = f32[32,64,256]{2,1,0:T(8,128)S(1)} custom-call(bf16[32,128]{1,0:T(8,128)(2,1)S(1)} %collective-permute-done.3.leader_ref, bf16[32,128]{1,0:T(8,128)(2,1)S(1)} %combine.1.own_ref, bf16[512,128]{1,0:T(8,128)(2,1)S(1)} %collective-permute-done.6.refs_0_, f32[32,64,256]{2,1,0:T(8,128)S(1)} %accumulate_0.1.refs_1_), custom_call_target="tpu_custom_call", output_to_operand_aliasing={{}: (3, {})} | custom-call | tf_op jit(solution)/shard_map/accumulate_1/pallas_call | solution.py:390
  27.0 0.0 collective-permute-done.5.refs_0_
  27.0 2.7 %accumulate_2.1.refs_1_ = f32[32,64,256]{2,1,0:T(8,128)S(1)} custom-call(bf16[32,128]{1,0:T(8,128)(2,1)S(1)} %collective-permute-done.3.leader_ref, bf16[32,128]{1,0:T(8,128)(2,1)S(1)} %combine.1.own_ref, bf16[512,128]{1,0:T(8,128)(2,1)S(1)} %collective-permute-done.5.refs_0_, f32[32,64,256]{2,1,0:T(8,128)S(1)} %accumulate_1.1.refs_1_), custom_call_target="tpu_custom_call", output_to_operand_aliasing={{}: (3, {})} | custom-call | tf_op jit(solution)/shard_map/accumulate_2/pallas_call | solution.py:390
  29.7 0.0 collective-permute-done.4.refs_0_
  29.7 3.7 %accumulate_3.1 = (f32[32,64,256]{2,1,0:T(8,128)}, f32[16,8,128]{2,1,0:T(8,128)S(1)}) custom-call(bf16[32,128]{1,0:T(8,128)(2,1)S(1)} %collective-permute-done.3.leader_ref, bf16[32,128]{1,0:T(8,128)(2,1)S(1)} %combine.1.own_ref, bf16[512,128]{1,0:T(8,128)(2,1)S(1)} %collective-permute-done.4.refs_0_, f32[32,64,256]{2,1,0:T(8,128)S(1)} %accumulate_2.1.refs_1_), custom_call_target="tpu_custom_call" | custom-call | tf_op jit(solution)/shard_map/accumulate_3/pallas_call | solution.py:390
  33.4 10.7 %all_to_all.5 = f32[16,8,128]{2,1,0:T(8,128)S(1)} all-to-all(f32[16,8,128]{2,1,0:T(8,128)S(1)} %get-tuple-element.23), channel_id=1, replica_groups=mesh['groups'=2,'rows'=4,'feat'=4] {'feat','rows'}, dimensions={0} | all-to-all | bytes 131072 | tf_op jit(solution)/shard_map/all_to_all | solution.py:402
  44.2 0.2 reshape.26
  44.3 0.7 %copy.12 = f32[4,4,4,8,32]{4,3,2,1,0:T(8,128)} copy(f32[4,4,4,8,32]{4,2,3,1,0:T(4,128)S(1)} %bitcast.10) | data formatting | bytes 131072 | tf_op jit(solution)/shard_map/transpose | solution.py:406
  (1 shorter events, 0.0 us)
Async XLA Ops:
  2.9 7.7 %collective-permute-start.2 = (bf16[32,128]{1,0:T(8,128)(2,1)S(1)}, bf16[32,128]{1,0:T(8,128)(2,1)S(1)}, u32[]{:S(2)}, u32[]{:S(2)}) collective-permute-start(bf16[32,128]{1,0:T(8,128)(2,1)S(1)} %get-tuple-element.13.refs_0_), channel_id=1, source_target_pairs={{1,13},{3,15},{5,9},{7,11},{9,5},{11,7},{13,1},{15,3},{17,29},{19,... | collective-permute-start | bytes 24584 | tf_op jit(solution)/shard_map/ppermute | solution.py:346
  3.6 7.0 %collective-permute-start.1 = (bf16[32,128]{1,0:T(8,128)(2,1)S(1)}, bf16[32,128]{1,0:T(8,128)(2,1)S(1)}, u32[]{:S(2)}, u32[]{:S(2)}) collective-permute-start(bf16[32,128]{1,0:T(8,128)(2,1)S(1)} %get-tuple-element.13.refs_0_), channel_id=1, source_target_pairs={{1,9},{3,11},{5,13},{7,15},{9,1},{11,3},{13,5},{15,7},{17,25},{19,... | collective-permute-start | bytes 24584 | tf_op jit(solution)/shard_map/ppermute | solution.py:346
  4.2 6.4 %collective-permute-start = (bf16[32,128]{1,0:T(8,128)(2,1)S(1)}, bf16[32,128]{1,0:T(8,128)(2,1)S(1)}, u32[]{:S(2)}, u32[]{:S(2)}) collective-permute-start(bf16[32,128]{1,0:T(8,128)(2,1)S(1)} %get-tuple-element.13.refs_0_), channel_id=1, source_target_pairs={{1,5},{3,7},{5,1},{7,3},{9,13},{11,15},{13,9},{15,11},{17,21},{19,... | collective-permute-start | bytes 24584 | tf_op jit(solution)/shard_map/ppermute | solution.py:346
  4.9 22.1 %collective-permute-start.5 = (bf16[512,128]{1,0:T(8,128)(2,1)S(1)}, bf16[512,128]{1,0:T(8,128)(2,1)S(1)}, u32[]{:S(2)}, u32[]{:S(2)}) collective-permute-start(bf16[512,128]{1,0:T(8,128)(2,1)S(1)} %get-tuple-element.19), channel_id=1, source_target_pairs={{0,8},{4,12},{8,0},{12,4},{1,9},{5,13},{9,1},{13,5},{2,10},{6,14},... | collective-permute-start | bytes 393224 | tf_op jit(solution)/shard_map/ppermute | solution.py:313
  9.0 15.2 %collective-permute-start.6 = (bf16[512,128]{1,0:T(8,128)(2,1)S(1)}, bf16[512,128]{1,0:T(8,128)(2,1)S(1)}, u32[]{:S(2)}, u32[]{:S(2)}) collective-permute-start(bf16[512,128]{1,0:T(8,128)(2,1)S(1)} %get-tuple-element.20), channel_id=1, source_target_pairs={{0,4},{4,0},{8,12},{12,8},{1,5},{5,1},{9,13},{13,9},{2,6},{6,2},{1... | collective-permute-start | bytes 393224 | tf_op jit(solution)/shard_map/ppermute | solution.py:313
  10.6 19.1 %collective-permute-start.4 = (bf16[512,128]{1,0:T(8,128)(2,1)S(1)}, bf16[512,128]{1,0:T(8,128)(2,1)S(1)}, u32[]{:S(2)}, u32[]{:S(2)}) collective-permute-start(bf16[512,128]{1,0:T(8,128)(2,1)S(1)} %get-tuple-element.18), channel_id=1, source_target_pairs={{0,12},{4,8},{8,4},{12,0},{1,13},{5,9},{9,5},{13,1},{2,14},{6,10},... | collective-permute-start | bytes 393224 | tf_op jit(solution)/shard_map/ppermute | solution.py:313
  11.5 10.0 %collective-permute-start.3 = (bf16[32,128]{1,0:T(8,128)(2,1)S(1)}, bf16[32,128]{1,0:T(8,128)(2,1)S(1)}, u32[]{:S(2)}, u32[]{:S(2)}) collective-permute-start(bf16[32,128]{1,0:T(8,128)(2,1)S(1)} %combine.1.own_ref), channel_id=1, source_target_pairs={{1,0},{3,2},{5,4},{7,6},{9,8},{11,10},{13,12},{15,14},{17,16},{19,... | collective-permute-start | bytes 24584 | tf_op jit(solution)/shard_map/ppermute | solution.py:365

commit v6 on v5

--- a/solution.py
+++ b/solution.py
@@ -23,7 +23,6 @@
 REGION_ROW = HORIZON
 NODE_ROW = HORIZON + 1
 TOTAL_ROW = HORIZON
-LEVEL_ROW = HORIZON + 1
 STORES = 16
 PIECES = 3
 SCALE = 256.0
@@ -70,7 +69,7 @@
 
 def prepare(rows, *refs):
     given, refs = refs[:5], refs[5:]
-    sums_ref, out_refs, refs = refs[0], refs[1 : 1 + rows], refs[1 + rows :]
+    sums_ref, own_ref, out_refs, refs = refs[0], refs[1], refs[2 : 2 + rows], refs[2 + rows :]
     taken, (held, sems) = refs[:5], refs[5:]
     counts_ref, region_ref, node_ref, bins_ref, taps_ref = taken
     copies = [
@@ -82,7 +81,6 @@
     series = counts_ref.shape[0]
     feats = bins_ref.shape[1] // rows
     pad = held.shape[1]
-    height = pad + DAYS
     me = lax.axis_index("rows")
 
     copies[4].wait()
@@ -100,7 +98,7 @@
         bins = held[partner(me, step, rows)]
         for block in range(series // LANES):
             lanes = slice(block * LANES, (block + 1) * LANES)
-            out_refs[step][block * height : block * height + pad] = bins[:, lanes]
+            out_refs[step][block * pad : (block + 1) * pad] = bins[:, lanes]
 
     for at in (0, 1, 2):
         copies[at].wait()
@@ -137,61 +135,67 @@
     day = lax.broadcasted_iota(jnp.int32, (DAYS, series), 0)
     own = jnp.where(day == REGION_ROW, region_ref[...].astype(F32), own)
     own = jnp.where(day == NODE_ROW, node_ref[...].astype(F32), own)
-    own = own.astype(BF16)
-    for step in range(rows):
-        for block in range(series // LANES):
-            lanes = slice(block * LANES, (block + 1) * LANES)
-            out_refs[step][block * height + pad : (block + 1) * height] = own[:, lanes]
-
-
-def leader(position, count):
-    return position | 1 if position | 1 < count else position
-
-
-def combine(rows, quant_ref, *refs):
-    sums_refs, shared_ref = refs[:rows], refs[rows]
+    own_ref[...] = own
+
+
+def columns(rows, quant_ref, *refs):
+    sums_refs, own_ref, refs = refs[:rows], refs[rows], refs[rows + 1 :]
+    bins_refs, out_refs = refs[:rows], refs[rows:]
+    series = own_ref.shape[1]
+    behind = bins_refs[0].shape[0]
     level = F32(0.0)
     for index, value in enumerate(LEVELS):
-        level = jnp.where(quant_ref[:, :1] == index, F32(value), level)
+        level = jnp.where(quant_ref[0] == index, F32(value), level)
     sums = jnp.zeros((DAYS, STORES), F32)
     for ref in sums_refs:
         parts = ref[...].astype(F32)
         for piece in range(PIECES):
             sums = sums + parts[:, piece * STORES : (piece + 1) * STORES]
     shared = sums / (sums[TOTAL_ROW : TOTAL_ROW + 1] / HIST + 1.0)
-    row = lax.broadcasted_iota(jnp.int32, (DAYS, STORES), 0)
-    shared = jnp.where(row == LEVEL_ROW, level, shared)
-    shared_ref[...] = jnp.concatenate(
-        split_parts(shared) + [jnp.zeros((DAYS, LANES - PIECES * STORES), BF16)], axis=1
-    )
-
-
-def series_columns(own, shared, cols_ref):
-    series = own.shape[1]
+    shared = jnp.concatenate(split_parts(shared), axis=1)
+
+    own = own_ref[...]
     day = lax.broadcasted_iota(jnp.int32, (DAYS, series), 0)
     store = lax.broadcasted_iota(jnp.int32, (PIECES * STORES, series), 0) % STORES
     region = own[REGION_ROW : REGION_ROW + 1].astype(jnp.int32)
-    node = own[NODE_ROW : NODE_ROW + 1].astype(jnp.int32)
     pick = jnp.where(store == region, 1.0, 0.0).astype(BF16)
-    shared = shared[:, : PIECES * STORES]
     regional = jnp.dot(shared, pick, preferred_element_type=F32)
-    level = shared[LEVEL_ROW : LEVEL_ROW + 1].astype(F32)
-    level = sum(level[:, piece * STORES : piece * STORES + 1] for piece in range(PIECES))
     wave = jnp.where(day < HORIZON, jnp.tanh(own + regional), 0.0)
     mean = jnp.sum(wave, axis=0, keepdims=True) / HORIZON
     square = jnp.sum(wave * wave, axis=0, keepdims=True) / HORIZON
     gradient = 0.5 + 0.5 * mean - level
     hessian = 0.5 * (1.0 - square)
-    here_node = lax.broadcasted_iota(jnp.int32, (NODES, series), 0) == node
+    rows_of = [
+        value[:, block * LANES : (block + 1) * LANES]
+        for value in (gradient, hessian, own[NODE_ROW : NODE_ROW + 1])
+        for block in range(series // LANES)
+    ]
+    spare = jnp.zeros((out_refs[0].shape[0] - behind - len(rows_of), LANES), F32)
+    tail = jnp.concatenate(rows_of + [spare], axis=0).astype(BF16)
+    for bins_ref, out_ref in zip(bins_refs, out_refs):
+        out_ref[:behind] = bins_ref[...]
+        out_ref[behind:] = tail
+
+
+def place(tail, cols_ref):
+    blocks = cols_ref.shape[1] // LANES
+    gradient, hessian, node = (
+        jnp.concatenate(
+            [tail[at * blocks + block : at * blocks + block + 1] for block in range(blocks)], axis=1
+        )
+        for at in range(3)
+    )
+    node_at = lax.broadcasted_iota(jnp.int32, (NODES, cols_ref.shape[1]), 0)
+    here_node = node_at == node.astype(jnp.int32)
     for part, value in enumerate((gradient, hessian)):
-        value = value.astype(BF16).astype(F32) * SCALE
+        value = value * SCALE
         high = value.astype(F8).astype(F32)
         for offset, piece in ((0, high), (2, value - high)):
             at = (part + offset) * NODES
             cols_ref[at : at + NODES] = jnp.where(here_node, piece, 0.0).astype(F8)
 
 
-def accumulate(sources, feats, first, last, led, leader_ref, own_ref, *refs):
+def accumulate(sources, feats, first, last, *refs):
     block_refs, refs = refs[:sources], refs[sources:]
     if not first:
         before_ref, refs = refs[0], refs[1:]
@@ -201,15 +205,13 @@
         left_ref, bins_held, cols_held = refs
     series = bins_held.shape[2]
     pad = max(feats, 16)
-    height = pad + DAYS
-    shared = jnp.where(led(lax.axis_index("feat")), leader_ref[...], own_ref[...])
+    behind = series // LANES * pad
     for source, ref in enumerate(block_refs):
-        both = jnp.concatenate(
-            [ref[block * height : (block + 1) * height] for block in range(series // LANES)],
-            axis=1,
-        ).astype(F32)
-        bins_held[source] = (both[:feats] - 128.0).astype(jnp.int32)
-        series_columns(both[pad:], shared, cols_held.at[source])
+        bins = jnp.concatenate(
+            [ref[block * pad : (block + 1) * pad] for block in range(series // LANES)], axis=1
+        )
+        bins_held[source] = (bins[:feats].astype(F32) - 128.0).astype(jnp.int32)
+        place(ref[behind:].astype(F32), cols_held.at[source])
 
     bin_at = lax.broadcasted_iota(jnp.int32, (32, series), 0)
 
@@ -301,8 +303,9 @@
     series = daily_unit_counts.shape[0]
     feats = bin_ids.shape[1] // rows
     pad = max(feats, 16)
-    height = pad + DAYS
+    blocks = series // LANES
     vmem = pl.BlockSpec(memory_space=pltpu.VMEM)
+    smem = pl.BlockSpec(memory_space=pltpu.SMEM)
     hbm = pl.BlockSpec(memory_space=pl.ANY)
     params = pltpu.CompilerParams(vmem_limit_bytes=VMEM_LIMIT)
     regions = region_ids.reshape(1, series)
@@ -312,12 +315,13 @@
         pairs = [(at, partner(at, step, rows)) for at in range(rows)]
         return lax.ppermute(array, "rows", pairs)
 
-    sums, *outgoing = pl.pallas_call(
+    sums, own, *bins = pl.pallas_call(
         functools.partial(prepare, rows),
         out_shape=[jax.ShapeDtypeStruct((DAYS, LANES), BF16)]
-        + [jax.ShapeDtypeStruct((series // LANES * height, LANES), BF16)] * rows,
+        + [jax.ShapeDtypeStruct((DAYS, series), F32)]
+        + [jax.ShapeDtypeStruct((blocks * pad, LANES), BF16)] * rows,
         in_specs=[hbm] * 5,
-        out_specs=[vmem] * (1 + rows),
+        out_specs=[vmem] * (2 + rows),
         scratch_shapes=[
             pltpu.VMEM(daily_unit_counts.shape, BF16),
             pltpu.VMEM((1, series), jnp.int32),
@@ -335,37 +339,16 @@
             for array in (daily_unit_counts, regions, nodes, bin_ids, filter_kernels.T)
         )
     )
-    leads = sorted({leader(at, feat_count) for at in range(feat_count)})
-    sums = [sums]
-    for step in range(1, rows):
-        pairs = [
-            (at * feat_count + lead, partner(at, step, rows) * feat_count + lead)
-            for at in range(rows)
-            for lead in leads
-        ]
-        sums.append(lax.ppermute(sums[0], ("rows", "feat"), pairs))
-    arrived = [outgoing[0]]
-    quant = lax.pad(quant_index, jnp.int32(0), [(0, LANES - 1, 0)]).reshape(1, LANES)
-    for step in range(1, rows):
-        block = outgoing[step]
-        if step == rows - 1:
-            block, sums[1:] = lax.optimization_barrier((block, sums[1:]))
-        arrived.append(exchange(block, step))
-
-    shared = pl.pallas_call(
-        functools.partial(combine, rows),
-        out_shape=jax.ShapeDtypeStruct((DAYS, LANES), BF16),
-        in_specs=[vmem] * (1 + rows),
-        out_specs=vmem,
+    sums = [sums] + [exchange(sums, step) for step in range(1, rows)]
+    outgoing = pl.pallas_call(
+        functools.partial(columns, rows),
+        out_shape=[jax.ShapeDtypeStruct((blocks * pad + 4 * blocks, LANES), BF16)] * rows,
+        in_specs=[smem] + [vmem] * (2 * rows + 1),
+        out_specs=[vmem] * rows,
         compiler_params=params,
-        name="combine",
-    )(quant, *sums)
-    followers = [at for at in range(feat_count) if leader(at, feat_count) != at]
-    pairs = [(leader(at, feat_count), at) for at in followers]
-    leaders_shared = lax.ppermute(shared, "feat", pairs)
-
-    def led(position):
-        return sum((position == at).astype(jnp.int32) for at in followers) > 0
+        name="columns",
+    )(quant_index, *sums, own, *bins)
+    arrived = [outgoing[0]] + [exchange(outgoing[step], step) for step in range(1, rows)]
 
     targets = rows * feat_count
     packed_rows = feats * NODES // LANES
@@ -373,14 +356,14 @@
     steps = [arrived[at : at + 1] for at in range(min(rows, 4) - 1)]
     steps.append(arrived[len(steps) :])
     histogram = None
-    for at, blocks in enumerate(steps):
+    for at, sources in enumerate(steps):
         first, last = at == 0, at == len(steps) - 1
-        count = len(blocks)
+        count = len(sources)
         held = [
             pltpu.VMEM((count, feats, series), jnp.int32),
             pltpu.VMEM((count, 4 * NODES, series), F8),
         ]
-        operands = [leaders_shared, shared, *blocks] + ([] if first else [histogram])
+        operands = sources + ([] if first else [histogram])
         if last:
             held += [pltpu.VMEM(hist_shape.shape, F32), pltpu.SemaphoreType.DMA]
             out_shape = [hist_shape, jax.ShapeDtypeStruct((targets, packed_rows, LANES), F32)]
@@ -388,7 +371,7 @@
         else:
             out_shape, out_specs = hist_shape, vmem
         histogram = pl.pallas_call(
-            functools.partial(accumulate, count, feats, first, last, led),
+            functools.partial(accumulate, count, feats, first, last),
             out_shape=out_shape,
             in_specs=[vmem] * len(operands),
             out_specs=out_specs,

time: 45.3 us -> 39.9 us (0.88)
  waiting for transfers between devices: 8.75 us -> 3.27 us
  starting transfers between devices: 9.02 us -> 10.2 us
  Pallas kernels: 14.2 us -> 13.7 us
    ppermute x4 -> x0, waiting for transfers between devices: 8.74 us -> none  [the longest x1 8.74 us: shards(): leaders_shared = lax.ppermute(shared, 'feat', pairs)]
    ppermute x3 -> x6, starting transfers between devices: 5.75 us -> 10.2 us  [exchange(): return lax.ppermute(array, 'rows', pairs)]
    ppermute x4 -> x0, starting transfers between devices: 3.27 us -> none  [the longest x3 1.98 us: shards(): sums.append(lax.ppermute(sums[0], ('rows', 'feat'), pairs))]
    ppermute x3 -> x6, waiting for transfers between devices: 0.01 us -> 3.27 us  [exchange(): return lax.ppermute(array, 'rows', pairs)]
    pallas_call x5, Pallas kernels: 12 us -> 11.4 us  [the longest x4 11.1 us: shards(): pl.pallas_call(functools.partial(accumulate, count, feats, first, last),...]
    all_to_all x1, blocking collectives: 10.7 us -> 10.3 us  [shards(): gathered = lax.all_to_all(best, ('feat', 'rows'), 0, 0, tiled=True)]
  transfers between devices with their start and end apart: 7 -> 6, of which waited for: 1 -> 2; matrix products, arithmetic and copies ran while one was open for 0% -> 0% of each run, Pallas kernels for 18% -> 19%
where the time goes in v6:
time: 39.9 us; the launch traced here: 39.7 us
  Pallas kernels  13.7 us (34%)
  blocking collectives  10.3 us (26%)
  starting transfers between devices  10.2 us (26%)
  waiting for transfers between devices  3.27 us (8%)
  between operations  1.37 us (3%)
  local copies, waits for them, and re-layouts  0.88 us (2%)
    pallas_call x4, Pallas kernels, shards(): pl.pallas_call(functools.partial(accumulate, count, feats, first, last),...  11.1 us
    all_to_all x1, blocking collectives, shards(): gathered = lax.all_to_all(best, ('feat', 'rows'), 0, 0, tiled=True)  10.3 us
    ppermute x6, starting transfers between devices, exchange(): return lax.ppermute(array, 'rows', pairs)  10.2 us
    ppermute x6, waiting for transfers between devices, exchange(): return lax.ppermute(array, 'rows', pairs)  3.27 us
    pallas_call x1, Pallas kernels, shards(): pl.pallas_call(functools.partial(prepare, rows), out_shape=[jax.ShapeDtyp...  2.26 us
  transfers between devices with their start and end apart: 6, of which 2 were waited for; matrix products, arithmetic and copies ran while one was open for 0% of the time, Pallas kernels for 19%

profile of v6, /device:TPU:0, one launch (start us, length us, event | category | flops | bytes accessed | tf_op | source)
XLA Modules:
  0.0 39.7 jit_solution(8505966979736028073)
XLA Ops:
  0.6 2.3 %prepare.1 = (bf16[32,128]{1,0:T(8,128)(2,1)S(1)}, f32[32,1024]{1,0:T(8,128)S(1)}, bf16[256,128]{1,0:T(8,128)(2,1)S(1)}, bf16[256,128]{1,0:T(8,128)(2,1)S(1)}, b...) custom-call(bf16[1024,512]{1,0:T(8,128)(2,1)} %refs_0_.1, s32[1,1024]{1,0:T(1,128)} %bitcast.10, ...), custom_call_target="tpu_custom_call" | custom-call | tf_op jit(solution)/shard_map/prepare/pallas_call | solution.py:318
  2.9 5.1 %collective-permute-start.2 = (bf16[32,128]{1,0:T(8,128)(2,1)S(1)}, bf16[32,128]{1,0:T(8,128)(2,1)S(1)}, u32[]{:S(2)}, u32[]{:S(2)}) collective-permute-start(bf16[32,128]{1,0:T(8,128)(2,1)S(1)} %get-tuple-element.14.refs_0_), channel_id=1, source_target_pairs={{0,12},{4,8},{8,4},{12,0},{1,13},{5,9},{9,5},{13,1},{2,14},{6,10},... | collective-permute-start | bytes 24584 | tf_op jit(solution)/shard_map/ppermute | solution.py:316
  8.0 0.0 collective-permute-start.1
  8.0 0.6 %collective-permute-start = (bf16[32,128]{1,0:T(8,128)(2,1)S(1)}, bf16[32,128]{1,0:T(8,128)(2,1)S(1)}, u32[]{:S(2)}, u32[]{:S(2)}) collective-permute-start(bf16[32,128]{1,0:T(8,128)(2,1)S(1)} %get-tuple-element.14.refs_0_), channel_id=1, source_target_pairs={{0,4},{4,0},{8,12},{12,8},{1,5},{5,1},{9,13},{13,9},{2,6},{6,2},{1... | collective-permute-start | bytes 24584 | tf_op jit(solution)/shard_map/ppermute | solution.py:316
  9.3 0.3 collective-permute-done.2.refs_3_
  9.6 2.9 %collective-permute-done.1.refs_2_ = bf16[32,128]{1,0:T(8,128)(2,1)S(1)} collective-permute-done((bf16[32,128]{1,0:T(8,128)(2,1)S(1)}, bf16[32,128]{1,0:T(8,128)(2,1)S(1)}, u32[]{:S(2)}, u32[]{:S(2)}) %collective-permute-start.1) | collective-permute-done | bytes 8224 | tf_op jit(solution)/shard_map/ppermute | solution.py:316
  12.6 0.0 collective-permute-done.refs_1_
  12.6 0.3 columns.1
  12.9 0.1 collective-permute-start.5
  13.0 2.1 %collective-permute-start.4 = (bf16[288,128]{1,0:T(8,128)(2,1)S(1)}, bf16[288,128]{1,0:T(8,128)(2,1)S(1)}, u32[]{:S(2)}, u32[]{:S(2)}) collective-permute-start(bf16[288,128]{1,0:T(8,128)(2,1)S(1)} %get-tuple-element.21), channel_id=1, source_target_pairs={{0,8},{4,12},{8,0},{12,4},{1,9},{5,13},{9,1},{13,5},{2,10},{6,14},... | collective-permute-start | bytes 221192 | tf_op jit(solution)/shard_map/ppermute | solution.py:316
  15.1 2.3 %collective-permute-start.3 = (bf16[288,128]{1,0:T(8,128)(2,1)S(1)}, bf16[288,128]{1,0:T(8,128)(2,1)S(1)}, u32[]{:S(2)}, u32[]{:S(2)}) collective-permute-start(bf16[288,128]{1,0:T(8,128)(2,1)S(1)} %get-tuple-element.20), channel_id=1, source_target_pairs={{0,12},{4,8},{8,4},{12,0},{1,13},{5,9},{9,5},{13,1},{2,14},{6,10},... | collective-permute-start | bytes 221192 | tf_op jit(solution)/shard_map/ppermute | solution.py:316
  17.4 2.5 %accumulate_0.1.refs_1_ = f32[32,64,256]{2,1,0:T(8,128)S(1)} custom-call(bf16[288,128]{1,0:T(8,128)(2,1)S(1)} %get-tuple-element.23.refs_0_), custom_call_target="tpu_custom_call" | custom-call | tf_op jit(solution)/shard_map/accumulate_0/pallas_call | solution.py:373
  19.9 0.0 collective-permute-done.5.refs_0_
  19.9 2.5 %accumulate_1.1.refs_1_ = f32[32,64,256]{2,1,0:T(8,128)S(1)} custom-call(bf16[288,128]{1,0:T(8,128)(2,1)S(1)} %collective-permute-done.5.refs_0_, f32[32,64,256]{2,1,0:T(8,128)S(1)} %accumulate_0.1.refs_1_), custom_call_target="tpu_custom_call", output_to_operand_aliasing={{}: (1, {})} | custom-call | tf_op jit(solution)/shard_map/accumulate_1/pallas_call | solution.py:373
  22.5 0.0 collective-permute-done.4.refs_0_
  22.5 2.5 %accumulate_2.1.refs_1_ = f32[32,64,256]{2,1,0:T(8,128)S(1)} custom-call(bf16[288,128]{1,0:T(8,128)(2,1)S(1)} %collective-permute-done.4.refs_0_, f32[32,64,256]{2,1,0:T(8,128)S(1)} %accumulate_1.1.refs_1_), custom_call_target="tpu_custom_call", output_to_operand_aliasing={{}: (1, {})} | custom-call | tf_op jit(solution)/shard_map/accumulate_2/pallas_call | solution.py:373
  25.0 0.0 collective-permute-done.3.refs_0_
  25.0 3.5 %accumulate_3.1 = (f32[32,64,256]{2,1,0:T(8,128)}, f32[16,8,128]{2,1,0:T(8,128)S(1)}) custom-call(bf16[288,128]{1,0:T(8,128)(2,1)S(1)} %collective-permute-done.3.refs_0_, f32[32,64,256]{2,1,0:T(8,128)S(1)} %accumulate_2.1.refs_1_), custom_call_target="tpu_custom_call" | custom-call | tf_op jit(solution)/shard_map/accumulate_3/pallas_call | solution.py:373
  28.5 10.3 %all_to_all.5 = f32[16,8,128]{2,1,0:T(8,128)S(1)} all-to-all(f32[16,8,128]{2,1,0:T(8,128)S(1)} %get-tuple-element.25), channel_id=1, replica_groups=mesh['groups'=2,'rows'=4,'feat'=4] {'feat','rows'}, dimensions={0} | all-to-all | bytes 131072 | tf_op jit(solution)/shard_map/all_to_all | solution.py:385
  38.8 0.2 reshape.22
  39.0 0.7 %copy.12 = f32[4,4,4,8,32]{4,3,2,1,0:T(8,128)} copy(f32[4,4,4,8,32]{4,2,3,1,0:T(4,128)S(1)} %bitcast.8) | data formatting | bytes 131072 | tf_op jit(solution)/shard_map/transpose | solution.py:389
Async XLA Ops:
  2.9 6.7 %collective-permute-start.2 = (bf16[32,128]{1,0:T(8,128)(2,1)S(1)}, bf16[32,128]{1,0:T(8,128)(2,1)S(1)}, u32[]{:S(2)}, u32[]{:S(2)}) collective-permute-start(bf16[32,128]{1,0:T(8,128)(2,1)S(1)} %get-tuple-element.14.refs_0_), channel_id=1, source_target_pairs={{0,12},{4,8},{8,4},{12,0},{1,13},{5,9},{9,5},{13,1},{2,14},{6,10},... | collective-permute-start | bytes 24584 | tf_op jit(solution)/shard_map/ppermute | solution.py:316
  8.0 4.5 %collective-permute-start.1 = (bf16[32,128]{1,0:T(8,128)(2,1)S(1)}, bf16[32,128]{1,0:T(8,128)(2,1)S(1)}, u32[]{:S(2)}, u32[]{:S(2)}) collective-permute-start(bf16[32,128]{1,0:T(8,128)(2,1)S(1)} %get-tuple-element.14.refs_0_), channel_id=1, source_target_pairs={{0,8},{4,12},{8,0},{12,4},{1,9},{5,13},{9,1},{13,5},{2,10},{6,14},... | collective-permute-start | bytes 24584 | tf_op jit(solution)/shard_map/ppermute | solution.py:316
  8.0 4.5 %collective-permute-start = (bf16[32,128]{1,0:T(8,128)(2,1)S(1)}, bf16[32,128]{1,0:T(8,128)(2,1)S(1)}, u32[]{:S(2)}, u32[]{:S(2)}) collective-permute-start(bf16[32,128]{1,0:T(8,128)(2,1)S(1)} %get-tuple-element.14.refs_0_), channel_id=1, source_target_pairs={{0,4},{4,0},{8,12},{12,8},{1,5},{5,1},{9,13},{13,9},{2,6},{6,2},{1... | collective-permute-start | bytes 24584 | tf_op jit(solution)/shard_map/ppermute | solution.py:316
  12.9 7.0 %collective-permute-start.5 = (bf16[288,128]{1,0:T(8,128)(2,1)S(1)}, bf16[288,128]{1,0:T(8,128)(2,1)S(1)}, u32[]{:S(2)}, u32[]{:S(2)}) collective-permute-start(bf16[288,128]{1,0:T(8,128)(2,1)S(1)} %get-tuple-element.22), channel_id=1, source_target_pairs={{0,4},{4,0},{8,12},{12,8},{1,5},{5,1},{9,13},{13,9},{2,6},{6,2},{1... | collective-permute-start | bytes 221192 | tf_op jit(solution)/shard_map/ppermute | solution.py:316
  13.0 9.5 %collective-permute-start.4 = (bf16[288,128]{1,0:T(8,128)(2,1)S(1)}, bf16[288,128]{1,0:T(8,128)(2,1)S(1)}, u32[]{:S(2)}, u32[]{:S(2)}) collective-permute-start(bf16[288,128]{1,0:T(8,128)(2,1)S(1)} %get-tuple-element.21), channel_id=1, source_target_pairs={{0,8},{4,12},{8,0},{12,4},{1,9},{5,13},{9,1},{13,5},{2,10},{6,14},... | collective-permute-start | bytes 221192 | tf_op jit(solution)/shard_map/ppermute | solution.py:316
  15.1 9.9 %collective-permute-start.3 = (bf16[288,128]{1,0:T(8,128)(2,1)S(1)}, bf16[288,128]{1,0:T(8,128)(2,1)S(1)}, u32[]{:S(2)}, u32[]{:S(2)}) collective-permute-start(bf16[288,128]{1,0:T(8,128)(2,1)S(1)} %get-tuple-element.20), channel_id=1, source_target_pairs={{0,12},{4,8},{8,4},{12,0},{1,13},{5,9},{9,5},{13,1},{2,14},{6,10},... | collective-permute-start | bytes 221192 | tf_op jit(solution)/shard_map/ppermute | solution.py:316

commit v7 on v6

--- a/solution.py
+++ b/solution.py
@@ -8,6 +8,7 @@
 from jax.sharding import PartitionSpec as P
 
 BINS = 256
+HALF = BINS // 2
 NODES = 32
 HIST = 512
 HORIZON = 28
@@ -203,66 +204,97 @@
         hist_ref, best_ref, bins_held, cols_held, hist_held, sem = refs
     else:
         left_ref, bins_held, cols_held = refs
-    series = bins_held.shape[2]
+    series = bins_held.shape[3]
     pad = max(feats, 16)
     behind = series // LANES * pad
     for source, ref in enumerate(block_refs):
         bins = jnp.concatenate(
             [ref[block * pad : (block + 1) * pad] for block in range(series // LANES)], axis=1
         )
-        bins_held[source] = (bins[:feats].astype(F32) - 128.0).astype(jnp.int32)
+        bins = bins[:feats].astype(jnp.int32)
+        bins_held[source, 0] = jnp.bitwise_and(bins, HALF - 1)
+        bins_held[source, 1] = jnp.where(bins >= HALF, 1, 0)
         place(ref[behind:].astype(F32), cols_held.at[source])
 
     bin_at = lax.broadcasted_iota(jnp.int32, (32, series), 0)
 
-    def products(source, feature):
-        bins = jnp.broadcast_to(bins_held[source, pl.ds(feature, 1)], (32, series)).astype(jnp.int8)
-        upto = jnp.concatenate(
-            [
+    def spread(source, part, feature):
+        row = bins_held[source, part, pl.ds(feature, 1)]
+        return jnp.broadcast_to(row, (32, series)).astype(jnp.int8)
+
+    def products(source, pair):
+        every = cols_held[source]
+        uptos, sets = [], [every]
+        for feature in pair:
+            within = spread(source, 0, feature)
+            uptos += [
                 jnp.where(
-                    bins <= (bin_at + (32 * part - 128)).astype(jnp.int8),
-                    jnp.ones((), F8),
-                    jnp.zeros((), F8),
+                    within <= (bin_at + at).astype(jnp.int8), jnp.ones((), F8), jnp.zeros((), F8)
                 )
-                for part in range(BINS // 32)
-            ],
-            axis=0,
+                for at in range(0, HALF, 32)
+            ]
+            upper = spread(source, 1, feature) == jnp.int8(1)
+            sets += [
+                jnp.where(upper, every[at : at + 32], jnp.zeros((), F8))
+                for at in range(0, every.shape[0], 32)
+            ]
+        product = lax.dot_general(
+            jnp.concatenate(sets, axis=0),
+            jnp.concatenate(uptos, axis=0),
+            ROW_BY_ROW,
+            preferred_element_type=F32,
         )
-        return lax.dot_general(cols_held[source], upto, ROW_BY_ROW, preferred_element_type=F32)
-
-    def one_feature(feature):
-        product = products(0, feature)
+        count = every.shape[0]
+        found = []
+        for at in range(len(pair)):
+            mine = product[:, at * HALF : (at + 1) * HALF]
+            both, upper = mine[:count], mine[(at + 1) * count : (at + 2) * count]
+            both = both[: count // 2] + both[count // 2 :]
+            upper = upper[: count // 2] + upper[count // 2 :]
+            found.append(jnp.concatenate([both - upper, upper], axis=1))
+        return found
+
+    def two_features(feature):
+        pair = (feature, feature + 1)
+        found = products(0, pair)
         if sources > 1:
-            product = lax.fori_loop(
-                1, sources, lambda at, total: total + products(at, feature), product
+            found = lax.fori_loop(
+                1,
+                sources,
+                lambda at, total: [a + b for a, b in zip(total, products(at, pair))],
+                found,
             )
-        left = product[: 2 * NODES] + product[2 * NODES :]
-        return left if first else left + before_ref[feature]
+        if not first:
+            found = [value + before_ref[at] for at, value in zip(pair, found)]
+        return found
 
     group = min(feats, 32 if last else 16)
 
     if not last:
 
         def one_group(at, carry):
-            for member in range(group):
+            for member in range(0, group, 2):
                 feature = at * group + member
-                left_ref[feature] = one_feature(feature)
+                left_ref[feature], left_ref[feature + 1] = two_features(feature)
             return carry
 
         lax.fori_loop(0, feats // group, one_group, 0)
         return
 
     feature_at = lax.broadcasted_iota(jnp.int32, (NODES, LANES), 1)
-    bin_lane = lax.broadcasted_iota(jnp.int32, (2 * NODES, BINS), 1)
-    last_bin = bin_lane[:NODES] == BINS - 1
+    last_bin = lax.broadcasted_iota(jnp.int32, (NODES, BINS), 1) == BINS - 1
 
     chunk = min(group, 8)
 
-    def histogram(feature):
-        left = one_feature(feature) * (1.0 / SCALE)
-        before = jnp.where(bin_lane == 0, 0.0, pltpu.roll(left, 1, axis=1))
-        hist_held[feature] = left - before
-        return left
+    def histogram(feature, halves):
+        halves = halves * (1.0 / SCALE)
+        parts = [halves[:, :HALF], halves[:, HALF:]]
+        first_bin = lax.broadcasted_iota(jnp.int32, parts[0].shape, 1) == 0
+        hist_held[feature] = jnp.concatenate(
+            [part - jnp.where(first_bin, 0.0, pltpu.roll(part, 1, axis=1)) for part in parts],
+            axis=1,
+        )
+        return jnp.concatenate([parts[0], parts[1] + parts[0][:, HALF - 1 :]], axis=1)
 
     def gains(feature, left, best):
         grad, hess = left[:NODES], left[NODES:]
@@ -275,11 +307,12 @@
 
     def final_group(at, best):
         waiting = []
-        for member in range(group):
+        for member in range(0, group, 2):
             feature = at * group + member
-            waiting.append((feature, histogram(feature)))
-            if member % chunk == chunk - 1:
-                here = pl.ds(feature - chunk + 1, chunk)
+            for offset, halves in enumerate(two_features(feature)):
+                waiting.append((feature + offset, histogram(feature + offset, halves)))
+            if (member + 2) % chunk == 0:
+                here = pl.ds(feature + 2 - chunk, chunk)
                 pltpu.make_async_copy(hist_held.at[here], hist_ref.at[here], sem).start()
                 for feature, left in waiting:
                     best = gains(feature, left, best)
@@ -360,7 +393,7 @@
         first, last = at == 0, at == len(steps) - 1
         count = len(sources)
         held = [
-            pltpu.VMEM((count, feats, series), jnp.int32),
+            pltpu.VMEM((count, 2, feats, series), jnp.int32),
             pltpu.VMEM((count, 4 * NODES, series), F8),
         ]
         operands = sources + ([] if first else [histogram])

time: 39.9 us -> 39.2 us (0.982)
  Pallas kernels: 13.7 us -> 13 us
    pallas_call x4, Pallas kernels: 11.1 us -> 10.3 us  [shards(): pl.pallas_call(functools.partial(accumulate, count, feats, first, last),...]
  transfers between devices with their start and end apart: 6 -> 6, of which waited for: 2 -> 2; matrix products, arithmetic and copies ran while one was open for 0% -> 0% of each run, Pallas kernels for 19% -> 16%
where the time goes in v7:
time: 39.2 us; the launch traced here: 39 us
  Pallas kernels  13 us (33%)
  blocking collectives  10.3 us (26%)
  starting transfers between devices  10.2 us (26%)
  waiting for transfers between devices  3.27 us (8%)
  between operations  1.37 us (3%)
  local copies, waits for them, and re-layouts  0.88 us (2%)
    pallas_call x4, Pallas kernels, shards(): pl.pallas_call(functools.partial(accumulate, count, feats, first, last),...  10.3 us
    all_to_all x1, blocking collectives, shards(): gathered = lax.all_to_all(best, ('feat', 'rows'), 0, 0, tiled=True)  10.3 us
    ppermute x6, starting transfers between devices, exchange(): return lax.ppermute(array, 'rows', pairs)  10.2 us
    ppermute x6, waiting for transfers between devices, exchange(): return lax.ppermute(array, 'rows', pairs)  3.27 us
    pallas_call x1, Pallas kernels, shards(): pl.pallas_call(functools.partial(prepare, rows), out_shape=[jax.ShapeDtyp...  2.26 us
  transfers between devices with their start and end apart: 6, of which 2 were waited for; matrix products, arithmetic and copies ran while one was open for 0% of the time, Pallas kernels for 16%

profile of v7, /device:TPU:0, one launch (start us, length us, event | category | flops | bytes accessed | tf_op | source)
XLA Modules:
  0.0 39.0 jit_solution(15516784236920358368)
XLA Ops:
  0.6 2.3 %prepare.1 = (bf16[32,128]{1,0:T(8,128)(2,1)S(1)}, f32[32,1024]{1,0:T(8,128)S(1)}, bf16[256,128]{1,0:T(8,128)(2,1)S(1)}, bf16[256,128]{1,0:T(8,128)(2,1)S(1)}, b...) custom-call(bf16[1024,512]{1,0:T(8,128)(2,1)} %refs_0_.1, s32[1,1024]{1,0:T(1,128)} %bitcast.10, ...), custom_call_target="tpu_custom_call" | custom-call | tf_op jit(solution)/shard_map/prepare/pallas_call | solution.py:351
  2.9 5.1 %collective-permute-start.2 = (bf16[32,128]{1,0:T(8,128)(2,1)S(1)}, bf16[32,128]{1,0:T(8,128)(2,1)S(1)}, u32[]{:S(2)}, u32[]{:S(2)}) collective-permute-start(bf16[32,128]{1,0:T(8,128)(2,1)S(1)} %get-tuple-element.14.refs_0_), channel_id=1, source_target_pairs={{0,12},{4,8},{8,4},{12,0},{1,13},{5,9},{9,5},{13,1},{2,14},{6,10},... | collective-permute-start | bytes 24584 | tf_op jit(solution)/shard_map/ppermute | solution.py:349
  8.0 0.0 collective-permute-start.1
  8.0 0.6 %collective-permute-start = (bf16[32,128]{1,0:T(8,128)(2,1)S(1)}, bf16[32,128]{1,0:T(8,128)(2,1)S(1)}, u32[]{:S(2)}, u32[]{:S(2)}) collective-permute-start(bf16[32,128]{1,0:T(8,128)(2,1)S(1)} %get-tuple-element.14.refs_0_), channel_id=1, source_target_pairs={{0,4},{4,0},{8,12},{12,8},{1,5},{5,1},{9,13},{13,9},{2,6},{6,2},{1... | collective-permute-start | bytes 24584 | tf_op jit(solution)/shard_map/ppermute | solution.py:349
  9.3 0.3 collective-permute-done.2.refs_3_
  9.6 2.9 %collective-permute-done.1.refs_2_ = bf16[32,128]{1,0:T(8,128)(2,1)S(1)} collective-permute-done((bf16[32,128]{1,0:T(8,128)(2,1)S(1)}, bf16[32,128]{1,0:T(8,128)(2,1)S(1)}, u32[]{:S(2)}, u32[]{:S(2)}) %collective-permute-start.1) | collective-permute-done | bytes 8224 | tf_op jit(solution)/shard_map/ppermute | solution.py:349
  12.6 0.0 collective-permute-done.refs_1_
  12.6 0.3 columns.1
  12.9 0.1 collective-permute-start.5
  13.0 2.1 %collective-permute-start.4 = (bf16[288,128]{1,0:T(8,128)(2,1)S(1)}, bf16[288,128]{1,0:T(8,128)(2,1)S(1)}, u32[]{:S(2)}, u32[]{:S(2)}) collective-permute-start(bf16[288,128]{1,0:T(8,128)(2,1)S(1)} %get-tuple-element.21), channel_id=1, source_target_pairs={{0,8},{4,12},{8,0},{12,4},{1,9},{5,13},{9,1},{13,5},{2,10},{6,14},... | collective-permute-start | bytes 221192 | tf_op jit(solution)/shard_map/ppermute | solution.py:349
  15.1 2.3 %collective-permute-start.3 = (bf16[288,128]{1,0:T(8,128)(2,1)S(1)}, bf16[288,128]{1,0:T(8,128)(2,1)S(1)}, u32[]{:S(2)}, u32[]{:S(2)}) collective-permute-start(bf16[288,128]{1,0:T(8,128)(2,1)S(1)} %get-tuple-element.20), channel_id=1, source_target_pairs={{0,12},{4,8},{8,4},{12,0},{1,13},{5,9},{9,5},{13,1},{2,14},{6,10},... | collective-permute-start | bytes 221192 | tf_op jit(solution)/shard_map/ppermute | solution.py:349
  17.4 2.0 %accumulate_0.1.refs_1_ = f32[32,64,256]{2,1,0:T(8,128)S(1)} custom-call(bf16[288,128]{1,0:T(8,128)(2,1)S(1)} %get-tuple-element.23.refs_0_), custom_call_target="tpu_custom_call" | custom-call | tf_op jit(solution)/shard_map/accumulate_0/pallas_call | solution.py:406
  19.4 0.0 collective-permute-done.5.refs_0_
  19.4 2.1 %accumulate_1.1.refs_1_ = f32[32,64,256]{2,1,0:T(8,128)S(1)} custom-call(bf16[288,128]{1,0:T(8,128)(2,1)S(1)} %collective-permute-done.5.refs_0_, f32[32,64,256]{2,1,0:T(8,128)S(1)} %accumulate_0.1.refs_1_), custom_call_target="tpu_custom_call", output_to_operand_aliasing={{}: (1, {})} | custom-call | tf_op jit(solution)/shard_map/accumulate_1/pallas_call | solution.py:406
  21.5 0.0 collective-permute-done.4.refs_0_
  21.5 2.1 %accumulate_2.1.refs_1_ = f32[32,64,256]{2,1,0:T(8,128)S(1)} custom-call(bf16[288,128]{1,0:T(8,128)(2,1)S(1)} %collective-permute-done.4.refs_0_, f32[32,64,256]{2,1,0:T(8,128)S(1)} %accumulate_1.1.refs_1_), custom_call_target="tpu_custom_call", output_to_operand_aliasing={{}: (1, {})} | custom-call | tf_op jit(solution)/shard_map/accumulate_2/pallas_call | solution.py:406
  23.7 0.0 collective-permute-done.3.refs_0_
  23.7 4.1 %accumulate_3.1 = (f32[32,64,256]{2,1,0:T(8,128)}, f32[16,8,128]{2,1,0:T(8,128)S(1)}) custom-call(bf16[288,128]{1,0:T(8,128)(2,1)S(1)} %collective-permute-done.3.refs_0_, f32[32,64,256]{2,1,0:T(8,128)S(1)} %accumulate_2.1.refs_1_), custom_call_target="tpu_custom_call" | custom-call | tf_op jit(solution)/shard_map/accumulate_3/pallas_call | solution.py:406
  27.8 10.3 %all_to_all.5 = f32[16,8,128]{2,1,0:T(8,128)S(1)} all-to-all(f32[16,8,128]{2,1,0:T(8,128)S(1)} %get-tuple-element.25), channel_id=1, replica_groups=mesh['groups'=2,'rows'=4,'feat'=4] {'feat','rows'}, dimensions={0} | all-to-all | bytes 131072 | tf_op jit(solution)/shard_map/all_to_all | solution.py:418
  38.1 0.2 reshape.22
  38.2 0.7 %copy.12 = f32[4,4,4,8,32]{4,3,2,1,0:T(8,128)} copy(f32[4,4,4,8,32]{4,2,3,1,0:T(4,128)S(1)} %bitcast.8) | data formatting | bytes 131072 | tf_op jit(solution)/shard_map/transpose | solution.py:422
Async XLA Ops:
  2.9 6.7 %collective-permute-start.2 = (bf16[32,128]{1,0:T(8,128)(2,1)S(1)}, bf16[32,128]{1,0:T(8,128)(2,1)S(1)}, u32[]{:S(2)}, u32[]{:S(2)}) collective-permute-start(bf16[32,128]{1,0:T(8,128)(2,1)S(1)} %get-tuple-element.14.refs_0_), channel_id=1, source_target_pairs={{0,12},{4,8},{8,4},{12,0},{1,13},{5,9},{9,5},{13,1},{2,14},{6,10},... | collective-permute-start | bytes 24584 | tf_op jit(solution)/shard_map/ppermute | solution.py:349
  8.0 4.5 %collective-permute-start.1 = (bf16[32,128]{1,0:T(8,128)(2,1)S(1)}, bf16[32,128]{1,0:T(8,128)(2,1)S(1)}, u32[]{:S(2)}, u32[]{:S(2)}) collective-permute-start(bf16[32,128]{1,0:T(8,128)(2,1)S(1)} %get-tuple-element.14.refs_0_), channel_id=1, source_target_pairs={{0,8},{4,12},{8,0},{12,4},{1,9},{5,13},{9,1},{13,5},{2,10},{6,14},... | collective-permute-start | bytes 24584 | tf_op jit(solution)/shard_map/ppermute | solution.py:349
  8.0 4.5 %collective-permute-start = (bf16[32,128]{1,0:T(8,128)(2,1)S(1)}, bf16[32,128]{1,0:T(8,128)(2,1)S(1)}, u32[]{:S(2)}, u32[]{:S(2)}) collective-permute-start(bf16[32,128]{1,0:T(8,128)(2,1)S(1)} %get-tuple-element.14.refs_0_), channel_id=1, source_target_pairs={{0,4},{4,0},{8,12},{12,8},{1,5},{5,1},{9,13},{13,9},{2,6},{6,2},{1... | collective-permute-start | bytes 24584 | tf_op jit(solution)/shard_map/ppermute | solution.py:349
  12.9 6.5 %collective-permute-start.5 = (bf16[288,128]{1,0:T(8,128)(2,1)S(1)}, bf16[288,128]{1,0:T(8,128)(2,1)S(1)}, u32[]{:S(2)}, u32[]{:S(2)}) collective-permute-start(bf16[288,128]{1,0:T(8,128)(2,1)S(1)} %get-tuple-element.22), channel_id=1, source_target_pairs={{0,4},{4,0},{8,12},{12,8},{1,5},{5,1},{9,13},{13,9},{2,6},{6,2},{1... | collective-permute-start | bytes 221192 | tf_op jit(solution)/shard_map/ppermute | solution.py:349
  13.0 8.5 %collective-permute-start.4 = (bf16[288,128]{1,0:T(8,128)(2,1)S(1)}, bf16[288,128]{1,0:T(8,128)(2,1)S(1)}, u32[]{:S(2)}, u32[]{:S(2)}) collective-permute-start(bf16[288,128]{1,0:T(8,128)(2,1)S(1)} %get-tuple-element.21), channel_id=1, source_target_pairs={{0,8},{4,12},{8,0},{12,4},{1,9},{5,13},{9,1},{13,5},{2,10},{6,14},... | collective-permute-start | bytes 221192 | tf_op jit(solution)/shard_map/ppermute | solution.py:349
  15.1 8.6 %collective-permute-start.3 = (bf16[288,128]{1,0:T(8,128)(2,1)S(1)}, bf16[288,128]{1,0:T(8,128)(2,1)S(1)}, u32[]{:S(2)}, u32[]{:S(2)}) collective-permute-start(bf16[288,128]{1,0:T(8,128)(2,1)S(1)} %get-tuple-element.20), channel_id=1, source_target_pairs={{0,12},{4,8},{8,4},{12,0},{1,13},{5,9},{9,5},{13,1},{2,14},{6,10},... | collective-permute-start | bytes 221192 | tf_op jit(solution)/shard_map/ppermute | solution.py:349

commit v8 on v7

--- a/solution.py
+++ b/solution.py
@@ -268,7 +268,7 @@
             found = [value + before_ref[at] for at, value in zip(pair, found)]
         return found
 
-    group = min(feats, 32 if last else 16)
+    group = min(feats, 16)
 
     if not last:
 
@@ -284,7 +284,7 @@
     feature_at = lax.broadcasted_iota(jnp.int32, (NODES, LANES), 1)
     last_bin = lax.broadcasted_iota(jnp.int32, (NODES, BINS), 1) == BINS - 1
 
-    chunk = min(group, 8)
+    chunk = min(group, 4)
 
     def histogram(feature, halves):
         halves = halves * (1.0 / SCALE)

time: 39.2 us -> 38.8 us (0.990)
  Pallas kernels: 13 us -> 12.5 us
    pallas_call x4, Pallas kernels: 10.3 us -> 9.94 us  [shards(): pl.pallas_call(functools.partial(accumulate, count, feats, first, last),...]
where the time goes in v8:
time: 38.8 us; the launch traced here: 38.6 us
  Pallas kernels  12.5 us (32%)
  blocking collectives  10.3 us (27%)
  starting transfers between devices  10.2 us (26%)
  waiting for transfers between devices  3.27 us (8%)
  between operations  1.37 us (4%)
  local copies, waits for them, and re-layouts  0.88 us (2%)
    all_to_all x1, blocking collectives, shards(): gathered = lax.all_to_all(best, ('feat', 'rows'), 0, 0, tiled=True)  10.3 us
    ppermute x6, starting transfers between devices, exchange(): return lax.ppermute(array, 'rows', pairs)  10.2 us
    pallas_call x4, Pallas kernels, shards(): pl.pallas_call(functools.partial(accumulate, count, feats, first, last),...  9.94 us
    ppermute x6, waiting for transfers between devices, exchange(): return lax.ppermute(array, 'rows', pairs)  3.27 us
    pallas_call x1, Pallas kernels, shards(): pl.pallas_call(functools.partial(prepare, rows), out_shape=[jax.ShapeDtyp...  2.26 us
  transfers between devices with their start and end apart: 6, of which 2 were waited for; matrix products, arithmetic and copies ran while one was open for 0% of the time, Pallas kernels for 16%

profile of v8, /device:TPU:0, one launch (start us, length us, event | category | flops | bytes accessed | tf_op | source)
XLA Modules:
  0.0 38.6 jit_solution(12349697645735969165)
XLA Ops:
  0.6 2.3 %prepare.1 = (bf16[32,128]{1,0:T(8,128)(2,1)S(1)}, f32[32,1024]{1,0:T(8,128)S(1)}, bf16[256,128]{1,0:T(8,128)(2,1)S(1)}, bf16[256,128]{1,0:T(8,128)(2,1)S(1)}, b...) custom-call(bf16[1024,512]{1,0:T(8,128)(2,1)} %refs_0_.1, s32[1,1024]{1,0:T(1,128)} %bitcast.10, ...), custom_call_target="tpu_custom_call" | custom-call | tf_op jit(solution)/shard_map/prepare/pallas_call | solution.py:351
  2.9 5.1 %collective-permute-start.2 = (bf16[32,128]{1,0:T(8,128)(2,1)S(1)}, bf16[32,128]{1,0:T(8,128)(2,1)S(1)}, u32[]{:S(2)}, u32[]{:S(2)}) collective-permute-start(bf16[32,128]{1,0:T(8,128)(2,1)S(1)} %get-tuple-element.14.refs_0_), channel_id=1, source_target_pairs={{0,12},{4,8},{8,4},{12,0},{1,13},{5,9},{9,5},{13,1},{2,14},{6,10},... | collective-permute-start | bytes 24584 | tf_op jit(solution)/shard_map/ppermute | solution.py:349
  8.0 0.0 collective-permute-start.1
  8.0 0.6 %collective-permute-start = (bf16[32,128]{1,0:T(8,128)(2,1)S(1)}, bf16[32,128]{1,0:T(8,128)(2,1)S(1)}, u32[]{:S(2)}, u32[]{:S(2)}) collective-permute-start(bf16[32,128]{1,0:T(8,128)(2,1)S(1)} %get-tuple-element.14.refs_0_), channel_id=1, source_target_pairs={{0,4},{4,0},{8,12},{12,8},{1,5},{5,1},{9,13},{13,9},{2,6},{6,2},{1... | collective-permute-start | bytes 24584 | tf_op jit(solution)/shard_map/ppermute | solution.py:349
  9.3 0.3 collective-permute-done.2.refs_3_
  9.6 2.9 %collective-permute-done.1.refs_2_ = bf16[32,128]{1,0:T(8,128)(2,1)S(1)} collective-permute-done((bf16[32,128]{1,0:T(8,128)(2,1)S(1)}, bf16[32,128]{1,0:T(8,128)(2,1)S(1)}, u32[]{:S(2)}, u32[]{:S(2)}) %collective-permute-start.1) | collective-permute-done | bytes 8224 | tf_op jit(solution)/shard_map/ppermute | solution.py:349
  12.6 0.0 collective-permute-done.refs_1_
  12.6 0.3 columns.1
  12.9 0.1 collective-permute-start.5
  13.0 2.1 %collective-permute-start.4 = (bf16[288,128]{1,0:T(8,128)(2,1)S(1)}, bf16[288,128]{1,0:T(8,128)(2,1)S(1)}, u32[]{:S(2)}, u32[]{:S(2)}) collective-permute-start(bf16[288,128]{1,0:T(8,128)(2,1)S(1)} %get-tuple-element.21), channel_id=1, source_target_pairs={{0,8},{4,12},{8,0},{12,4},{1,9},{5,13},{9,1},{13,5},{2,10},{6,14},... | collective-permute-start | bytes 221192 | tf_op jit(solution)/shard_map/ppermute | solution.py:349
  15.1 2.3 %collective-permute-start.3 = (bf16[288,128]{1,0:T(8,128)(2,1)S(1)}, bf16[288,128]{1,0:T(8,128)(2,1)S(1)}, u32[]{:S(2)}, u32[]{:S(2)}) collective-permute-start(bf16[288,128]{1,0:T(8,128)(2,1)S(1)} %get-tuple-element.20), channel_id=1, source_target_pairs={{0,12},{4,8},{8,4},{12,0},{1,13},{5,9},{9,5},{13,1},{2,14},{6,10},... | collective-permute-start | bytes 221192 | tf_op jit(solution)/shard_map/ppermute | solution.py:349
  17.4 2.0 %accumulate_0.1.refs_1_ = f32[32,64,256]{2,1,0:T(8,128)S(1)} custom-call(bf16[288,128]{1,0:T(8,128)(2,1)S(1)} %get-tuple-element.23.refs_0_), custom_call_target="tpu_custom_call" | custom-call | tf_op jit(solution)/shard_map/accumulate_0/pallas_call | solution.py:406
  19.4 0.0 collective-permute-done.5.refs_0_
  19.4 2.1 %accumulate_1.1.refs_1_ = f32[32,64,256]{2,1,0:T(8,128)S(1)} custom-call(bf16[288,128]{1,0:T(8,128)(2,1)S(1)} %collective-permute-done.5.refs_0_, f32[32,64,256]{2,1,0:T(8,128)S(1)} %accumulate_0.1.refs_1_), custom_call_target="tpu_custom_call", output_to_operand_aliasing={{}: (1, {})} | custom-call | tf_op jit(solution)/shard_map/accumulate_1/pallas_call | solution.py:406
  21.5 0.0 collective-permute-done.4.refs_0_
  21.5 2.1 %accumulate_2.1.refs_1_ = f32[32,64,256]{2,1,0:T(8,128)S(1)} custom-call(bf16[288,128]{1,0:T(8,128)(2,1)S(1)} %collective-permute-done.4.refs_0_, f32[32,64,256]{2,1,0:T(8,128)S(1)} %accumulate_1.1.refs_1_), custom_call_target="tpu_custom_call", output_to_operand_aliasing={{}: (1, {})} | custom-call | tf_op jit(solution)/shard_map/accumulate_2/pallas_call | solution.py:406
  23.7 0.0 collective-permute-done.3.refs_0_
  23.7 3.7 %accumulate_3.1 = (f32[32,64,256]{2,1,0:T(8,128)}, f32[16,8,128]{2,1,0:T(8,128)S(1)}) custom-call(bf16[288,128]{1,0:T(8,128)(2,1)S(1)} %collective-permute-done.3.refs_0_, f32[32,64,256]{2,1,0:T(8,128)S(1)} %accumulate_2.1.refs_1_), custom_call_target="tpu_custom_call" | custom-call | tf_op jit(solution)/shard_map/accumulate_3/pallas_call | solution.py:406
  27.4 10.3 %all_to_all.5 = f32[16,8,128]{2,1,0:T(8,128)S(1)} all-to-all(f32[16,8,128]{2,1,0:T(8,128)S(1)} %get-tuple-element.25), channel_id=1, replica_groups=mesh['groups'=2,'rows'=4,'feat'=4] {'feat','rows'}, dimensions={0} | all-to-all | bytes 131072 | tf_op jit(solution)/shard_map/all_to_all | solution.py:418
  37.7 0.2 reshape.22
  37.8 0.7 %copy.12 = f32[4,4,4,8,32]{4,3,2,1,0:T(8,128)} copy(f32[4,4,4,8,32]{4,2,3,1,0:T(4,128)S(1)} %bitcast.8) | data formatting | bytes 131072 | tf_op jit(solution)/shard_map/transpose | solution.py:422
Async XLA Ops:
  2.9 6.7 %collective-permute-start.2 = (bf16[32,128]{1,0:T(8,128)(2,1)S(1)}, bf16[32,128]{1,0:T(8,128)(2,1)S(1)}, u32[]{:S(2)}, u32[]{:S(2)}) collective-permute-start(bf16[32,128]{1,0:T(8,128)(2,1)S(1)} %get-tuple-element.14.refs_0_), channel_id=1, source_target_pairs={{0,12},{4,8},{8,4},{12,0},{1,13},{5,9},{9,5},{13,1},{2,14},{6,10},... | collective-permute-start | bytes 24584 | tf_op jit(solution)/shard_map/ppermute | solution.py:349
  8.0 4.5 %collective-permute-start.1 = (bf16[32,128]{1,0:T(8,128)(2,1)S(1)}, bf16[32,128]{1,0:T(8,128)(2,1)S(1)}, u32[]{:S(2)}, u32[]{:S(2)}) collective-permute-start(bf16[32,128]{1,0:T(8,128)(2,1)S(1)} %get-tuple-element.14.refs_0_), channel_id=1, source_target_pairs={{0,8},{4,12},{8,0},{12,4},{1,9},{5,13},{9,1},{13,5},{2,10},{6,14},... | collective-permute-start | bytes 24584 | tf_op jit(solution)/shard_map/ppermute | solution.py:349
  8.0 4.5 %collective-permute-start = (bf16[32,128]{1,0:T(8,128)(2,1)S(1)}, bf16[32,128]{1,0:T(8,128)(2,1)S(1)}, u32[]{:S(2)}, u32[]{:S(2)}) collective-permute-start(bf16[32,128]{1,0:T(8,128)(2,1)S(1)} %get-tuple-element.14.refs_0_), channel_id=1, source_target_pairs={{0,4},{4,0},{8,12},{12,8},{1,5},{5,1},{9,13},{13,9},{2,6},{6,2},{1... | collective-permute-start | bytes 24584 | tf_op jit(solution)/shard_map/ppermute | solution.py:349
  12.9 6.5 %collective-permute-start.5 = (bf16[288,128]{1,0:T(8,128)(2,1)S(1)}, bf16[288,128]{1,0:T(8,128)(2,1)S(1)}, u32[]{:S(2)}, u32[]{:S(2)}) collective-permute-start(bf16[288,128]{1,0:T(8,128)(2,1)S(1)} %get-tuple-element.22), channel_id=1, source_target_pairs={{0,4},{4,0},{8,12},{12,8},{1,5},{5,1},{9,13},{13,9},{2,6},{6,2},{1... | collective-permute-start | bytes 221192 | tf_op jit(solution)/shard_map/ppermute | solution.py:349
  13.0 8.5 %collective-permute-start.4 = (bf16[288,128]{1,0:T(8,128)(2,1)S(1)}, bf16[288,128]{1,0:T(8,128)(2,1)S(1)}, u32[]{:S(2)}, u32[]{:S(2)}) collective-permute-start(bf16[288,128]{1,0:T(8,128)(2,1)S(1)} %get-tuple-element.21), channel_id=1, source_target_pairs={{0,8},{4,12},{8,0},{12,4},{1,9},{5,13},{9,1},{13,5},{2,10},{6,14},... | collective-permute-start | bytes 221192 | tf_op jit(solution)/shard_map/ppermute | solution.py:349
  15.1 8.6 %collective-permute-start.3 = (bf16[288,128]{1,0:T(8,128)(2,1)S(1)}, bf16[288,128]{1,0:T(8,128)(2,1)S(1)}, u32[]{:S(2)}, u32[]{:S(2)}) collective-permute-start(bf16[288,128]{1,0:T(8,128)(2,1)S(1)} %get-tuple-element.20), channel_id=1, source_target_pairs={{0,12},{4,8},{8,4},{12,0},{1,13},{5,9},{9,5},{13,1},{2,14},{6,10},... | collective-permute-start | bytes 221192 | tf_op jit(solution)/shard_map/ppermute | solution.py:349

commit v9 on v7

--- a/solution.py
+++ b/solution.py
@@ -200,10 +200,10 @@
     block_refs, refs = refs[:sources], refs[sources:]
     if not first:
         before_ref, refs = refs[0], refs[1:]
+    left_ref, refs = refs[0], refs[1:]
     if last:
-        hist_ref, best_ref, bins_held, cols_held, hist_held, sem = refs
-    else:
-        left_ref, bins_held, cols_held = refs
+        best_ref, refs = refs[0], refs[1:]
+    bins_held, cols_held = refs
     series = bins_held.shape[3]
     pad = max(feats, 16)
     behind = series // LANES * pad
@@ -284,17 +284,10 @@
     feature_at = lax.broadcasted_iota(jnp.int32, (NODES, LANES), 1)
     last_bin = lax.broadcasted_iota(jnp.int32, (NODES, BINS), 1) == BINS - 1
 
-    chunk = min(group, 8)
-
-    def histogram(feature, halves):
-        halves = halves * (1.0 / SCALE)
-        parts = [halves[:, :HALF], halves[:, HALF:]]
-        first_bin = lax.broadcasted_iota(jnp.int32, parts[0].shape, 1) == 0
-        hist_held[feature] = jnp.concatenate(
-            [part - jnp.where(first_bin, 0.0, pltpu.roll(part, 1, axis=1)) for part in parts],
-            axis=1,
-        )
-        return jnp.concatenate([parts[0], parts[1] + parts[0][:, HALF - 1 :]], axis=1)
+
+    def over_all(halves):
+        lower, upper = halves[:, :HALF], halves[:, HALF:]
+        return jnp.concatenate([lower, upper + lower[:, HALF - 1 :]], axis=1) * (1.0 / SCALE)
 
     def gains(feature, left, best):
         grad, hess = left[:NODES], left[NODES:]
@@ -306,17 +299,11 @@
         return jnp.where(feature_at == feature, gain, best)
 
     def final_group(at, best):
-        waiting = []
         for member in range(0, group, 2):
             feature = at * group + member
             for offset, halves in enumerate(two_features(feature)):
-                waiting.append((feature + offset, histogram(feature + offset, halves)))
-            if (member + 2) % chunk == 0:
-                here = pl.ds(feature + 2 - chunk, chunk)
-                pltpu.make_async_copy(hist_held.at[here], hist_ref.at[here], sem).start()
-                for feature, left in waiting:
-                    best = gains(feature, left, best)
-                waiting = []
+                left_ref[feature + offset] = halves
+                best = gains(feature + offset, over_all(halves), best)
         return best
 
     best = lax.fori_loop(0, feats // group, final_group, jnp.zeros((NODES, LANES), F32))
@@ -327,7 +314,37 @@
     )
     for target in range(best_ref.shape[0]):
         best_ref[target] = packed
-    pltpu.make_async_copy(hist_held, hist_ref, sem).wait()
+
+
+def results(left_ref, packed_ref, hist_ref, best_ref, hist_held, best_held, sems):
+    feats = left_ref.shape[0]
+    targets, packed_rows, _ = packed_ref.shape
+    for target in range(targets):
+        packed = packed_ref[target]
+        for at in range(LANES // NODES):
+            best_held[target, at * packed_rows : (at + 1) * packed_rows] = packed[
+                :, at * NODES : (at + 1) * NODES
+            ]
+    best_copy = pltpu.make_async_copy(best_held, best_ref, sems.at[1])
+    best_copy.start()
+    first_bin = lax.broadcasted_iota(jnp.int32, (2 * NODES, HALF), 1) == 0
+    group = min(feats, 4)
+
+    def one_group(at, carry):
+        for member in range(group):
+            feature = at * group + member
+            for half in range(2):
+                lanes = slice(half * HALF, (half + 1) * HALF)
+                left = left_ref[feature, :, lanes] * (1.0 / SCALE)
+                before = jnp.where(first_bin, 0.0, pltpu.roll(left, 1, axis=1))
+                hist_held[feature, :, lanes] = left - before
+        here = pl.ds(at * group, group)
+        pltpu.make_async_copy(hist_held.at[here], hist_ref.at[here], sems.at[0]).start()
+        return carry
+
+    lax.fori_loop(0, feats // group, one_group, 0)
+    pltpu.make_async_copy(hist_held, hist_ref, sems.at[0]).wait()
+    best_copy.wait()
 
 
 def shards(daily_unit_counts, region_ids, node_ids, bin_ids, quant_index, filter_kernels):
@@ -398,9 +415,8 @@
         ]
         operands = sources + ([] if first else [histogram])
         if last:
-            held += [pltpu.VMEM(hist_shape.shape, F32), pltpu.SemaphoreType.DMA]
             out_shape = [hist_shape, jax.ShapeDtypeStruct((targets, packed_rows, LANES), F32)]
-            out_specs = [hbm, vmem]
+            out_specs = [vmem, vmem]
         else:
             out_shape, out_specs = hist_shape, vmem
         histogram = pl.pallas_call(
@@ -409,20 +425,31 @@
             in_specs=[vmem] * len(operands),
             out_specs=out_specs,
             scratch_shapes=held,
-            input_output_aliases={} if first or last else {len(operands) - 1: 0},
+            input_output_aliases={} if first else {len(operands) - 1: 0},
             compiler_params=params,
             name=f"accumulate_{at}",
         )(*operands)
-    histogram, best = histogram
+    left, best = histogram
 
     gathered = lax.all_to_all(best, ("feat", "rows"), 0, 0, tiled=True)
-    width = LANES // NODES
-    feature_best = (
-        gathered.reshape(feat_count, rows, packed_rows, width, NODES)
-        .transpose(0, 1, 3, 2, 4)
-        .reshape(feat_count, rows, feats, NODES)
-    )
-    return histogram.reshape(1, 1, feats, 2, NODES, BINS), feature_best
+    best_shape = jax.ShapeDtypeStruct((targets, feats, NODES), F32)
+    histogram, feature_best = pl.pallas_call(
+        results,
+        out_shape=[hist_shape, best_shape],
+        in_specs=[vmem] * 2,
+        out_specs=[hbm] * 2,
+        scratch_shapes=[
+            pltpu.VMEM(hist_shape.shape, F32),
+            pltpu.VMEM(best_shape.shape, F32),
+            pltpu.SemaphoreType.DMA((2,)),
+        ],
+        compiler_params=params,
+        name="results",
+    )(left, gathered)
+    return (
+        histogram.reshape(1, 1, feats, 2, NODES, BINS),
+        feature_best.reshape(feat_count, rows, feats, NODES),
+    )
 
 
 def solution(mesh):

time: 39.2 us -> 38.9 us (level)
  local copies, waits for them, and re-layouts: 0.88 us -> 0 us
  Pallas kernels: 13 us -> 13.5 us
    pallas_call x0 -> x1, Pallas kernels: none -> 1.94 us  [shards(): pl.pallas_call(results, out_shape=[hist_shape, best_shape], in_specs=[vme...]
    pallas_call x4, Pallas kernels: 10.3 us -> 8.98 us  [shards(): pl.pallas_call(functools.partial(accumulate, count, feats, first, last),...]
    transpose x1 -> x0, local copies, waits for them, and re-layouts: 0.72 us -> none  [shards(): feature_best = gathered.reshape(feat_count, rows, packed_rows, width, NOD...]
where the time goes in v9:
time: 38.9 us; the launch traced here: 38.7 us
  Pallas kernels  13.5 us (35%)
  blocking collectives  10.3 us (26%)
  starting transfers between devices  10.2 us (26%)
  waiting for transfers between devices  3.27 us (8%)
  between operations  1.36 us (3%)
    all_to_all x1, blocking collectives, shards(): gathered = lax.all_to_all(best, ('feat', 'rows'), 0, 0, tiled=True)  10.3 us
    ppermute x6, starting transfers between devices, exchange(): return lax.ppermute(array, 'rows', pairs)  10.2 us
    pallas_call x4, Pallas kernels, shards(): pl.pallas_call(functools.partial(accumulate, count, feats, first, last),...  8.98 us
    ppermute x6, waiting for transfers between devices, exchange(): return lax.ppermute(array, 'rows', pairs)  3.27 us
    pallas_call x1, Pallas kernels, shards(): pl.pallas_call(functools.partial(prepare, rows), out_shape=[jax.ShapeDtyp...  2.26 us
    pallas_call x1, Pallas kernels, shards(): pl.pallas_call(results, out_shape=[hist_shape, best_shape], in_specs=[vme...  1.94 us
  transfers between devices with their start and end apart: 6, of which 2 were waited for; matrix products, arithmetic and copies ran while one was open for 0% of the time, Pallas kernels for 16%

profile of v9, /device:TPU:0, one launch (start us, length us, event | category | flops | bytes accessed | tf_op | source)
XLA Modules:
  0.0 38.7 jit_solution(15844536434184100552)
XLA Ops:
  0.6 2.3 %prepare.1 = (bf16[32,128]{1,0:T(8,128)(2,1)S(1)}, f32[32,1024]{1,0:T(8,128)S(1)}, bf16[256,128]{1,0:T(8,128)(2,1)S(1)}, bf16[256,128]{1,0:T(8,128)(2,1)S(1)}, b...) custom-call(bf16[1024,512]{1,0:T(8,128)(2,1)} %refs_0_.1, s32[1,1024]{1,0:T(1,128)} %bitcast.5, ...), custom_call_target="tpu_custom_call" | custom-call | tf_op jit(solution)/shard_map/prepare/pallas_call | solution.py:368
  2.9 5.1 %collective-permute-start.2 = (bf16[32,128]{1,0:T(8,128)(2,1)S(1)}, bf16[32,128]{1,0:T(8,128)(2,1)S(1)}, u32[]{:S(2)}, u32[]{:S(2)}) collective-permute-start(bf16[32,128]{1,0:T(8,128)(2,1)S(1)} %get-tuple-element.16.refs_0_), channel_id=1, source_target_pairs={{0,12},{4,8},{8,4},{12,0},{1,13},{5,9},{9,5},{13,1},{2,14},{6,10},... | collective-permute-start | bytes 24584 | tf_op jit(solution)/shard_map/ppermute | solution.py:366
  8.0 0.0 collective-permute-start.1
  8.0 0.6 %collective-permute-start = (bf16[32,128]{1,0:T(8,128)(2,1)S(1)}, bf16[32,128]{1,0:T(8,128)(2,1)S(1)}, u32[]{:S(2)}, u32[]{:S(2)}) collective-permute-start(bf16[32,128]{1,0:T(8,128)(2,1)S(1)} %get-tuple-element.16.refs_0_), channel_id=1, source_target_pairs={{0,4},{4,0},{8,12},{12,8},{1,5},{5,1},{9,13},{13,9},{2,6},{6,2},{1... | collective-permute-start | bytes 24584 | tf_op jit(solution)/shard_map/ppermute | solution.py:366
  9.3 0.3 collective-permute-done.2.refs_3_
  9.6 2.9 %collective-permute-done.1.refs_2_ = bf16[32,128]{1,0:T(8,128)(2,1)S(1)} collective-permute-done((bf16[32,128]{1,0:T(8,128)(2,1)S(1)}, bf16[32,128]{1,0:T(8,128)(2,1)S(1)}, u32[]{:S(2)}, u32[]{:S(2)}) %collective-permute-start.1) | collective-permute-done | bytes 8224 | tf_op jit(solution)/shard_map/ppermute | solution.py:366
  12.6 0.0 collective-permute-done.refs_1_
  12.6 0.3 columns.1
  12.9 0.1 collective-permute-start.5
  13.0 2.1 %collective-permute-start.4 = (bf16[288,128]{1,0:T(8,128)(2,1)S(1)}, bf16[288,128]{1,0:T(8,128)(2,1)S(1)}, u32[]{:S(2)}, u32[]{:S(2)}) collective-permute-start(bf16[288,128]{1,0:T(8,128)(2,1)S(1)} %get-tuple-element.23), channel_id=1, source_target_pairs={{0,8},{4,12},{8,0},{12,4},{1,9},{5,13},{9,1},{13,5},{2,10},{6,14},... | collective-permute-start | bytes 221192 | tf_op jit(solution)/shard_map/ppermute | solution.py:366
  15.1 2.3 %collective-permute-start.3 = (bf16[288,128]{1,0:T(8,128)(2,1)S(1)}, bf16[288,128]{1,0:T(8,128)(2,1)S(1)}, u32[]{:S(2)}, u32[]{:S(2)}) collective-permute-start(bf16[288,128]{1,0:T(8,128)(2,1)S(1)} %get-tuple-element.22), channel_id=1, source_target_pairs={{0,12},{4,8},{8,4},{12,0},{1,13},{5,9},{9,5},{13,1},{2,14},{6,10},... | collective-permute-start | bytes 221192 | tf_op jit(solution)/shard_map/ppermute | solution.py:366
  17.4 2.0 %accumulate_0.1.refs_1_ = f32[32,64,256]{2,1,0:T(8,128)S(1)} custom-call(bf16[288,128]{1,0:T(8,128)(2,1)S(1)} %get-tuple-element.25.refs_0_), custom_call_target="tpu_custom_call" | custom-call | tf_op jit(solution)/shard_map/accumulate_0/pallas_call | solution.py:422
  19.4 0.0 collective-permute-done.5.refs_0_
  19.4 2.1 %accumulate_1.1.refs_1_ = f32[32,64,256]{2,1,0:T(8,128)S(1)} custom-call(bf16[288,128]{1,0:T(8,128)(2,1)S(1)} %collective-permute-done.5.refs_0_, f32[32,64,256]{2,1,0:T(8,128)S(1)} %accumulate_0.1.refs_1_), custom_call_target="tpu_custom_call", output_to_operand_aliasing={{}: (1, {})} | custom-call | tf_op jit(solution)/shard_map/accumulate_1/pallas_call | solution.py:422
  21.5 0.0 collective-permute-done.4.refs_0_
  21.5 2.1 %accumulate_2.1.refs_1_ = f32[32,64,256]{2,1,0:T(8,128)S(1)} custom-call(bf16[288,128]{1,0:T(8,128)(2,1)S(1)} %collective-permute-done.4.refs_0_, f32[32,64,256]{2,1,0:T(8,128)S(1)} %accumulate_1.1.refs_1_), custom_call_target="tpu_custom_call", output_to_operand_aliasing={{}: (1, {})} | custom-call | tf_op jit(solution)/shard_map/accumulate_2/pallas_call | solution.py:422
  23.7 0.0 collective-permute-done.3.refs_0_
  23.7 2.7 %accumulate_3.1 = (f32[32,64,256]{2,1,0:T(8,128)S(1)}, f32[16,8,128]{2,1,0:T(8,128)S(1)}) custom-call(bf16[288,128]{1,0:T(8,128)(2,1)S(1)} %collective-permute-done.3.refs_0_, f32[32,64,256]{2,1,0:T(8,128)S(1)} %accumulate_2.1.refs_1_), custom_call_target="tpu_custom_call", output_to_operand_aliasing={{0}: (1, {})} | custom-call | tf_op jit(solution)/shard_map/accumulate_3/pallas_call | solution.py:422
  26.4 10.3 %all_to_all.5.packed_ref = f32[16,8,128]{2,1,0:T(8,128)S(1)} all-to-all(f32[16,8,128]{2,1,0:T(8,128)S(1)} %get-tuple-element.27), channel_id=1, replica_groups=mesh['groups'=2,'rows'=4,'feat'=4] {'feat','rows'}, dimensions={0} | all-to-all | bytes 131072 | tf_op jit(solution)/shard_map/all_to_all | solution.py:434
  36.7 1.9 %results.1 = (f32[32,64,256]{2,1,0:T(8,128)}, f32[16,32,32]{2,1,0:T(8,128)}) custom-call(f32[32,64,256]{2,1,0:T(8,128)S(1)} %get-tuple-element.26.left_ref, f32[16,8,128]{2,1,0:T(8,128)S(1)} %all_to_all.5.packed_ref), custom_call_target="tpu_custom_call" | custom-call | tf_op jit(solution)/shard_map/results/pallas_call | solution.py:436
Async XLA Ops:
  2.9 6.7 %collective-permute-start.2 = (bf16[32,128]{1,0:T(8,128)(2,1)S(1)}, bf16[32,128]{1,0:T(8,128)(2,1)S(1)}, u32[]{:S(2)}, u32[]{:S(2)}) collective-permute-start(bf16[32,128]{1,0:T(8,128)(2,1)S(1)} %get-tuple-element.16.refs_0_), channel_id=1, source_target_pairs={{0,12},{4,8},{8,4},{12,0},{1,13},{5,9},{9,5},{13,1},{2,14},{6,10},... | collective-permute-start | bytes 24584 | tf_op jit(solution)/shard_map/ppermute | solution.py:366
  8.0 4.5 %collective-permute-start.1 = (bf16[32,128]{1,0:T(8,128)(2,1)S(1)}, bf16[32,128]{1,0:T(8,128)(2,1)S(1)}, u32[]{:S(2)}, u32[]{:S(2)}) collective-permute-start(bf16[32,128]{1,0:T(8,128)(2,1)S(1)} %get-tuple-element.16.refs_0_), channel_id=1, source_target_pairs={{0,8},{4,12},{8,0},{12,4},{1,9},{5,13},{9,1},{13,5},{2,10},{6,14},... | collective-permute-start | bytes 24584 | tf_op jit(solution)/shard_map/ppermute | solution.py:366
  8.0 4.5 %collective-permute-start = (bf16[32,128]{1,0:T(8,128)(2,1)S(1)}, bf16[32,128]{1,0:T(8,128)(2,1)S(1)}, u32[]{:S(2)}, u32[]{:S(2)}) collective-permute-start(bf16[32,128]{1,0:T(8,128)(2,1)S(1)} %get-tuple-element.16.refs_0_), channel_id=1, source_target_pairs={{0,4},{4,0},{8,12},{12,8},{1,5},{5,1},{9,13},{13,9},{2,6},{6,2},{1... | collective-permute-start | bytes 24584 | tf_op jit(solution)/shard_map/ppermute | solution.py:366
  12.9 6.5 %collective-permute-start.5 = (bf16[288,128]{1,0:T(8,128)(2,1)S(1)}, bf16[288,128]{1,0:T(8,128)(2,1)S(1)}, u32[]{:S(2)}, u32[]{:S(2)}) collective-permute-start(bf16[288,128]{1,0:T(8,128)(2,1)S(1)} %get-tuple-element.24), channel_id=1, source_target_pairs={{0,4},{4,0},{8,12},{12,8},{1,5},{5,1},{9,13},{13,9},{2,6},{6,2},{1... | collective-permute-start | bytes 221192 | tf_op jit(solution)/shard_map/ppermute | solution.py:366
  13.0 8.5 %collective-permute-start.4 = (bf16[288,128]{1,0:T(8,128)(2,1)S(1)}, bf16[288,128]{1,0:T(8,128)(2,1)S(1)}, u32[]{:S(2)}, u32[]{:S(2)}) collective-permute-start(bf16[288,128]{1,0:T(8,128)(2,1)S(1)} %get-tuple-element.23), channel_id=1, source_target_pairs={{0,8},{4,12},{8,0},{12,4},{1,9},{5,13},{9,1},{13,5},{2,10},{6,14},... | collective-permute-start | bytes 221192 | tf_op jit(solution)/shard_map/ppermute | solution.py:366
  15.1 8.6 %collective-permute-start.3 = (bf16[288,128]{1,0:T(8,128)(2,1)S(1)}, bf16[288,128]{1,0:T(8,128)(2,1)S(1)}, u32[]{:S(2)}, u32[]{:S(2)}) collective-permute-start(bf16[288,128]{1,0:T(8,128)(2,1)S(1)} %get-tuple-element.22), channel_id=1, source_target_pairs={{0,12},{4,8},{8,4},{12,0},{1,13},{5,9},{9,5},{13,1},{2,14},{6,10},... | collective-permute-start | bytes 221192 | tf_op jit(solution)/shard_map/ppermute | solution.py:366

commit v10 on v9

--- a/solution.py
+++ b/solution.py
@@ -70,9 +70,9 @@
 
 def prepare(rows, *refs):
     given, refs = refs[:5], refs[5:]
-    sums_ref, own_ref, out_refs, refs = refs[0], refs[1], refs[2 : 2 + rows], refs[2 + rows :]
-    taken, (held, sems) = refs[:5], refs[5:]
-    counts_ref, region_ref, node_ref, bins_ref, taps_ref = taken
+    sums_ref, out_refs, refs = refs[0], refs[1 : 1 + rows], refs[1 + rows :]
+    counts_ref, region_ref, node_ref, own_taps_ref, bins_ref, taps_ref, held, sems = refs
+    taken = (counts_ref, region_ref, node_ref, bins_ref, taps_ref)
     copies = [
         pltpu.make_async_copy(source, target, sems.at[at])
         for at, (source, target) in enumerate(zip(given, taken))
@@ -85,7 +85,7 @@
     me = lax.axis_index("rows")
 
     copies[4].wait()
-    own_taps = jnp.concatenate(split_parts(tap_matrix(taps_ref, 0)), axis=0)
+    own_taps_ref[...] = jnp.concatenate(split_parts(tap_matrix(taps_ref, 0)), axis=0)
     store_taps = tap_matrix(taps_ref, 1)
 
     copies[3].wait()
@@ -104,7 +104,6 @@
     for at in (0, 1, 2):
         copies[at].wait()
     counts = counts_ref[...]
-    recent = counts_ref[:, HIST - LANES :]
     store = lax.broadcasted_iota(jnp.int32, (STORES, series), 0)
     pick = jnp.where(store == region_ref[...], 1.0, 0.0).astype(BF16)
     totals = jnp.dot(pick, counts, preferred_element_type=F32)
@@ -128,15 +127,20 @@
         split_parts(forecast) + [jnp.zeros((DAYS, LANES - PIECES * STORES), BF16)], axis=1
     )
 
-    own = lax.dot_general(own_taps, recent, ROW_BY_ROW, preferred_element_type=F32)
+
+def own_terms(counts_ref, region_ref, node_ref, taps_ref, own_ref):
+    counts = counts_ref[...]
+    series = counts.shape[0]
+    own = lax.dot_general(
+        taps_ref[...], counts[:, HIST - LANES :], ROW_BY_ROW, preferred_element_type=F32
+    )
     own = own[:DAYS] + own[DAYS : 2 * DAYS] + own[2 * DAYS :]
     ones = jnp.ones((8, HIST), BF16)
-    level = lax.dot_general(ones, counts, ROW_BY_ROW, preferred_element_type=F32)[:1] / HIST
-    own = own / level
+    mean = lax.dot_general(ones, counts, ROW_BY_ROW, preferred_element_type=F32)[:1] / HIST
+    own = own / mean
     day = lax.broadcasted_iota(jnp.int32, (DAYS, series), 0)
     own = jnp.where(day == REGION_ROW, region_ref[...].astype(F32), own)
-    own = jnp.where(day == NODE_ROW, node_ref[...].astype(F32), own)
-    own_ref[...] = own
+    own_ref[...] = jnp.where(day == NODE_ROW, node_ref[...].astype(F32), own)
 
 
 def columns(rows, quant_ref, *refs):
@@ -319,16 +323,8 @@
 def results(left_ref, packed_ref, hist_ref, best_ref, hist_held, best_held, sems):
     feats = left_ref.shape[0]
     targets, packed_rows, _ = packed_ref.shape
-    for target in range(targets):
-        packed = packed_ref[target]
-        for at in range(LANES // NODES):
-            best_held[target, at * packed_rows : (at + 1) * packed_rows] = packed[
-                :, at * NODES : (at + 1) * NODES
-            ]
-    best_copy = pltpu.make_async_copy(best_held, best_ref, sems.at[1])
-    best_copy.start()
     first_bin = lax.broadcasted_iota(jnp.int32, (2 * NODES, HALF), 1) == 0
-    group = min(feats, 4)
+    group = min(feats, 8)
 
     def one_group(at, carry):
         for member in range(group):
@@ -343,6 +339,14 @@
         return carry
 
     lax.fori_loop(0, feats // group, one_group, 0)
+    for target in range(targets):
+        packed = packed_ref[target]
+        for at in range(LANES // NODES):
+            best_held[target, at * packed_rows : (at + 1) * packed_rows] = packed[
+                :, at * NODES : (at + 1) * NODES
+            ]
+    best_copy = pltpu.make_async_copy(best_held, best_ref, sems.at[1])
+    best_copy.start()
     pltpu.make_async_copy(hist_held, hist_ref, sems.at[0]).wait()
     best_copy.wait()
 
@@ -365,17 +369,19 @@
         pairs = [(at, partner(at, step, rows)) for at in range(rows)]
         return lax.ppermute(array, "rows", pairs)
 
-    sums, own, *bins = pl.pallas_call(
+    sums, *bins = pl.pallas_call(
         functools.partial(prepare, rows),
         out_shape=[jax.ShapeDtypeStruct((DAYS, LANES), BF16)]
-        + [jax.ShapeDtypeStruct((DAYS, series), F32)]
-        + [jax.ShapeDtypeStruct((blocks * pad, LANES), BF16)] * rows,
+        + [jax.ShapeDtypeStruct((blocks * pad, LANES), BF16)] * rows
+        + [
+            jax.ShapeDtypeStruct(daily_unit_counts.shape, BF16),
+            jax.ShapeDtypeStruct((1, series), jnp.int32),
+            jax.ShapeDtypeStruct((1, series), jnp.int32),
+            jax.ShapeDtypeStruct((PIECES * DAYS, LANES), BF16),
+        ],
         in_specs=[hbm] * 5,
-        out_specs=[vmem] * (2 + rows),
+        out_specs=[vmem] * (5 + rows),
         scratch_shapes=[
-            pltpu.VMEM(daily_unit_counts.shape, BF16),
-            pltpu.VMEM((1, series), jnp.int32),
-            pltpu.VMEM((1, series), jnp.int32),
             pltpu.VMEM(bin_ids.shape, jnp.int32),
             pltpu.VMEM((TAPS, CHANNELS), F32),
             pltpu.VMEM((rows, pad, series), BF16),
@@ -389,6 +395,15 @@
             for array in (daily_unit_counts, regions, nodes, bin_ids, filter_kernels.T)
         )
     )
+    bins, passed = bins[:rows], bins[rows:]
+    own = pl.pallas_call(
+        own_terms,
+        out_shape=jax.ShapeDtypeStruct((DAYS, series), F32),
+        in_specs=[vmem] * 4,
+        out_specs=vmem,
+        compiler_params=params,
+        name="own_terms",
+    )(*passed)
     sums = [sums] + [exchange(sums, step) for step in range(1, rows)]
     outgoing = pl.pallas_call(
         functools.partial(columns, rows),

time: 38.9 us -> 38.4 us (0.987)
  waiting for transfers between devices: 3.27 us -> 2.77 us
    ppermute x6, waiting for transfers between devices: 3.27 us -> 2.77 us  [exchange(): return lax.ppermute(array, 'rows', pairs)]
    pallas_call x0 -> x1, Pallas kernels: none -> 0.48 us  [shards(): pl.pallas_call(own_terms, out_shape=jax.ShapeDtypeStruct((DAYS, series),...]
  transfers between devices with their start and end apart: 6 -> 6, of which waited for: 2 -> 1; matrix products, arithmetic and copies ran while one was open for 0% -> 0% of each run, Pallas kernels for 16% -> 18%
where the time goes in v10:
time: 38.4 us; the launch traced here: 38.2 us
  Pallas kernels  13.5 us (35%)
  blocking collectives  10.3 us (27%)
  starting transfers between devices  10.2 us (27%)
  waiting for transfers between devices  2.77 us (7%)
  between operations  1.38 us (4%)
    all_to_all x1, blocking collectives, shards(): gathered = lax.all_to_all(best, ('feat', 'rows'), 0, 0, tiled=True)  10.3 us
    ppermute x6, starting transfers between devices, exchange(): return lax.ppermute(array, 'rows', pairs)  10.2 us
    pallas_call x4, Pallas kernels, shards(): pl.pallas_call(functools.partial(accumulate, count, feats, first, last),...  8.98 us
    ppermute x6, waiting for transfers between devices, exchange(): return lax.ppermute(array, 'rows', pairs)  2.77 us
    pallas_call x1, Pallas kernels, shards(): pl.pallas_call(functools.partial(prepare, rows), out_shape=[jax.ShapeDtyp...  2.01 us
    pallas_call x1, Pallas kernels, shards(): pl.pallas_call(results, out_shape=[hist_shape, best_shape], in_specs=[vme...  1.72 us
  transfers between devices with their start and end apart: 6, of which 1 were waited for; matrix products, arithmetic and copies ran while one was open for 0% of the time, Pallas kernels for 18%

profile of v10, /device:TPU:0, one launch (start us, length us, event | category | flops | bytes accessed | tf_op | source)
XLA Modules:
  0.0 38.2 jit_solution(6556541419981887355)
XLA Ops:
  0.6 2.0 %prepare.1 = (bf16[32,128]{1,0:T(8,128)(2,1)S(1)}, bf16[256,128]{1,0:T(8,128)(2,1)S(1)}, bf16[256,128]{1,0:T(8,128)(2,1)S(1)}, bf16[256,128]{1,0:T(8,128)(2,1)S(...) custom-call(bf16[1024,512]{1,0:T(8,128)(2,1)} %refs_0_.1, ...), custom_call_target="tpu_custom_call" | custom-call | tf_op jit(solution)/shard_map/prepare/pallas_call | solution.py:372
  2.6 5.1 %collective-permute-start.2 = (bf16[32,128]{1,0:T(8,128)(2,1)S(1)}, bf16[32,128]{1,0:T(8,128)(2,1)S(1)}, u32[]{:S(2)}, u32[]{:S(2)}) collective-permute-start(bf16[32,128]{1,0:T(8,128)(2,1)S(1)} %get-tuple-element.19.refs_0_), channel_id=1, source_target_pairs={{0,12},{4,8},{8,4},{12,0},{1,13},{5,9},{9,5},{13,1},{2,14},{6,10},... | collective-permute-start | bytes 24584 | tf_op jit(solution)/shard_map/ppermute | solution.py:370
  7.8 0.0 collective-permute-start.1
  7.8 0.6 %collective-permute-start = (bf16[32,128]{1,0:T(8,128)(2,1)S(1)}, bf16[32,128]{1,0:T(8,128)(2,1)S(1)}, u32[]{:S(2)}, u32[]{:S(2)}) collective-permute-start(bf16[32,128]{1,0:T(8,128)(2,1)S(1)} %get-tuple-element.19.refs_0_), channel_id=1, source_target_pairs={{0,4},{4,0},{8,12},{12,8},{1,5},{5,1},{9,13},{13,9},{2,6},{6,2},{1... | collective-permute-start | bytes 24584 | tf_op jit(solution)/shard_map/ppermute | solution.py:370
  9.1 0.5 %own_terms.1.refs_4_ = f32[32,1024]{1,0:T(8,128)S(1)} custom-call(bf16[1024,512]{1,0:T(8,128)(2,1)S(1)} %get-tuple-element.20.counts_ref, s32[1,1024]{1,0:T(1,128)S(1)} %get-tuple-element.21.region_ref, s32[1,1024]{1,0:T(1,128)S(1)} %get-tuple-element.22.node_ref, bf16[96,128]{1,0:T(8,128)(2,1)S(1)} %get-tuple-element.23.taps_ref), custom_call_target="tpu_custom_call" | custom-call | tf_op jit(solution)/shard_map/own_terms/pallas_call | solution.py:399
  9.5 0.0 collective-permute-done.2.refs_3_
  9.5 2.8 %collective-permute-done.1.refs_2_ = bf16[32,128]{1,0:T(8,128)(2,1)S(1)} collective-permute-done((bf16[32,128]{1,0:T(8,128)(2,1)S(1)}, bf16[32,128]{1,0:T(8,128)(2,1)S(1)}, u32[]{:S(2)}, u32[]{:S(2)}) %collective-permute-start.1) | collective-permute-done | bytes 8224 | tf_op jit(solution)/shard_map/ppermute | solution.py:370
  12.3 0.0 collective-permute-done.refs_1_
  12.3 0.3 columns.1
  12.7 0.1 collective-permute-start.5
  12.7 2.1 %collective-permute-start.4 = (bf16[288,128]{1,0:T(8,128)(2,1)S(1)}, bf16[288,128]{1,0:T(8,128)(2,1)S(1)}, u32[]{:S(2)}, u32[]{:S(2)}) collective-permute-start(bf16[288,128]{1,0:T(8,128)(2,1)S(1)} %get-tuple-element.29), channel_id=1, source_target_pairs={{0,8},{4,12},{8,0},{12,4},{1,9},{5,13},{9,1},{13,5},{2,10},{6,14},... | collective-permute-start | bytes 221192 | tf_op jit(solution)/shard_map/ppermute | solution.py:370
  14.8 2.3 %collective-permute-start.3 = (bf16[288,128]{1,0:T(8,128)(2,1)S(1)}, bf16[288,128]{1,0:T(8,128)(2,1)S(1)}, u32[]{:S(2)}, u32[]{:S(2)}) collective-permute-start(bf16[288,128]{1,0:T(8,128)(2,1)S(1)} %get-tuple-element.28), channel_id=1, source_target_pairs={{0,12},{4,8},{8,4},{12,0},{1,13},{5,9},{9,5},{13,1},{2,14},{6,10},... | collective-permute-start | bytes 221192 | tf_op jit(solution)/shard_map/ppermute | solution.py:370
  17.1 2.0 %accumulate_0.1.refs_1_ = f32[32,64,256]{2,1,0:T(8,128)S(1)} custom-call(bf16[288,128]{1,0:T(8,128)(2,1)S(1)} %get-tuple-element.31.refs_0_), custom_call_target="tpu_custom_call" | custom-call | tf_op jit(solution)/shard_map/accumulate_0/pallas_call | solution.py:437
  19.2 0.0 collective-permute-done.5.refs_0_
  19.2 2.1 %accumulate_1.1.refs_1_ = f32[32,64,256]{2,1,0:T(8,128)S(1)} custom-call(bf16[288,128]{1,0:T(8,128)(2,1)S(1)} %collective-permute-done.5.refs_0_, f32[32,64,256]{2,1,0:T(8,128)S(1)} %accumulate_0.1.refs_1_), custom_call_target="tpu_custom_call", output_to_operand_aliasing={{}: (1, {})} | custom-call | tf_op jit(solution)/shard_map/accumulate_1/pallas_call | solution.py:437
  21.3 0.0 collective-permute-done.4.refs_0_
  21.3 2.1 %accumulate_2.1.refs_1_ = f32[32,64,256]{2,1,0:T(8,128)S(1)} custom-call(bf16[288,128]{1,0:T(8,128)(2,1)S(1)} %collective-permute-done.4.refs_0_, f32[32,64,256]{2,1,0:T(8,128)S(1)} %accumulate_1.1.refs_1_), custom_call_target="tpu_custom_call", output_to_operand_aliasing={{}: (1, {})} | custom-call | tf_op jit(solution)/shard_map/accumulate_2/pallas_call | solution.py:437
  23.4 0.0 collective-permute-done.3.refs_0_
  23.4 2.7 %accumulate_3.1 = (f32[32,64,256]{2,1,0:T(8,128)S(1)}, f32[16,8,128]{2,1,0:T(8,128)S(1)}) custom-call(bf16[288,128]{1,0:T(8,128)(2,1)S(1)} %collective-permute-done.3.refs_0_, f32[32,64,256]{2,1,0:T(8,128)S(1)} %accumulate_2.1.refs_1_), custom_call_target="tpu_custom_call", output_to_operand_aliasing={{0}: (1, {})} | custom-call | tf_op jit(solution)/shard_map/accumulate_3/pallas_call | solution.py:437
  26.2 10.3 %all_to_all.5.packed_ref = f32[16,8,128]{2,1,0:T(8,128)S(1)} all-to-all(f32[16,8,128]{2,1,0:T(8,128)S(1)} %get-tuple-element.33), channel_id=1, replica_groups=mesh['groups'=2,'rows'=4,'feat'=4] {'feat','rows'}, dimensions={0} | all-to-all | bytes 131072 | tf_op jit(solution)/shard_map/all_to_all | solution.py:449
  36.5 1.7 %results.1 = (f32[32,64,256]{2,1,0:T(8,128)}, f32[16,32,32]{2,1,0:T(8,128)}) custom-call(f32[32,64,256]{2,1,0:T(8,128)S(1)} %get-tuple-element.32.left_ref, f32[16,8,128]{2,1,0:T(8,128)S(1)} %all_to_all.5.packed_ref), custom_call_target="tpu_custom_call" | custom-call | tf_op jit(solution)/shard_map/results/pallas_call | solution.py:451
Async XLA Ops:
  2.6 6.9 %collective-permute-start.2 = (bf16[32,128]{1,0:T(8,128)(2,1)S(1)}, bf16[32,128]{1,0:T(8,128)(2,1)S(1)}, u32[]{:S(2)}, u32[]{:S(2)}) collective-permute-start(bf16[32,128]{1,0:T(8,128)(2,1)S(1)} %get-tuple-element.19.refs_0_), channel_id=1, source_target_pairs={{0,12},{4,8},{8,4},{12,0},{1,13},{5,9},{9,5},{13,1},{2,14},{6,10},... | collective-permute-start | bytes 24584 | tf_op jit(solution)/shard_map/ppermute | solution.py:370
  7.8 4.5 %collective-permute-start.1 = (bf16[32,128]{1,0:T(8,128)(2,1)S(1)}, bf16[32,128]{1,0:T(8,128)(2,1)S(1)}, u32[]{:S(2)}, u32[]{:S(2)}) collective-permute-start(bf16[32,128]{1,0:T(8,128)(2,1)S(1)} %get-tuple-element.19.refs_0_), channel_id=1, source_target_pairs={{0,8},{4,12},{8,0},{12,4},{1,9},{5,13},{9,1},{13,5},{2,10},{6,14},... | collective-permute-start | bytes 24584 | tf_op jit(solution)/shard_map/ppermute | solution.py:370
  7.8 4.5 %collective-permute-start = (bf16[32,128]{1,0:T(8,128)(2,1)S(1)}, bf16[32,128]{1,0:T(8,128)(2,1)S(1)}, u32[]{:S(2)}, u32[]{:S(2)}) collective-permute-start(bf16[32,128]{1,0:T(8,128)(2,1)S(1)} %get-tuple-element.19.refs_0_), channel_id=1, source_target_pairs={{0,4},{4,0},{8,12},{12,8},{1,5},{5,1},{9,13},{13,9},{2,6},{6,2},{1... | collective-permute-start | bytes 24584 | tf_op jit(solution)/shard_map/ppermute | solution.py:370
  12.7 6.5 %collective-permute-start.5 = (bf16[288,128]{1,0:T(8,128)(2,1)S(1)}, bf16[288,128]{1,0:T(8,128)(2,1)S(1)}, u32[]{:S(2)}, u32[]{:S(2)}) collective-permute-start(bf16[288,128]{1,0:T(8,128)(2,1)S(1)} %get-tuple-element.30), channel_id=1, source_target_pairs={{0,4},{4,0},{8,12},{12,8},{1,5},{5,1},{9,13},{13,9},{2,6},{6,2},{1... | collective-permute-start | bytes 221192 | tf_op jit(solution)/shard_map/ppermute | solution.py:370
  12.7 8.5 %collective-permute-start.4 = (bf16[288,128]{1,0:T(8,128)(2,1)S(1)}, bf16[288,128]{1,0:T(8,128)(2,1)S(1)}, u32[]{:S(2)}, u32[]{:S(2)}) collective-permute-start(bf16[288,128]{1,0:T(8,128)(2,1)S(1)} %get-tuple-element.29), channel_id=1, source_target_pairs={{0,8},{4,12},{8,0},{12,4},{1,9},{5,13},{9,1},{13,5},{2,10},{6,14},... | collective-permute-start | bytes 221192 | tf_op jit(solution)/shard_map/ppermute | solution.py:370
  14.8 8.6 %collective-permute-start.3 = (bf16[288,128]{1,0:T(8,128)(2,1)S(1)}, bf16[288,128]{1,0:T(8,128)(2,1)S(1)}, u32[]{:S(2)}, u32[]{:S(2)}) collective-permute-start(bf16[288,128]{1,0:T(8,128)(2,1)S(1)} %get-tuple-element.28), channel_id=1, source_target_pairs={{0,12},{4,8},{8,4},{12,0},{1,13},{5,9},{9,5},{13,1},{2,14},{6,10},... | collective-permute-start | bytes 221192 | tf_op jit(solution)/shard_map/ppermute | solution.py:370

commit v11 on v10

--- a/solution.py
+++ b/solution.py
@@ -68,38 +68,20 @@
     return jnp.where(day < HORIZON, matrix, 0.0)
 
 
-def prepare(rows, *refs):
-    given, refs = refs[:5], refs[5:]
-    sums_ref, out_refs, refs = refs[0], refs[1 : 1 + rows], refs[1 + rows :]
-    counts_ref, region_ref, node_ref, own_taps_ref, bins_ref, taps_ref, held, sems = refs
+def prepare(*refs):
+    given, sums_ref, refs = refs[:5], refs[5], refs[6:]
+    counts_ref, region_ref, node_ref, bins_ref, own_taps_ref, taps_ref, sems = refs
     taken = (counts_ref, region_ref, node_ref, bins_ref, taps_ref)
     copies = [
         pltpu.make_async_copy(source, target, sems.at[at])
         for at, (source, target) in enumerate(zip(given, taken))
     ]
-    for at in (4, 3, 0, 1, 2):
+    for at in (4, 0, 1, 2, 3):
         copies[at].start()
     series = counts_ref.shape[0]
-    feats = bins_ref.shape[1] // rows
-    pad = held.shape[1]
-    me = lax.axis_index("rows")
-
     copies[4].wait()
     own_taps_ref[...] = jnp.concatenate(split_parts(tap_matrix(taps_ref, 0)), axis=0)
     store_taps = tap_matrix(taps_ref, 1)
-
-    copies[3].wait()
-    turned = bins_ref[...].astype(F32).T
-    for row_block in range(rows):
-        part = turned[row_block * feats : (row_block + 1) * feats]
-        if pad > feats:
-            part = jnp.concatenate([part, jnp.zeros((pad - feats, series), F32)], axis=0)
-        held[row_block] = part.astype(BF16)
-    for step in range(rows):
-        bins = held[partner(me, step, rows)]
-        for block in range(series // LANES):
-            lanes = slice(block * LANES, (block + 1) * LANES)
-            out_refs[step][block * pad : (block + 1) * pad] = bins[:, lanes]
 
     for at in (0, 1, 2):
         copies[at].wait()
@@ -126,11 +108,16 @@
     sums_ref[...] = jnp.concatenate(
         split_parts(forecast) + [jnp.zeros((DAYS, LANES - PIECES * STORES), BF16)], axis=1
     )
-
-
-def own_terms(counts_ref, region_ref, node_ref, taps_ref, own_ref):
+    copies[3].wait()
+
+
+def local_terms(rows, counts_ref, region_ref, node_ref, bins_ref, taps_ref, own_ref, *refs):
+    out_refs, held = refs[:rows], refs[rows]
     counts = counts_ref[...]
     series = counts.shape[0]
+    feats = bins_ref.shape[1] // rows
+    pad = held.shape[1]
+    me = lax.axis_index("rows")
     own = lax.dot_general(
         taps_ref[...], counts[:, HIST - LANES :], ROW_BY_ROW, preferred_element_type=F32
     )
@@ -141,6 +128,18 @@
     day = lax.broadcasted_iota(jnp.int32, (DAYS, series), 0)
     own = jnp.where(day == REGION_ROW, region_ref[...].astype(F32), own)
     own_ref[...] = jnp.where(day == NODE_ROW, node_ref[...].astype(F32), own)
+
+    turned = bins_ref[...].astype(F32).T
+    for row_block in range(rows):
+        part = turned[row_block * feats : (row_block + 1) * feats]
+        if pad > feats:
+            part = jnp.concatenate([part, jnp.zeros((pad - feats, series), F32)], axis=0)
+        held[row_block] = part.astype(BF16)
+    for step in range(rows):
+        bins = held[partner(me, step, rows)]
+        for block in range(series // LANES):
+            lanes = slice(block * LANES, (block + 1) * LANES)
+            out_refs[step][block * pad : (block + 1) * pad] = bins[:, lanes]
 
 
 def columns(rows, quant_ref, *refs):
@@ -324,7 +323,7 @@
     feats = left_ref.shape[0]
     targets, packed_rows, _ = packed_ref.shape
     first_bin = lax.broadcasted_iota(jnp.int32, (2 * NODES, HALF), 1) == 0
-    group = min(feats, 8)
+    group = min(feats, 4)
 
     def one_group(at, carry):
         for member in range(group):
@@ -338,7 +337,8 @@
         pltpu.make_async_copy(hist_held.at[here], hist_ref.at[here], sems.at[0]).start()
         return carry
 
-    lax.fori_loop(0, feats // group, one_group, 0)
+    for step in range(feats // group):
+        one_group(step, 0)
     for target in range(targets):
         packed = packed_ref[target]
         for at in range(LANES // NODES):
@@ -369,24 +369,19 @@
         pairs = [(at, partner(at, step, rows)) for at in range(rows)]
         return lax.ppermute(array, "rows", pairs)
 
-    sums, *bins = pl.pallas_call(
-        functools.partial(prepare, rows),
-        out_shape=[jax.ShapeDtypeStruct((DAYS, LANES), BF16)]
-        + [jax.ShapeDtypeStruct((blocks * pad, LANES), BF16)] * rows
-        + [
+    sums, *passed = pl.pallas_call(
+        prepare,
+        out_shape=[
+            jax.ShapeDtypeStruct((DAYS, LANES), BF16),
             jax.ShapeDtypeStruct(daily_unit_counts.shape, BF16),
             jax.ShapeDtypeStruct((1, series), jnp.int32),
             jax.ShapeDtypeStruct((1, series), jnp.int32),
+            jax.ShapeDtypeStruct(bin_ids.shape, jnp.int32),
             jax.ShapeDtypeStruct((PIECES * DAYS, LANES), BF16),
         ],
         in_specs=[hbm] * 5,
-        out_specs=[vmem] * (5 + rows),
-        scratch_shapes=[
-            pltpu.VMEM(bin_ids.shape, jnp.int32),
-            pltpu.VMEM((TAPS, CHANNELS), F32),
-            pltpu.VMEM((rows, pad, series), BF16),
-            pltpu.SemaphoreType.DMA((5,)),
-        ],
+        out_specs=[vmem] * 6,
+        scratch_shapes=[pltpu.VMEM((TAPS, CHANNELS), F32), pltpu.SemaphoreType.DMA((5,))],
         compiler_params=params,
         name="prepare",
     )(
@@ -395,14 +390,15 @@
             for array in (daily_unit_counts, regions, nodes, bin_ids, filter_kernels.T)
         )
     )
-    bins, passed = bins[:rows], bins[rows:]
-    own = pl.pallas_call(
-        own_terms,
-        out_shape=jax.ShapeDtypeStruct((DAYS, series), F32),
-        in_specs=[vmem] * 4,
-        out_specs=vmem,
+    own, *bins = pl.pallas_call(
+        functools.partial(local_terms, rows),
+        out_shape=[jax.ShapeDtypeStruct((DAYS, series), F32)]
+        + [jax.ShapeDtypeStruct((blocks * pad, LANES), BF16)] * rows,
+        in_specs=[vmem] * 5,
+        out_specs=[vmem] * (1 + rows),
+        scratch_shapes=[pltpu.VMEM((rows, pad, series), BF16)],
         compiler_params=params,
-        name="own_terms",
+        name="local_terms",
     )(*passed)
     sums = [sums] + [exchange(sums, step) for step in range(1, rows)]
     outgoing = pl.pallas_call(

time: 38.4 us -> 38.1 us (level)
  no operation moved by 1% of the time
where the time goes in v11:
time: 38.1 us; the launch traced here: 37.9 us
  Pallas kernels  13.2 us (35%)
  blocking collectives  10.3 us (27%)
  starting transfers between devices  10.2 us (27%)
  waiting for transfers between devices  2.77 us (7%)
  between operations  1.37 us (4%)
    all_to_all x1, blocking collectives, shards(): gathered = lax.all_to_all(best, ('feat', 'rows'), 0, 0, tiled=True)  10.3 us
    ppermute x6, starting transfers between devices, exchange(): return lax.ppermute(array, 'rows', pairs)  10.2 us
    pallas_call x4, Pallas kernels, shards(): pl.pallas_call(functools.partial(accumulate, count, feats, first, last),...  8.98 us
    ppermute x6, waiting for transfers between devices, exchange(): return lax.ppermute(array, 'rows', pairs)  2.77 us
    pallas_call x1, Pallas kernels, shards(): pl.pallas_call(prepare, out_shape=[jax.ShapeDtypeStruct((DAYS, LANES), BF...  1.85 us
    pallas_call x1, Pallas kernels, shards(): pl.pallas_call(results, out_shape=[hist_shape, best_shape], in_specs=[vme...  1.54 us
  transfers between devices with their start and end apart: 6, of which 1 were waited for; matrix products, arithmetic and copies ran while one was open for 0% of the time, Pallas kernels for 18%

profile of v11, /device:TPU:0, one launch (start us, length us, event | category | flops | bytes accessed | tf_op | source)
XLA Modules:
  0.0 37.9 jit_solution(16366325702920242814)
XLA Ops:
  0.6 1.8 %prepare.1 = (bf16[32,128]{1,0:T(8,128)(2,1)S(1)}, bf16[1024,512]{1,0:T(8,128)(2,1)S(1)}, s32[1,1024]{1,0:T(1,128)S(1)}, s32[1,1024]{1,0:T(1,128)S(1)}, s32[1024...) custom-call(bf16[1024,512]{1,0:T(8,128)(2,1)} %refs_0_.1, s32[1,1024]{1,0:T(1,128)} %bitcast.5, s32[1,1024]{1,0:T(1,128)} %bitcast.6, ...), custom_call_target="tpu_custom_call" | custom-call | tf_op jit(solution)/shard_map/prepare/pallas_call | solution.py:372
  2.5 5.1 %collective-permute-start.2 = (bf16[32,128]{1,0:T(8,128)(2,1)S(1)}, bf16[32,128]{1,0:T(8,128)(2,1)S(1)}, u32[]{:S(2)}, u32[]{:S(2)}) collective-permute-start(bf16[32,128]{1,0:T(8,128)(2,1)S(1)} %get-tuple-element.21.refs_0_), channel_id=1, source_target_pairs={{0,12},{4,8},{8,4},{12,0},{1,13},{5,9},{9,5},{13,1},{2,14},{6,10},... | collective-permute-start | bytes 24584 | tf_op jit(solution)/shard_map/ppermute | solution.py:370
  7.6 0.0 collective-permute-start.1
  7.6 0.6 %collective-permute-start = (bf16[32,128]{1,0:T(8,128)(2,1)S(1)}, bf16[32,128]{1,0:T(8,128)(2,1)S(1)}, u32[]{:S(2)}, u32[]{:S(2)}) collective-permute-start(bf16[32,128]{1,0:T(8,128)(2,1)S(1)} %get-tuple-element.21.refs_0_), channel_id=1, source_target_pairs={{0,4},{4,0},{8,12},{12,8},{1,5},{5,1},{9,13},{13,9},{2,6},{6,2},{1... | collective-permute-start | bytes 24584 | tf_op jit(solution)/shard_map/ppermute | solution.py:370
  8.9 0.5 %local_terms.1 = (f32[32,1024]{1,0:T(8,128)S(1)}, bf16[256,128]{1,0:T(8,128)(2,1)S(1)}, bf16[256,128]{1,0:T(8,128)(2,1)S(1)}, bf16[256,128]{1,0:T(8,128)(2,1)S(1)}, bf16[256,128]{1,0:T(8,128)(2,1)S(1)}) custom-call(bf16[1024,512]{1,0:T(8,128)(2,1)S(1)} %get-tuple-element.22.counts_ref, s32[1,1024]{1,0:T(1,128)S(1)} %get-tuple-element.23.region_ref, ...), custom_call_target="tpu_custom_call" | custom-call | tf_op jit(solution)/shard_map/local_terms/pallas_call | solution.py:393
  9.4 0.0 collective-permute-done.2.refs_3_
  9.4 2.8 %collective-permute-done.1.refs_2_ = bf16[32,128]{1,0:T(8,128)(2,1)S(1)} collective-permute-done((bf16[32,128]{1,0:T(8,128)(2,1)S(1)}, bf16[32,128]{1,0:T(8,128)(2,1)S(1)}, u32[]{:S(2)}, u32[]{:S(2)}) %collective-permute-start.1) | collective-permute-done | bytes 8224 | tf_op jit(solution)/shard_map/ppermute | solution.py:370
  12.1 0.0 collective-permute-done.refs_1_
  12.2 0.3 columns.1
  12.5 0.1 collective-permute-start.5
  12.6 2.1 %collective-permute-start.4 = (bf16[288,128]{1,0:T(8,128)(2,1)S(1)}, bf16[288,128]{1,0:T(8,128)(2,1)S(1)}, u32[]{:S(2)}, u32[]{:S(2)}) collective-permute-start(bf16[288,128]{1,0:T(8,128)(2,1)S(1)} %get-tuple-element.33), channel_id=1, source_target_pairs={{0,8},{4,12},{8,0},{12,4},{1,9},{5,13},{9,1},{13,5},{2,10},{6,14},... | collective-permute-start | bytes 221192 | tf_op jit(solution)/shard_map/ppermute | solution.py:370
  14.7 2.3 %collective-permute-start.3 = (bf16[288,128]{1,0:T(8,128)(2,1)S(1)}, bf16[288,128]{1,0:T(8,128)(2,1)S(1)}, u32[]{:S(2)}, u32[]{:S(2)}) collective-permute-start(bf16[288,128]{1,0:T(8,128)(2,1)S(1)} %get-tuple-element.32), channel_id=1, source_target_pairs={{0,12},{4,8},{8,4},{12,0},{1,13},{5,9},{9,5},{13,1},{2,14},{6,10},... | collective-permute-start | bytes 221192 | tf_op jit(solution)/shard_map/ppermute | solution.py:370
  17.0 2.0 %accumulate_0.1.refs_1_ = f32[32,64,256]{2,1,0:T(8,128)S(1)} custom-call(bf16[288,128]{1,0:T(8,128)(2,1)S(1)} %get-tuple-element.35.refs_0_), custom_call_target="tpu_custom_call" | custom-call | tf_op jit(solution)/shard_map/accumulate_0/pallas_call | solution.py:433
  19.0 0.0 collective-permute-done.5.refs_0_
  19.0 2.1 %accumulate_1.1.refs_1_ = f32[32,64,256]{2,1,0:T(8,128)S(1)} custom-call(bf16[288,128]{1,0:T(8,128)(2,1)S(1)} %collective-permute-done.5.refs_0_, f32[32,64,256]{2,1,0:T(8,128)S(1)} %accumulate_0.1.refs_1_), custom_call_target="tpu_custom_call", output_to_operand_aliasing={{}: (1, {})} | custom-call | tf_op jit(solution)/shard_map/accumulate_1/pallas_call | solution.py:433
  21.1 0.0 collective-permute-done.4.refs_0_
  21.1 2.1 %accumulate_2.1.refs_1_ = f32[32,64,256]{2,1,0:T(8,128)S(1)} custom-call(bf16[288,128]{1,0:T(8,128)(2,1)S(1)} %collective-permute-done.4.refs_0_, f32[32,64,256]{2,1,0:T(8,128)S(1)} %accumulate_1.1.refs_1_), custom_call_target="tpu_custom_call", output_to_operand_aliasing={{}: (1, {})} | custom-call | tf_op jit(solution)/shard_map/accumulate_2/pallas_call | solution.py:433
  23.2 0.0 collective-permute-done.3.refs_0_
  23.3 2.7 %accumulate_3.1 = (f32[32,64,256]{2,1,0:T(8,128)S(1)}, f32[16,8,128]{2,1,0:T(8,128)S(1)}) custom-call(bf16[288,128]{1,0:T(8,128)(2,1)S(1)} %collective-permute-done.3.refs_0_, f32[32,64,256]{2,1,0:T(8,128)S(1)} %accumulate_2.1.refs_1_), custom_call_target="tpu_custom_call", output_to_operand_aliasing={{0}: (1, {})} | custom-call | tf_op jit(solution)/shard_map/accumulate_3/pallas_call | solution.py:433
  26.0 10.3 %all_to_all.5.packed_ref = f32[16,8,128]{2,1,0:T(8,128)S(1)} all-to-all(f32[16,8,128]{2,1,0:T(8,128)S(1)} %get-tuple-element.37), channel_id=1, replica_groups=mesh['groups'=2,'rows'=4,'feat'=4] {'feat','rows'}, dimensions={0} | all-to-all | bytes 131072 | tf_op jit(solution)/shard_map/all_to_all | solution.py:445
  36.3 1.5 %results.1 = (f32[32,64,256]{2,1,0:T(8,128)}, f32[16,32,32]{2,1,0:T(8,128)}) custom-call(f32[32,64,256]{2,1,0:T(8,128)S(1)} %get-tuple-element.36.left_ref, f32[16,8,128]{2,1,0:T(8,128)S(1)} %all_to_all.5.packed_ref), custom_call_target="tpu_custom_call" | custom-call | tf_op jit(solution)/shard_map/results/pallas_call | solution.py:447
Async XLA Ops:
  2.5 6.9 %collective-permute-start.2 = (bf16[32,128]{1,0:T(8,128)(2,1)S(1)}, bf16[32,128]{1,0:T(8,128)(2,1)S(1)}, u32[]{:S(2)}, u32[]{:S(2)}) collective-permute-start(bf16[32,128]{1,0:T(8,128)(2,1)S(1)} %get-tuple-element.21.refs_0_), channel_id=1, source_target_pairs={{0,12},{4,8},{8,4},{12,0},{1,13},{5,9},{9,5},{13,1},{2,14},{6,10},... | collective-permute-start | bytes 24584 | tf_op jit(solution)/shard_map/ppermute | solution.py:370
  7.6 4.5 %collective-permute-start.1 = (bf16[32,128]{1,0:T(8,128)(2,1)S(1)}, bf16[32,128]{1,0:T(8,128)(2,1)S(1)}, u32[]{:S(2)}, u32[]{:S(2)}) collective-permute-start(bf16[32,128]{1,0:T(8,128)(2,1)S(1)} %get-tuple-element.21.refs_0_), channel_id=1, source_target_pairs={{0,8},{4,12},{8,0},{12,4},{1,9},{5,13},{9,1},{13,5},{2,10},{6,14},... | collective-permute-start | bytes 24584 | tf_op jit(solution)/shard_map/ppermute | solution.py:370
  7.6 4.5 %collective-permute-start = (bf16[32,128]{1,0:T(8,128)(2,1)S(1)}, bf16[32,128]{1,0:T(8,128)(2,1)S(1)}, u32[]{:S(2)}, u32[]{:S(2)}) collective-permute-start(bf16[32,128]{1,0:T(8,128)(2,1)S(1)} %get-tuple-element.21.refs_0_), channel_id=1, source_target_pairs={{0,4},{4,0},{8,12},{12,8},{1,5},{5,1},{9,13},{13,9},{2,6},{6,2},{1... | collective-permute-start | bytes 24584 | tf_op jit(solution)/shard_map/ppermute | solution.py:370
  12.5 6.5 %collective-permute-start.5 = (bf16[288,128]{1,0:T(8,128)(2,1)S(1)}, bf16[288,128]{1,0:T(8,128)(2,1)S(1)}, u32[]{:S(2)}, u32[]{:S(2)}) collective-permute-start(bf16[288,128]{1,0:T(8,128)(2,1)S(1)} %get-tuple-element.34), channel_id=1, source_target_pairs={{0,4},{4,0},{8,12},{12,8},{1,5},{5,1},{9,13},{13,9},{2,6},{6,2},{1... | collective-permute-start | bytes 221192 | tf_op jit(solution)/shard_map/ppermute | solution.py:370
  12.6 8.5 %collective-permute-start.4 = (bf16[288,128]{1,0:T(8,128)(2,1)S(1)}, bf16[288,128]{1,0:T(8,128)(2,1)S(1)}, u32[]{:S(2)}, u32[]{:S(2)}) collective-permute-start(bf16[288,128]{1,0:T(8,128)(2,1)S(1)} %get-tuple-element.33), channel_id=1, source_target_pairs={{0,8},{4,12},{8,0},{12,4},{1,9},{5,13},{9,1},{13,5},{2,10},{6,14},... | collective-permute-start | bytes 221192 | tf_op jit(solution)/shard_map/ppermute | solution.py:370
  14.7 8.6 %collective-permute-start.3 = (bf16[288,128]{1,0:T(8,128)(2,1)S(1)}, bf16[288,128]{1,0:T(8,128)(2,1)S(1)}, u32[]{:S(2)}, u32[]{:S(2)}) collective-permute-start(bf16[288,128]{1,0:T(8,128)(2,1)S(1)} %get-tuple-element.32), channel_id=1, source_target_pairs={{0,12},{4,8},{8,4},{12,0},{1,13},{5,9},{9,5},{13,1},{2,14},{6,10},... | collective-permute-start | bytes 221192 | tf_op jit(solution)/shard_map/ppermute | solution.py:370

commit v12 on v11

--- a/solution.py
+++ b/solution.py
@@ -400,7 +400,19 @@
         compiler_params=params,
         name="local_terms",
     )(*passed)
-    sums = [sums] + [exchange(sums, step) for step in range(1, rows)]
+
+    def exchange_sums(step):
+        pairs = [
+            (at * feat_count + lane, partner(at, step, rows) * feat_count + beside(lane))
+            for at in range(rows)
+            for lane in range(feat_count)
+        ]
+        return lax.ppermute(sums, ("rows", "feat"), pairs)
+
+    def beside(lane):
+        return lane ^ 1 if lane ^ 1 < feat_count else lane
+
+    every_sums = [sums] + [exchange_sums(step) for step in range(1, rows)]
     outgoing = pl.pallas_call(
         functools.partial(columns, rows),
         out_shape=[jax.ShapeDtypeStruct((blocks * pad + 4 * blocks, LANES), BF16)] * rows,
@@ -408,7 +420,7 @@
         out_specs=[vmem] * rows,
         compiler_params=params,
         name="columns",
-    )(quant_index, *sums, own, *bins)
+    )(quant_index, *every_sums, own, *bins)
     arrived = [outgoing[0]] + [exchange(outgoing[step], step) for step in range(1, rows)]
 
     targets = rows * feat_count

time: 38.1 us -> 38.6 us (1.013)
  blocking collectives: 10.3 us -> 12 us
  waiting for transfers between devices: 2.77 us -> 1.96 us
    ppermute x6 -> x3, starting transfers between devices: 10.2 us -> 4.44 us  [exchange(): return lax.ppermute(array, 'rows', pairs)]
    ppermute x0 -> x3, starting transfers between devices: none -> 5.48 us  [exchange_sums(): return lax.ppermute(sums, ('rows', 'feat'), pairs)]
    ppermute x6 -> x3, waiting for transfers between devices: 2.77 us -> 0.01 us  [exchange(): return lax.ppermute(array, 'rows', pairs)]
    ppermute x0 -> x3, waiting for transfers between devices: none -> 1.95 us  [exchange_sums(): return lax.ppermute(sums, ('rows', 'feat'), pairs)]
    all_to_all x1, blocking collectives: 10.3 us -> 12 us  [shards(): gathered = lax.all_to_all(best, ('feat', 'rows'), 0, 0, tiled=True)]
where the time goes in v12:
time: 38.6 us; the launch traced here: 38.4 us
  Pallas kernels  13.2 us (34%)
  blocking collectives  12 us (31%)
  starting transfers between devices  9.92 us (26%)
  waiting for transfers between devices  1.96 us (5%)
  between operations  1.37 us (4%)
    all_to_all x1, blocking collectives, shards(): gathered = lax.all_to_all(best, ('feat', 'rows'), 0, 0, tiled=True)  12 us
    pallas_call x4, Pallas kernels, shards(): pl.pallas_call(functools.partial(accumulate, count, feats, first, last),...  8.98 us
    ppermute x3, starting transfers between devices, exchange_sums(): return lax.ppermute(sums, ('rows', 'feat'), pairs)  5.48 us
    ppermute x3, starting transfers between devices, exchange(): return lax.ppermute(array, 'rows', pairs)  4.44 us
    ppermute x3, waiting for transfers between devices, exchange_sums(): return lax.ppermute(sums, ('rows', 'feat'), pairs)  1.95 us
    pallas_call x1, Pallas kernels, shards(): pl.pallas_call(prepare, out_shape=[jax.ShapeDtypeStruct((DAYS, LANES), BF...  1.85 us
    pallas_call x1, Pallas kernels, shards(): pl.pallas_call(results, out_shape=[hist_shape, best_shape], in_specs=[vme...  1.54 us
  transfers between devices with their start and end apart: 6, of which 1 were waited for; matrix products, arithmetic and copies ran while one was open for 0% of the time, Pallas kernels for 18%

profile of v12, /device:TPU:0, one launch (start us, length us, event | category | flops | bytes accessed | tf_op | source)
XLA Modules:
  0.0 38.4 jit_solution(16473277252925802121)
XLA Ops:
  0.6 1.8 %prepare.1 = (bf16[32,128]{1,0:T(8,128)(2,1)S(1)}, bf16[1024,512]{1,0:T(8,128)(2,1)S(1)}, s32[1,1024]{1,0:T(1,128)S(1)}, s32[1,1024]{1,0:T(1,128)S(1)}, s32[1024...) custom-call(bf16[1024,512]{1,0:T(8,128)(2,1)} %refs_0_.1, s32[1,1024]{1,0:T(1,128)} %bitcast.5, s32[1,1024]{1,0:T(1,128)} %bitcast.6, ...), custom_call_target="tpu_custom_call" | custom-call | tf_op jit(solution)/shard_map/prepare/pallas_call | solution.py:372
  2.5 4.6 %collective-permute-start.2 = (bf16[32,128]{1,0:T(8,128)(2,1)S(1)}, bf16[32,128]{1,0:T(8,128)(2,1)S(1)}, u32[]{:S(2)}, u32[]{:S(2)}) collective-permute-start(bf16[32,128]{1,0:T(8,128)(2,1)S(1)} %get-tuple-element.21.refs_0_), channel_id=1, source_target_pairs={{0,13},{1,12},{2,15},{3,14},{4,9},{5,8},{6,11},{7,10},{8,5},{9,4},... | collective-permute-start | bytes 24584 | tf_op jit(solution)/shard_map/ppermute | solution.py:410
  7.0 0.0 collective-permute-start.1
  7.0 0.9 %collective-permute-start = (bf16[32,128]{1,0:T(8,128)(2,1)S(1)}, bf16[32,128]{1,0:T(8,128)(2,1)S(1)}, u32[]{:S(2)}, u32[]{:S(2)}) collective-permute-start(bf16[32,128]{1,0:T(8,128)(2,1)S(1)} %get-tuple-element.21.refs_0_), channel_id=1, source_target_pairs={{0,5},{1,4},{2,7},{3,6},{4,1},{5,0},{6,3},{7,2},{8,13},{9,12},{10,... | collective-permute-start | bytes 24584 | tf_op jit(solution)/shard_map/ppermute | solution.py:410
  8.6 0.5 %local_terms.1 = (f32[32,1024]{1,0:T(8,128)S(1)}, bf16[256,128]{1,0:T(8,128)(2,1)S(1)}, bf16[256,128]{1,0:T(8,128)(2,1)S(1)}, bf16[256,128]{1,0:T(8,128)(2,1)S(1)}, bf16[256,128]{1,0:T(8,128)(2,1)S(1)}) custom-call(bf16[1024,512]{1,0:T(8,128)(2,1)S(1)} %get-tuple-element.22.counts_ref, s32[1,1024]{1,0:T(1,128)S(1)} %get-tuple-element.23.region_ref, ...), custom_call_target="tpu_custom_call" | custom-call | tf_op jit(solution)/shard_map/local_terms/pallas_call | solution.py:393
  9.1 0.0 collective-permute-done.2.refs_3_
  9.1 1.9 %collective-permute-done.1.refs_2_ = bf16[32,128]{1,0:T(8,128)(2,1)S(1)} collective-permute-done((bf16[32,128]{1,0:T(8,128)(2,1)S(1)}, bf16[32,128]{1,0:T(8,128)(2,1)S(1)}, u32[]{:S(2)}, u32[]{:S(2)}) %collective-permute-start.1) | collective-permute-done | bytes 8224 | tf_op jit(solution)/shard_map/ppermute | solution.py:410
  11.1 0.0 collective-permute-done.refs_1_
  11.1 0.3 columns.1
  11.4 0.1 collective-permute-start.5
  11.5 2.4 %collective-permute-start.4 = (bf16[288,128]{1,0:T(8,128)(2,1)S(1)}, bf16[288,128]{1,0:T(8,128)(2,1)S(1)}, u32[]{:S(2)}, u32[]{:S(2)}) collective-permute-start(bf16[288,128]{1,0:T(8,128)(2,1)S(1)} %get-tuple-element.33), channel_id=1, source_target_pairs={{0,8},{4,12},{8,0},{12,4},{1,9},{5,13},{9,1},{13,5},{2,10},{6,14},... | collective-permute-start | bytes 221192 | tf_op jit(solution)/shard_map/ppermute | solution.py:370
  13.9 2.0 %collective-permute-start.3 = (bf16[288,128]{1,0:T(8,128)(2,1)S(1)}, bf16[288,128]{1,0:T(8,128)(2,1)S(1)}, u32[]{:S(2)}, u32[]{:S(2)}) collective-permute-start(bf16[288,128]{1,0:T(8,128)(2,1)S(1)} %get-tuple-element.32), channel_id=1, source_target_pairs={{0,12},{4,8},{8,4},{12,0},{1,13},{5,9},{9,5},{13,1},{2,14},{6,10},... | collective-permute-start | bytes 221192 | tf_op jit(solution)/shard_map/ppermute | solution.py:370
  15.9 2.0 %accumulate_0.1.refs_1_ = f32[32,64,256]{2,1,0:T(8,128)S(1)} custom-call(bf16[288,128]{1,0:T(8,128)(2,1)S(1)} %get-tuple-element.35.refs_0_), custom_call_target="tpu_custom_call" | custom-call | tf_op jit(solution)/shard_map/accumulate_0/pallas_call | solution.py:445
  17.9 0.0 collective-permute-done.5.refs_0_
  17.9 2.1 %accumulate_1.1.refs_1_ = f32[32,64,256]{2,1,0:T(8,128)S(1)} custom-call(bf16[288,128]{1,0:T(8,128)(2,1)S(1)} %collective-permute-done.5.refs_0_, f32[32,64,256]{2,1,0:T(8,128)S(1)} %accumulate_0.1.refs_1_), custom_call_target="tpu_custom_call", output_to_operand_aliasing={{}: (1, {})} | custom-call | tf_op jit(solution)/shard_map/accumulate_1/pallas_call | solution.py:445
  20.0 0.0 collective-permute-done.4.refs_0_
  20.0 2.1 %accumulate_2.1.refs_1_ = f32[32,64,256]{2,1,0:T(8,128)S(1)} custom-call(bf16[288,128]{1,0:T(8,128)(2,1)S(1)} %collective-permute-done.4.refs_0_, f32[32,64,256]{2,1,0:T(8,128)S(1)} %accumulate_1.1.refs_1_), custom_call_target="tpu_custom_call", output_to_operand_aliasing={{}: (1, {})} | custom-call | tf_op jit(solution)/shard_map/accumulate_2/pallas_call | solution.py:445
  22.2 0.0 collective-permute-done.3.refs_0_
  22.2 2.7 %accumulate_3.1 = (f32[32,64,256]{2,1,0:T(8,128)S(1)}, f32[16,8,128]{2,1,0:T(8,128)S(1)}) custom-call(bf16[288,128]{1,0:T(8,128)(2,1)S(1)} %collective-permute-done.3.refs_0_, f32[32,64,256]{2,1,0:T(8,128)S(1)} %accumulate_2.1.refs_1_), custom_call_target="tpu_custom_call", output_to_operand_aliasing={{0}: (1, {})} | custom-call | tf_op jit(solution)/shard_map/accumulate_3/pallas_call | solution.py:445
  24.9 12.0 %all_to_all.5.packed_ref = f32[16,8,128]{2,1,0:T(8,128)S(1)} all-to-all(f32[16,8,128]{2,1,0:T(8,128)S(1)} %get-tuple-element.37), channel_id=1, replica_groups=mesh['groups'=2,'rows'=4,'feat'=4] {'feat','rows'}, dimensions={0} | all-to-all | bytes 131072 | tf_op jit(solution)/shard_map/all_to_all | solution.py:457
  36.9 1.5 %results.1 = (f32[32,64,256]{2,1,0:T(8,128)}, f32[16,32,32]{2,1,0:T(8,128)}) custom-call(f32[32,64,256]{2,1,0:T(8,128)S(1)} %get-tuple-element.36.left_ref, f32[16,8,128]{2,1,0:T(8,128)S(1)} %all_to_all.5.packed_ref), custom_call_target="tpu_custom_call" | custom-call | tf_op jit(solution)/shard_map/results/pallas_call | solution.py:459
Async XLA Ops:
  2.5 6.6 %collective-permute-start.2 = (bf16[32,128]{1,0:T(8,128)(2,1)S(1)}, bf16[32,128]{1,0:T(8,128)(2,1)S(1)}, u32[]{:S(2)}, u32[]{:S(2)}) collective-permute-start(bf16[32,128]{1,0:T(8,128)(2,1)S(1)} %get-tuple-element.21.refs_0_), channel_id=1, source_target_pairs={{0,13},{1,12},{2,15},{3,14},{4,9},{5,8},{6,11},{7,10},{8,5},{9,4},... | collective-permute-start | bytes 24584 | tf_op jit(solution)/shard_map/ppermute | solution.py:410
  7.0 4.0 %collective-permute-start.1 = (bf16[32,128]{1,0:T(8,128)(2,1)S(1)}, bf16[32,128]{1,0:T(8,128)(2,1)S(1)}, u32[]{:S(2)}, u32[]{:S(2)}) collective-permute-start(bf16[32,128]{1,0:T(8,128)(2,1)S(1)} %get-tuple-element.21.refs_0_), channel_id=1, source_target_pairs={{0,9},{1,8},{2,11},{3,10},{4,13},{5,12},{6,15},{7,14},{8,1},{9,0},... | collective-permute-start | bytes 24584 | tf_op jit(solution)/shard_map/ppermute | solution.py:410
  7.0 4.0 %collective-permute-start = (bf16[32,128]{1,0:T(8,128)(2,1)S(1)}, bf16[32,128]{1,0:T(8,128)(2,1)S(1)}, u32[]{:S(2)}, u32[]{:S(2)}) collective-permute-start(bf16[32,128]{1,0:T(8,128)(2,1)S(1)} %get-tuple-element.21.refs_0_), channel_id=1, source_target_pairs={{0,5},{1,4},{2,7},{3,6},{4,1},{5,0},{6,3},{7,2},{8,13},{9,12},{10,... | collective-permute-start | bytes 24584 | tf_op jit(solution)/shard_map/ppermute | solution.py:410
  11.4 6.5 %collective-permute-start.5 = (bf16[288,128]{1,0:T(8,128)(2,1)S(1)}, bf16[288,128]{1,0:T(8,128)(2,1)S(1)}, u32[]{:S(2)}, u32[]{:S(2)}) collective-permute-start(bf16[288,128]{1,0:T(8,128)(2,1)S(1)} %get-tuple-element.34), channel_id=1, source_target_pairs={{0,4},{4,0},{8,12},{12,8},{1,5},{5,1},{9,13},{13,9},{2,6},{6,2},{1... | collective-permute-start | bytes 221192 | tf_op jit(solution)/shard_map/ppermute | solution.py:370
  11.5 8.5 %collective-permute-start.4 = (bf16[288,128]{1,0:T(8,128)(2,1)S(1)}, bf16[288,128]{1,0:T(8,128)(2,1)S(1)}, u32[]{:S(2)}, u32[]{:S(2)}) collective-permute-start(bf16[288,128]{1,0:T(8,128)(2,1)S(1)} %get-tuple-element.33), channel_id=1, source_target_pairs={{0,8},{4,12},{8,0},{12,4},{1,9},{5,13},{9,1},{13,5},{2,10},{6,14},... | collective-permute-start | bytes 221192 | tf_op jit(solution)/shard_map/ppermute | solution.py:370
  13.9 8.3 %collective-permute-start.3 = (bf16[288,128]{1,0:T(8,128)(2,1)S(1)}, bf16[288,128]{1,0:T(8,128)(2,1)S(1)}, u32[]{:S(2)}, u32[]{:S(2)}) collective-permute-start(bf16[288,128]{1,0:T(8,128)(2,1)S(1)} %get-tuple-element.32), channel_id=1, source_target_pairs={{0,12},{4,8},{8,4},{12,0},{1,13},{5,9},{9,5},{13,1},{2,14},{6,10},... | collective-permute-start | bytes 221192 | tf_op jit(solution)/shard_map/ppermute | solution.py:370

commit v13 on v12

--- a/solution.py
+++ b/solution.py
@@ -421,7 +421,8 @@
         compiler_params=params,
         name="columns",
     )(quant_index, *every_sums, own, *bins)
-    arrived = [outgoing[0]] + [exchange(outgoing[step], step) for step in range(1, rows)]
+    order = [2, 1, *range(3, rows)] if rows > 2 else [*range(1, rows)]
+    arrived = [outgoing[0]] + [exchange(outgoing[step], step) for step in order]
 
     targets = rows * feat_count
     packed_rows = feats * NODES // LANES

time: 38.6 us -> 37.7 us (0.977)
  blocking collectives: 12 us -> 10.2 us
  waiting for transfers between devices: 1.96 us -> 2.86 us
    all_to_all x1, blocking collectives: 12 us -> 10.2 us  [shards(): gathered = lax.all_to_all(best, ('feat', 'rows'), 0, 0, tiled=True)]
    ppermute x3, waiting for transfers between devices: 0.01 us -> 0.9 us  [exchange(): return lax.ppermute(array, 'rows', pairs)]
  transfers between devices with their start and end apart: 6 -> 6, of which waited for: 1 -> 3; matrix products, arithmetic and copies ran while one was open for 0% -> 0% of each run, Pallas kernels for 18% -> 18%
where the time goes in v13:
time: 37.7 us; the launch traced here: 37.5 us
  Pallas kernels  13.2 us (35%)
  blocking collectives  10.2 us (27%)
  starting transfers between devices  9.93 us (26%)
  waiting for transfers between devices  2.86 us (8%)
  between operations  1.35 us (4%)
    all_to_all x1, blocking collectives, shards(): gathered = lax.all_to_all(best, ('feat', 'rows'), 0, 0, tiled=True)  10.2 us
    pallas_call x4, Pallas kernels, shards(): pl.pallas_call(functools.partial(accumulate, count, feats, first, last),...  8.98 us
    ppermute x3, starting transfers between devices, exchange_sums(): return lax.ppermute(sums, ('rows', 'feat'), pairs)  5.48 us
    ppermute x3, starting transfers between devices, exchange(): return lax.ppermute(array, 'rows', pairs)  4.45 us
    ppermute x3, waiting for transfers between devices, exchange_sums(): return lax.ppermute(sums, ('rows', 'feat'), pairs)  1.95 us
    pallas_call x1, Pallas kernels, shards(): pl.pallas_call(prepare, out_shape=[jax.ShapeDtypeStruct((DAYS, LANES), BF...  1.85 us
    pallas_call x1, Pallas kernels, shards(): pl.pallas_call(results, out_shape=[hist_shape, best_shape], in_specs=[vme...  1.54 us
    ppermute x3, waiting for transfers between devices, exchange(): return lax.ppermute(array, 'rows', pairs)  0.9 us
  transfers between devices with their start and end apart: 6, of which 3 were waited for; matrix products, arithmetic and copies ran while one was open for 0% of the time, Pallas kernels for 18%

profile of v13, /device:TPU:0, one launch (start us, length us, event | category | flops | bytes accessed | tf_op | source)
XLA Modules:
  0.0 37.5 jit_solution(8092686718928337015)
XLA Ops:
  0.6 1.8 %prepare.1 = (bf16[32,128]{1,0:T(8,128)(2,1)S(1)}, bf16[1024,512]{1,0:T(8,128)(2,1)S(1)}, s32[1,1024]{1,0:T(1,128)S(1)}, s32[1,1024]{1,0:T(1,128)S(1)}, s32[1024...) custom-call(bf16[1024,512]{1,0:T(8,128)(2,1)} %refs_0_.1, s32[1,1024]{1,0:T(1,128)} %bitcast.5, s32[1,1024]{1,0:T(1,128)} %bitcast.6, ...), custom_call_target="tpu_custom_call" | custom-call | tf_op jit(solution)/shard_map/prepare/pallas_call | solution.py:372
  2.5 4.6 %collective-permute-start.2 = (bf16[32,128]{1,0:T(8,128)(2,1)S(1)}, bf16[32,128]{1,0:T(8,128)(2,1)S(1)}, u32[]{:S(2)}, u32[]{:S(2)}) collective-permute-start(bf16[32,128]{1,0:T(8,128)(2,1)S(1)} %get-tuple-element.21.refs_0_), channel_id=1, source_target_pairs={{0,13},{1,12},{2,15},{3,14},{4,9},{5,8},{6,11},{7,10},{8,5},{9,4},... | collective-permute-start | bytes 24584 | tf_op jit(solution)/shard_map/ppermute | solution.py:410
  7.0 0.0 collective-permute-start.1
  7.0 0.9 %collective-permute-start = (bf16[32,128]{1,0:T(8,128)(2,1)S(1)}, bf16[32,128]{1,0:T(8,128)(2,1)S(1)}, u32[]{:S(2)}, u32[]{:S(2)}) collective-permute-start(bf16[32,128]{1,0:T(8,128)(2,1)S(1)} %get-tuple-element.21.refs_0_), channel_id=1, source_target_pairs={{0,5},{1,4},{2,7},{3,6},{4,1},{5,0},{6,3},{7,2},{8,13},{9,12},{10,... | collective-permute-start | bytes 24584 | tf_op jit(solution)/shard_map/ppermute | solution.py:410
  8.6 0.5 %local_terms.1 = (f32[32,1024]{1,0:T(8,128)S(1)}, bf16[256,128]{1,0:T(8,128)(2,1)S(1)}, bf16[256,128]{1,0:T(8,128)(2,1)S(1)}, bf16[256,128]{1,0:T(8,128)(2,1)S(1)}, bf16[256,128]{1,0:T(8,128)(2,1)S(1)}) custom-call(bf16[1024,512]{1,0:T(8,128)(2,1)S(1)} %get-tuple-element.22.counts_ref, s32[1,1024]{1,0:T(1,128)S(1)} %get-tuple-element.23.region_ref, ...), custom_call_target="tpu_custom_call" | custom-call | tf_op jit(solution)/shard_map/local_terms/pallas_call | solution.py:393
  9.1 0.0 collective-permute-done.2.refs_3_
  9.1 1.9 %collective-permute-done.1.refs_2_ = bf16[32,128]{1,0:T(8,128)(2,1)S(1)} collective-permute-done((bf16[32,128]{1,0:T(8,128)(2,1)S(1)}, bf16[32,128]{1,0:T(8,128)(2,1)S(1)}, u32[]{:S(2)}, u32[]{:S(2)}) %collective-permute-start.1) | collective-permute-done | bytes 8224 | tf_op jit(solution)/shard_map/ppermute | solution.py:410
  11.1 0.0 collective-permute-done.refs_1_
  11.1 0.3 columns.1
  11.4 2.4 %collective-permute-start.5 = (bf16[288,128]{1,0:T(8,128)(2,1)S(1)}, bf16[288,128]{1,0:T(8,128)(2,1)S(1)}, u32[]{:S(2)}, u32[]{:S(2)}) collective-permute-start(bf16[288,128]{1,0:T(8,128)(2,1)S(1)} %get-tuple-element.34), channel_id=1, source_target_pairs={{0,8},{4,12},{8,0},{12,4},{1,9},{5,13},{9,1},{13,5},{2,10},{6,14},... | collective-permute-start | bytes 221192 | tf_op jit(solution)/shard_map/ppermute | solution.py:370
  13.8 0.0 collective-permute-start.4
  13.8 2.1 %collective-permute-start.3 = (bf16[288,128]{1,0:T(8,128)(2,1)S(1)}, bf16[288,128]{1,0:T(8,128)(2,1)S(1)}, u32[]{:S(2)}, u32[]{:S(2)}) collective-permute-start(bf16[288,128]{1,0:T(8,128)(2,1)S(1)} %get-tuple-element.32), channel_id=1, source_target_pairs={{0,12},{4,8},{8,4},{12,0},{1,13},{5,9},{9,5},{13,1},{2,14},{6,10},... | collective-permute-start | bytes 221192 | tf_op jit(solution)/shard_map/ppermute | solution.py:370
  15.9 2.0 %accumulate_0.1.refs_1_ = f32[32,64,256]{2,1,0:T(8,128)S(1)} custom-call(bf16[288,128]{1,0:T(8,128)(2,1)S(1)} %get-tuple-element.35.refs_0_), custom_call_target="tpu_custom_call" | custom-call | tf_op jit(solution)/shard_map/accumulate_0/pallas_call | solution.py:446
  17.9 0.2 collective-permute-done.5.refs_0_
  18.1 2.1 %accumulate_1.1.refs_1_ = f32[32,64,256]{2,1,0:T(8,128)S(1)} custom-call(bf16[288,128]{1,0:T(8,128)(2,1)S(1)} %collective-permute-done.5.refs_0_, f32[32,64,256]{2,1,0:T(8,128)S(1)} %accumulate_0.1.refs_1_), custom_call_target="tpu_custom_call", output_to_operand_aliasing={{}: (1, {})} | custom-call | tf_op jit(solution)/shard_map/accumulate_1/pallas_call | solution.py:446
  20.2 0.7 %collective-permute-done.4.refs_0_ = bf16[288,128]{1,0:T(8,128)(2,1)S(1)} collective-permute-done((bf16[288,128]{1,0:T(8,128)(2,1)S(1)}, bf16[288,128]{1,0:T(8,128)(2,1)S(1)}, u32[]{:S(2)}, u32[]{:S(2)}) %collective-permute-start.4) | collective-permute-done | bytes 73760 | tf_op jit(solution)/shard_map/ppermute | solution.py:370
  20.9 2.1 %accumulate_2.1.refs_1_ = f32[32,64,256]{2,1,0:T(8,128)S(1)} custom-call(bf16[288,128]{1,0:T(8,128)(2,1)S(1)} %collective-permute-done.4.refs_0_, f32[32,64,256]{2,1,0:T(8,128)S(1)} %accumulate_1.1.refs_1_), custom_call_target="tpu_custom_call", output_to_operand_aliasing={{}: (1, {})} | custom-call | tf_op jit(solution)/shard_map/accumulate_2/pallas_call | solution.py:446
  23.0 0.0 collective-permute-done.3.refs_0_
  23.0 2.7 %accumulate_3.1 = (f32[32,64,256]{2,1,0:T(8,128)S(1)}, f32[16,8,128]{2,1,0:T(8,128)S(1)}) custom-call(bf16[288,128]{1,0:T(8,128)(2,1)S(1)} %collective-permute-done.3.refs_0_, f32[32,64,256]{2,1,0:T(8,128)S(1)} %accumulate_2.1.refs_1_), custom_call_target="tpu_custom_call", output_to_operand_aliasing={{0}: (1, {})} | custom-call | tf_op jit(solution)/shard_map/accumulate_3/pallas_call | solution.py:446
  25.8 10.2 %all_to_all.5.packed_ref = f32[16,8,128]{2,1,0:T(8,128)S(1)} all-to-all(f32[16,8,128]{2,1,0:T(8,128)S(1)} %get-tuple-element.37), channel_id=1, replica_groups=mesh['groups'=2,'rows'=4,'feat'=4] {'feat','rows'}, dimensions={0} | all-to-all | bytes 131072 | tf_op jit(solution)/shard_map/all_to_all | solution.py:458
  35.9 1.5 %results.1 = (f32[32,64,256]{2,1,0:T(8,128)}, f32[16,32,32]{2,1,0:T(8,128)}) custom-call(f32[32,64,256]{2,1,0:T(8,128)S(1)} %get-tuple-element.36.left_ref, f32[16,8,128]{2,1,0:T(8,128)S(1)} %all_to_all.5.packed_ref), custom_call_target="tpu_custom_call" | custom-call | tf_op jit(solution)/shard_map/results/pallas_call | solution.py:460
Async XLA Ops:
  2.5 6.6 %collective-permute-start.2 = (bf16[32,128]{1,0:T(8,128)(2,1)S(1)}, bf16[32,128]{1,0:T(8,128)(2,1)S(1)}, u32[]{:S(2)}, u32[]{:S(2)}) collective-permute-start(bf16[32,128]{1,0:T(8,128)(2,1)S(1)} %get-tuple-element.21.refs_0_), channel_id=1, source_target_pairs={{0,13},{1,12},{2,15},{3,14},{4,9},{5,8},{6,11},{7,10},{8,5},{9,4},... | collective-permute-start | bytes 24584 | tf_op jit(solution)/shard_map/ppermute | solution.py:410
  7.0 4.0 %collective-permute-start.1 = (bf16[32,128]{1,0:T(8,128)(2,1)S(1)}, bf16[32,128]{1,0:T(8,128)(2,1)S(1)}, u32[]{:S(2)}, u32[]{:S(2)}) collective-permute-start(bf16[32,128]{1,0:T(8,128)(2,1)S(1)} %get-tuple-element.21.refs_0_), channel_id=1, source_target_pairs={{0,9},{1,8},{2,11},{3,10},{4,13},{5,12},{6,15},{7,14},{8,1},{9,0},... | collective-permute-start | bytes 24584 | tf_op jit(solution)/shard_map/ppermute | solution.py:410
  7.0 4.0 %collective-permute-start = (bf16[32,128]{1,0:T(8,128)(2,1)S(1)}, bf16[32,128]{1,0:T(8,128)(2,1)S(1)}, u32[]{:S(2)}, u32[]{:S(2)}) collective-permute-start(bf16[32,128]{1,0:T(8,128)(2,1)S(1)} %get-tuple-element.21.refs_0_), channel_id=1, source_target_pairs={{0,5},{1,4},{2,7},{3,6},{4,1},{5,0},{6,3},{7,2},{8,13},{9,12},{10,... | collective-permute-start | bytes 24584 | tf_op jit(solution)/shard_map/ppermute | solution.py:410
  11.4 6.6 %collective-permute-start.5 = (bf16[288,128]{1,0:T(8,128)(2,1)S(1)}, bf16[288,128]{1,0:T(8,128)(2,1)S(1)}, u32[]{:S(2)}, u32[]{:S(2)}) collective-permute-start(bf16[288,128]{1,0:T(8,128)(2,1)S(1)} %get-tuple-element.34), channel_id=1, source_target_pairs={{0,8},{4,12},{8,0},{12,4},{1,9},{5,13},{9,1},{13,5},{2,10},{6,14},... | collective-permute-start | bytes 221192 | tf_op jit(solution)/shard_map/ppermute | solution.py:370
  13.8 7.1 %collective-permute-start.4 = (bf16[288,128]{1,0:T(8,128)(2,1)S(1)}, bf16[288,128]{1,0:T(8,128)(2,1)S(1)}, u32[]{:S(2)}, u32[]{:S(2)}) collective-permute-start(bf16[288,128]{1,0:T(8,128)(2,1)S(1)} %get-tuple-element.33), channel_id=1, source_target_pairs={{0,4},{4,0},{8,12},{12,8},{1,5},{5,1},{9,13},{13,9},{2,6},{6,2},{1... | collective-permute-start | bytes 221192 | tf_op jit(solution)/shard_map/ppermute | solution.py:370
  13.8 9.2 %collective-permute-start.3 = (bf16[288,128]{1,0:T(8,128)(2,1)S(1)}, bf16[288,128]{1,0:T(8,128)(2,1)S(1)}, u32[]{:S(2)}, u32[]{:S(2)}) collective-permute-start(bf16[288,128]{1,0:T(8,128)(2,1)S(1)} %get-tuple-element.32), channel_id=1, source_target_pairs={{0,12},{4,8},{8,4},{12,0},{1,13},{5,9},{9,5},{13,1},{2,14},{6,10},... | collective-permute-start | bytes 221192 | tf_op jit(solution)/shard_map/ppermute | solution.py:370

commit v14 on v13

--- a/solution.py
+++ b/solution.py
@@ -402,8 +402,9 @@
     )(*passed)
 
     def exchange_sums(step):
+        to = beside if step < 3 else int
         pairs = [
-            (at * feat_count + lane, partner(at, step, rows) * feat_count + beside(lane))
+            (at * feat_count + lane, partner(at, step, rows) * feat_count + to(lane))
             for at in range(rows)
             for lane in range(feat_count)
         ]

time: 37.7 us -> 38.1 us (1.011)
    ppermute x3, waiting for transfers between devices: 1.95 us -> 2.48 us  [exchange_sums(): return lax.ppermute(sums, ('rows', 'feat'), pairs)]
where the time goes in v14:
time: 38.1 us; the launch traced here: 37.9 us
  Pallas kernels  13.2 us (35%)
  blocking collectives  10.5 us (28%)
  starting transfers between devices  9.93 us (26%)
  waiting for transfers between devices  3 us (8%)
  between operations  1.35 us (4%)
    all_to_all x1, blocking collectives, shards(): gathered = lax.all_to_all(best, ('feat', 'rows'), 0, 0, tiled=True)  10.5 us
    pallas_call x4, Pallas kernels, shards(): pl.pallas_call(functools.partial(accumulate, count, feats, first, last),...  8.98 us
    ppermute x3, starting transfers between devices, exchange_sums(): return lax.ppermute(sums, ('rows', 'feat'), pairs)  5.48 us
    ppermute x3, starting transfers between devices, exchange(): return lax.ppermute(array, 'rows', pairs)  4.45 us
    ppermute x3, waiting for transfers between devices, exchange_sums(): return lax.ppermute(sums, ('rows', 'feat'), pairs)  2.48 us
    pallas_call x1, Pallas kernels, shards(): pl.pallas_call(prepare, out_shape=[jax.ShapeDtypeStruct((DAYS, LANES), BF...  1.85 us
    pallas_call x1, Pallas kernels, shards(): pl.pallas_call(results, out_shape=[hist_shape, best_shape], in_specs=[vme...  1.54 us
  transfers between devices with their start and end apart: 6, of which 3 were waited for; matrix products, arithmetic and copies ran while one was open for 0% of the time, Pallas kernels for 18%

profile of v14, /device:TPU:0, one launch (start us, length us, event | category | flops | bytes accessed | tf_op | source)
XLA Modules:
  0.0 37.9 jit_solution(11647070830950237763)
XLA Ops:
  0.6 1.8 %prepare.1 = (bf16[32,128]{1,0:T(8,128)(2,1)S(1)}, bf16[1024,512]{1,0:T(8,128)(2,1)S(1)}, s32[1,1024]{1,0:T(1,128)S(1)}, s32[1,1024]{1,0:T(1,128)S(1)}, s32[1024...) custom-call(bf16[1024,512]{1,0:T(8,128)(2,1)} %refs_0_.1, s32[1,1024]{1,0:T(1,128)} %bitcast.5, s32[1,1024]{1,0:T(1,128)} %bitcast.6, ...), custom_call_target="tpu_custom_call" | custom-call | tf_op jit(solution)/shard_map/prepare/pallas_call | solution.py:372
  2.5 5.1 %collective-permute-start.2 = (bf16[32,128]{1,0:T(8,128)(2,1)S(1)}, bf16[32,128]{1,0:T(8,128)(2,1)S(1)}, u32[]{:S(2)}, u32[]{:S(2)}) collective-permute-start(bf16[32,128]{1,0:T(8,128)(2,1)S(1)} %get-tuple-element.21.refs_0_), channel_id=1, source_target_pairs={{0,12},{1,13},{2,14},{3,15},{4,8},{5,9},{6,10},{7,11},{8,4},{9,5},... | collective-permute-start | bytes 24584 | tf_op jit(solution)/shard_map/ppermute | solution.py:411
  7.6 0.0 collective-permute-start.1
  7.6 0.4 collective-permute-start
  8.6 0.5 %local_terms.1 = (f32[32,1024]{1,0:T(8,128)S(1)}, bf16[256,128]{1,0:T(8,128)(2,1)S(1)}, bf16[256,128]{1,0:T(8,128)(2,1)S(1)}, bf16[256,128]{1,0:T(8,128)(2,1)S(1)}, bf16[256,128]{1,0:T(8,128)(2,1)S(1)}) custom-call(bf16[1024,512]{1,0:T(8,128)(2,1)S(1)} %get-tuple-element.22.counts_ref, s32[1,1024]{1,0:T(1,128)S(1)} %get-tuple-element.23.region_ref, ...), custom_call_target="tpu_custom_call" | custom-call | tf_op jit(solution)/shard_map/local_terms/pallas_call | solution.py:393
  9.1 0.1 collective-permute-done.2.refs_3_
  9.2 2.3 %collective-permute-done.1.refs_2_ = bf16[32,128]{1,0:T(8,128)(2,1)S(1)} collective-permute-done((bf16[32,128]{1,0:T(8,128)(2,1)S(1)}, bf16[32,128]{1,0:T(8,128)(2,1)S(1)}, u32[]{:S(2)}, u32[]{:S(2)}) %collective-permute-start.1) | collective-permute-done | bytes 8224 | tf_op jit(solution)/shard_map/ppermute | solution.py:411
  11.6 0.0 collective-permute-done.refs_1_
  11.6 0.3 columns.1
  11.9 1.2 %collective-permute-start.5 = (bf16[288,128]{1,0:T(8,128)(2,1)S(1)}, bf16[288,128]{1,0:T(8,128)(2,1)S(1)}, u32[]{:S(2)}, u32[]{:S(2)}) collective-permute-start(bf16[288,128]{1,0:T(8,128)(2,1)S(1)} %get-tuple-element.34), channel_id=1, source_target_pairs={{0,8},{4,12},{8,0},{12,4},{1,9},{5,13},{9,1},{13,5},{2,10},{6,14},... | collective-permute-start | bytes 221192 | tf_op jit(solution)/shard_map/ppermute | solution.py:370
  13.2 0.9 %collective-permute-start.4 = (bf16[288,128]{1,0:T(8,128)(2,1)S(1)}, bf16[288,128]{1,0:T(8,128)(2,1)S(1)}, u32[]{:S(2)}, u32[]{:S(2)}) collective-permute-start(bf16[288,128]{1,0:T(8,128)(2,1)S(1)} %get-tuple-element.33), channel_id=1, source_target_pairs={{0,4},{4,0},{8,12},{12,8},{1,5},{5,1},{9,13},{13,9},{2,6},{6,2},{1... | collective-permute-start | bytes 221192 | tf_op jit(solution)/shard_map/ppermute | solution.py:370
  14.1 2.3 %collective-permute-start.3 = (bf16[288,128]{1,0:T(8,128)(2,1)S(1)}, bf16[288,128]{1,0:T(8,128)(2,1)S(1)}, u32[]{:S(2)}, u32[]{:S(2)}) collective-permute-start(bf16[288,128]{1,0:T(8,128)(2,1)S(1)} %get-tuple-element.32), channel_id=1, source_target_pairs={{0,12},{4,8},{8,4},{12,0},{1,13},{5,9},{9,5},{13,1},{2,14},{6,10},... | collective-permute-start | bytes 221192 | tf_op jit(solution)/shard_map/ppermute | solution.py:370
  16.4 2.0 %accumulate_0.1.refs_1_ = f32[32,64,256]{2,1,0:T(8,128)S(1)} custom-call(bf16[288,128]{1,0:T(8,128)(2,1)S(1)} %get-tuple-element.35.refs_0_), custom_call_target="tpu_custom_call" | custom-call | tf_op jit(solution)/shard_map/accumulate_0/pallas_call | solution.py:447
  18.4 0.0 collective-permute-done.5.refs_0_
  18.4 2.1 %accumulate_1.1.refs_1_ = f32[32,64,256]{2,1,0:T(8,128)S(1)} custom-call(bf16[288,128]{1,0:T(8,128)(2,1)S(1)} %collective-permute-done.5.refs_0_, f32[32,64,256]{2,1,0:T(8,128)S(1)} %accumulate_0.1.refs_1_), custom_call_target="tpu_custom_call", output_to_operand_aliasing={{}: (1, {})} | custom-call | tf_op jit(solution)/shard_map/accumulate_1/pallas_call | solution.py:447
  20.5 0.5 %collective-permute-done.4.refs_0_ = bf16[288,128]{1,0:T(8,128)(2,1)S(1)} collective-permute-done((bf16[288,128]{1,0:T(8,128)(2,1)S(1)}, bf16[288,128]{1,0:T(8,128)(2,1)S(1)}, u32[]{:S(2)}, u32[]{:S(2)}) %collective-permute-start.4) | collective-permute-done | bytes 73760 | tf_op jit(solution)/shard_map/ppermute | solution.py:370
  21.1 2.1 %accumulate_2.1.refs_1_ = f32[32,64,256]{2,1,0:T(8,128)S(1)} custom-call(bf16[288,128]{1,0:T(8,128)(2,1)S(1)} %collective-permute-done.4.refs_0_, f32[32,64,256]{2,1,0:T(8,128)S(1)} %accumulate_1.1.refs_1_), custom_call_target="tpu_custom_call", output_to_operand_aliasing={{}: (1, {})} | custom-call | tf_op jit(solution)/shard_map/accumulate_2/pallas_call | solution.py:447
  23.2 0.0 collective-permute-done.3.refs_0_
  23.2 2.7 %accumulate_3.1 = (f32[32,64,256]{2,1,0:T(8,128)S(1)}, f32[16,8,128]{2,1,0:T(8,128)S(1)}) custom-call(bf16[288,128]{1,0:T(8,128)(2,1)S(1)} %collective-permute-done.3.refs_0_, f32[32,64,256]{2,1,0:T(8,128)S(1)} %accumulate_2.1.refs_1_), custom_call_target="tpu_custom_call", output_to_operand_aliasing={{0}: (1, {})} | custom-call | tf_op jit(solution)/shard_map/accumulate_3/pallas_call | solution.py:447
  25.9 10.5 %all_to_all.5.packed_ref = f32[16,8,128]{2,1,0:T(8,128)S(1)} all-to-all(f32[16,8,128]{2,1,0:T(8,128)S(1)} %get-tuple-element.37), channel_id=1, replica_groups=mesh['groups'=2,'rows'=4,'feat'=4] {'feat','rows'}, dimensions={0} | all-to-all | bytes 131072 | tf_op jit(solution)/shard_map/all_to_all | solution.py:459
  36.4 1.5 %results.1 = (f32[32,64,256]{2,1,0:T(8,128)}, f32[16,32,32]{2,1,0:T(8,128)}) custom-call(f32[32,64,256]{2,1,0:T(8,128)S(1)} %get-tuple-element.36.left_ref, f32[16,8,128]{2,1,0:T(8,128)S(1)} %all_to_all.5.packed_ref), custom_call_target="tpu_custom_call" | custom-call | tf_op jit(solution)/shard_map/results/pallas_call | solution.py:461
Async XLA Ops:
  2.5 6.7 %collective-permute-start.2 = (bf16[32,128]{1,0:T(8,128)(2,1)S(1)}, bf16[32,128]{1,0:T(8,128)(2,1)S(1)}, u32[]{:S(2)}, u32[]{:S(2)}) collective-permute-start(bf16[32,128]{1,0:T(8,128)(2,1)S(1)} %get-tuple-element.21.refs_0_), channel_id=1, source_target_pairs={{0,12},{1,13},{2,14},{3,15},{4,8},{5,9},{6,10},{7,11},{8,4},{9,5},... | collective-permute-start | bytes 24584 | tf_op jit(solution)/shard_map/ppermute | solution.py:411
  7.6 4.0 %collective-permute-start.1 = (bf16[32,128]{1,0:T(8,128)(2,1)S(1)}, bf16[32,128]{1,0:T(8,128)(2,1)S(1)}, u32[]{:S(2)}, u32[]{:S(2)}) collective-permute-start(bf16[32,128]{1,0:T(8,128)(2,1)S(1)} %get-tuple-element.21.refs_0_), channel_id=1, source_target_pairs={{0,9},{1,8},{2,11},{3,10},{4,13},{5,12},{6,15},{7,14},{8,1},{9,0},... | collective-permute-start | bytes 24584 | tf_op jit(solution)/shard_map/ppermute | solution.py:411
  7.6 4.0 %collective-permute-start = (bf16[32,128]{1,0:T(8,128)(2,1)S(1)}, bf16[32,128]{1,0:T(8,128)(2,1)S(1)}, u32[]{:S(2)}, u32[]{:S(2)}) collective-permute-start(bf16[32,128]{1,0:T(8,128)(2,1)S(1)} %get-tuple-element.21.refs_0_), channel_id=1, source_target_pairs={{0,5},{1,4},{2,7},{3,6},{4,1},{5,0},{6,3},{7,2},{8,13},{9,12},{10,... | collective-permute-start | bytes 24584 | tf_op jit(solution)/shard_map/ppermute | solution.py:411
  11.9 6.5 %collective-permute-start.5 = (bf16[288,128]{1,0:T(8,128)(2,1)S(1)}, bf16[288,128]{1,0:T(8,128)(2,1)S(1)}, u32[]{:S(2)}, u32[]{:S(2)}) collective-permute-start(bf16[288,128]{1,0:T(8,128)(2,1)S(1)} %get-tuple-element.34), channel_id=1, source_target_pairs={{0,8},{4,12},{8,0},{12,4},{1,9},{5,13},{9,1},{13,5},{2,10},{6,14},... | collective-permute-start | bytes 221192 | tf_op jit(solution)/shard_map/ppermute | solution.py:370
  13.2 7.9 %collective-permute-start.4 = (bf16[288,128]{1,0:T(8,128)(2,1)S(1)}, bf16[288,128]{1,0:T(8,128)(2,1)S(1)}, u32[]{:S(2)}, u32[]{:S(2)}) collective-permute-start(bf16[288,128]{1,0:T(8,128)(2,1)S(1)} %get-tuple-element.33), channel_id=1, source_target_pairs={{0,4},{4,0},{8,12},{12,8},{1,5},{5,1},{9,13},{13,9},{2,6},{6,2},{1... | collective-permute-start | bytes 221192 | tf_op jit(solution)/shard_map/ppermute | solution.py:370
  14.1 9.1 %collective-permute-start.3 = (bf16[288,128]{1,0:T(8,128)(2,1)S(1)}, bf16[288,128]{1,0:T(8,128)(2,1)S(1)}, u32[]{:S(2)}, u32[]{:S(2)}) collective-permute-start(bf16[288,128]{1,0:T(8,128)(2,1)S(1)} %get-tuple-element.32), channel_id=1, source_target_pairs={{0,12},{4,8},{8,4},{12,0},{1,13},{5,9},{9,5},{13,1},{2,14},{6,10},... | collective-permute-start | bytes 221192 | tf_op jit(solution)/shard_map/ppermute | solution.py:370

commit v15 on v13

--- a/solution.py
+++ b/solution.py
@@ -337,7 +337,9 @@
         pltpu.make_async_copy(hist_held.at[here], hist_ref.at[here], sems.at[0]).start()
         return carry
 
-    for step in range(feats // group):
+    steps = feats // group
+    early = -(-steps // 4)
+    for step in range(early):
         one_group(step, 0)
     for target in range(targets):
         packed = packed_ref[target]
@@ -347,6 +349,8 @@
             ]
     best_copy = pltpu.make_async_copy(best_held, best_ref, sems.at[1])
     best_copy.start()
+    for step in range(early, steps):
+        one_group(step, 0)
     pltpu.make_async_copy(hist_held, hist_ref, sems.at[0]).wait()
     best_copy.wait()
 

time: 37.7 us -> 37.7 us (level)
  no operation moved by 1% of the time
where the time goes in v15:
time: 37.7 us; the launch traced here: 37.5 us
  Pallas kernels  13.2 us (35%)
  blocking collectives  10.2 us (27%)
  starting transfers between devices  9.93 us (26%)
  waiting for transfers between devices  2.86 us (8%)
  between operations  1.35 us (4%)
    all_to_all x1, blocking collectives, shards(): gathered = lax.all_to_all(best, ('feat', 'rows'), 0, 0, tiled=True)  10.2 us
    pallas_call x4, Pallas kernels, shards(): pl.pallas_call(functools.partial(accumulate, count, feats, first, last),...  8.98 us
    ppermute x3, starting transfers between devices, exchange_sums(): return lax.ppermute(sums, ('rows', 'feat'), pairs)  5.48 us
    ppermute x3, starting transfers between devices, exchange(): return lax.ppermute(array, 'rows', pairs)  4.45 us
    ppermute x3, waiting for transfers between devices, exchange_sums(): return lax.ppermute(sums, ('rows', 'feat'), pairs)  1.95 us
    pallas_call x1, Pallas kernels, shards(): pl.pallas_call(prepare, out_shape=[jax.ShapeDtypeStruct((DAYS, LANES), BF...  1.85 us
    pallas_call x1, Pallas kernels, shards(): pl.pallas_call(results, out_shape=[hist_shape, best_shape], in_specs=[vme...  1.55 us
    ppermute x3, waiting for transfers between devices, exchange(): return lax.ppermute(array, 'rows', pairs)  0.9 us
  transfers between devices with their start and end apart: 6, of which 3 were waited for; matrix products, arithmetic and copies ran while one was open for 0% of the time, Pallas kernels for 18%

profile of v15, /device:TPU:0, one launch (start us, length us, event | category | flops | bytes accessed | tf_op | source)
XLA Modules:
  0.0 37.5 jit_solution(14263772542076016525)
XLA Ops:
  0.6 1.8 %prepare.1 = (bf16[32,128]{1,0:T(8,128)(2,1)S(1)}, bf16[1024,512]{1,0:T(8,128)(2,1)S(1)}, s32[1,1024]{1,0:T(1,128)S(1)}, s32[1,1024]{1,0:T(1,128)S(1)}, s32[1024...) custom-call(bf16[1024,512]{1,0:T(8,128)(2,1)} %refs_0_.1, s32[1,1024]{1,0:T(1,128)} %bitcast.5, s32[1,1024]{1,0:T(1,128)} %bitcast.6, ...), custom_call_target="tpu_custom_call" | custom-call | tf_op jit(solution)/shard_map/prepare/pallas_call | solution.py:376
  2.5 4.6 %collective-permute-start.2 = (bf16[32,128]{1,0:T(8,128)(2,1)S(1)}, bf16[32,128]{1,0:T(8,128)(2,1)S(1)}, u32[]{:S(2)}, u32[]{:S(2)}) collective-permute-start(bf16[32,128]{1,0:T(8,128)(2,1)S(1)} %get-tuple-element.21.refs_0_), channel_id=1, source_target_pairs={{0,13},{1,12},{2,15},{3,14},{4,9},{5,8},{6,11},{7,10},{8,5},{9,4},... | collective-permute-start | bytes 24584 | tf_op jit(solution)/shard_map/ppermute | solution.py:414
  7.0 0.0 collective-permute-start.1
  7.0 0.9 %collective-permute-start = (bf16[32,128]{1,0:T(8,128)(2,1)S(1)}, bf16[32,128]{1,0:T(8,128)(2,1)S(1)}, u32[]{:S(2)}, u32[]{:S(2)}) collective-permute-start(bf16[32,128]{1,0:T(8,128)(2,1)S(1)} %get-tuple-element.21.refs_0_), channel_id=1, source_target_pairs={{0,5},{1,4},{2,7},{3,6},{4,1},{5,0},{6,3},{7,2},{8,13},{9,12},{10,... | collective-permute-start | bytes 24584 | tf_op jit(solution)/shard_map/ppermute | solution.py:414
  8.6 0.5 %local_terms.1 = (f32[32,1024]{1,0:T(8,128)S(1)}, bf16[256,128]{1,0:T(8,128)(2,1)S(1)}, bf16[256,128]{1,0:T(8,128)(2,1)S(1)}, bf16[256,128]{1,0:T(8,128)(2,1)S(1)}, bf16[256,128]{1,0:T(8,128)(2,1)S(1)}) custom-call(bf16[1024,512]{1,0:T(8,128)(2,1)S(1)} %get-tuple-element.22.counts_ref, s32[1,1024]{1,0:T(1,128)S(1)} %get-tuple-element.23.region_ref, ...), custom_call_target="tpu_custom_call" | custom-call | tf_op jit(solution)/shard_map/local_terms/pallas_call | solution.py:397
  9.1 0.0 collective-permute-done.2.refs_3_
  9.1 1.9 %collective-permute-done.1.refs_2_ = bf16[32,128]{1,0:T(8,128)(2,1)S(1)} collective-permute-done((bf16[32,128]{1,0:T(8,128)(2,1)S(1)}, bf16[32,128]{1,0:T(8,128)(2,1)S(1)}, u32[]{:S(2)}, u32[]{:S(2)}) %collective-permute-start.1) | collective-permute-done | bytes 8224 | tf_op jit(solution)/shard_map/ppermute | solution.py:414
  11.1 0.0 collective-permute-done.refs_1_
  11.1 0.3 columns.1
  11.4 2.4 %collective-permute-start.5 = (bf16[288,128]{1,0:T(8,128)(2,1)S(1)}, bf16[288,128]{1,0:T(8,128)(2,1)S(1)}, u32[]{:S(2)}, u32[]{:S(2)}) collective-permute-start(bf16[288,128]{1,0:T(8,128)(2,1)S(1)} %get-tuple-element.34), channel_id=1, source_target_pairs={{0,8},{4,12},{8,0},{12,4},{1,9},{5,13},{9,1},{13,5},{2,10},{6,14},... | collective-permute-start | bytes 221192 | tf_op jit(solution)/shard_map/ppermute | solution.py:374
  13.8 0.0 collective-permute-start.4
  13.8 2.1 %collective-permute-start.3 = (bf16[288,128]{1,0:T(8,128)(2,1)S(1)}, bf16[288,128]{1,0:T(8,128)(2,1)S(1)}, u32[]{:S(2)}, u32[]{:S(2)}) collective-permute-start(bf16[288,128]{1,0:T(8,128)(2,1)S(1)} %get-tuple-element.32), channel_id=1, source_target_pairs={{0,12},{4,8},{8,4},{12,0},{1,13},{5,9},{9,5},{13,1},{2,14},{6,10},... | collective-permute-start | bytes 221192 | tf_op jit(solution)/shard_map/ppermute | solution.py:374
  15.9 2.0 %accumulate_0.1.refs_1_ = f32[32,64,256]{2,1,0:T(8,128)S(1)} custom-call(bf16[288,128]{1,0:T(8,128)(2,1)S(1)} %get-tuple-element.35.refs_0_), custom_call_target="tpu_custom_call" | custom-call | tf_op jit(solution)/shard_map/accumulate_0/pallas_call | solution.py:450
  17.9 0.2 collective-permute-done.5.refs_0_
  18.1 2.1 %accumulate_1.1.refs_1_ = f32[32,64,256]{2,1,0:T(8,128)S(1)} custom-call(bf16[288,128]{1,0:T(8,128)(2,1)S(1)} %collective-permute-done.5.refs_0_, f32[32,64,256]{2,1,0:T(8,128)S(1)} %accumulate_0.1.refs_1_), custom_call_target="tpu_custom_call", output_to_operand_aliasing={{}: (1, {})} | custom-call | tf_op jit(solution)/shard_map/accumulate_1/pallas_call | solution.py:450
  20.2 0.7 %collective-permute-done.4.refs_0_ = bf16[288,128]{1,0:T(8,128)(2,1)S(1)} collective-permute-done((bf16[288,128]{1,0:T(8,128)(2,1)S(1)}, bf16[288,128]{1,0:T(8,128)(2,1)S(1)}, u32[]{:S(2)}, u32[]{:S(2)}) %collective-permute-start.4) | collective-permute-done | bytes 73760 | tf_op jit(solution)/shard_map/ppermute | solution.py:374
  20.9 2.1 %accumulate_2.1.refs_1_ = f32[32,64,256]{2,1,0:T(8,128)S(1)} custom-call(bf16[288,128]{1,0:T(8,128)(2,1)S(1)} %collective-permute-done.4.refs_0_, f32[32,64,256]{2,1,0:T(8,128)S(1)} %accumulate_1.1.refs_1_), custom_call_target="tpu_custom_call", output_to_operand_aliasing={{}: (1, {})} | custom-call | tf_op jit(solution)/shard_map/accumulate_2/pallas_call | solution.py:450
  23.0 0.0 collective-permute-done.3.refs_0_
  23.0 2.7 %accumulate_3.1 = (f32[32,64,256]{2,1,0:T(8,128)S(1)}, f32[16,8,128]{2,1,0:T(8,128)S(1)}) custom-call(bf16[288,128]{1,0:T(8,128)(2,1)S(1)} %collective-permute-done.3.refs_0_, f32[32,64,256]{2,1,0:T(8,128)S(1)} %accumulate_2.1.refs_1_), custom_call_target="tpu_custom_call", output_to_operand_aliasing={{0}: (1, {})} | custom-call | tf_op jit(solution)/shard_map/accumulate_3/pallas_call | solution.py:450
  25.8 10.2 %all_to_all.5.packed_ref = f32[16,8,128]{2,1,0:T(8,128)S(1)} all-to-all(f32[16,8,128]{2,1,0:T(8,128)S(1)} %get-tuple-element.37), channel_id=1, replica_groups=mesh['groups'=2,'rows'=4,'feat'=4] {'feat','rows'}, dimensions={0} | all-to-all | bytes 131072 | tf_op jit(solution)/shard_map/all_to_all | solution.py:462
  35.9 1.5 %results.1 = (f32[32,64,256]{2,1,0:T(8,128)}, f32[16,32,32]{2,1,0:T(8,128)}) custom-call(f32[32,64,256]{2,1,0:T(8,128)S(1)} %get-tuple-element.36.left_ref, f32[16,8,128]{2,1,0:T(8,128)S(1)} %all_to_all.5.packed_ref), custom_call_target="tpu_custom_call" | custom-call | tf_op jit(solution)/shard_map/results/pallas_call | solution.py:464
Async XLA Ops:
  2.5 6.6 %collective-permute-start.2 = (bf16[32,128]{1,0:T(8,128)(2,1)S(1)}, bf16[32,128]{1,0:T(8,128)(2,1)S(1)}, u32[]{:S(2)}, u32[]{:S(2)}) collective-permute-start(bf16[32,128]{1,0:T(8,128)(2,1)S(1)} %get-tuple-element.21.refs_0_), channel_id=1, source_target_pairs={{0,13},{1,12},{2,15},{3,14},{4,9},{5,8},{6,11},{7,10},{8,5},{9,4},... | collective-permute-start | bytes 24584 | tf_op jit(solution)/shard_map/ppermute | solution.py:414
  7.0 4.0 %collective-permute-start.1 = (bf16[32,128]{1,0:T(8,128)(2,1)S(1)}, bf16[32,128]{1,0:T(8,128)(2,1)S(1)}, u32[]{:S(2)}, u32[]{:S(2)}) collective-permute-start(bf16[32,128]{1,0:T(8,128)(2,1)S(1)} %get-tuple-element.21.refs_0_), channel_id=1, source_target_pairs={{0,9},{1,8},{2,11},{3,10},{4,13},{5,12},{6,15},{7,14},{8,1},{9,0},... | collective-permute-start | bytes 24584 | tf_op jit(solution)/shard_map/ppermute | solution.py:414
  7.0 4.0 %collective-permute-start = (bf16[32,128]{1,0:T(8,128)(2,1)S(1)}, bf16[32,128]{1,0:T(8,128)(2,1)S(1)}, u32[]{:S(2)}, u32[]{:S(2)}) collective-permute-start(bf16[32,128]{1,0:T(8,128)(2,1)S(1)} %get-tuple-element.21.refs_0_), channel_id=1, source_target_pairs={{0,5},{1,4},{2,7},{3,6},{4,1},{5,0},{6,3},{7,2},{8,13},{9,12},{10,... | collective-permute-start | bytes 24584 | tf_op jit(solution)/shard_map/ppermute | solution.py:414
  11.4 6.6 %collective-permute-start.5 = (bf16[288,128]{1,0:T(8,128)(2,1)S(1)}, bf16[288,128]{1,0:T(8,128)(2,1)S(1)}, u32[]{:S(2)}, u32[]{:S(2)}) collective-permute-start(bf16[288,128]{1,0:T(8,128)(2,1)S(1)} %get-tuple-element.34), channel_id=1, source_target_pairs={{0,8},{4,12},{8,0},{12,4},{1,9},{5,13},{9,1},{13,5},{2,10},{6,14},... | collective-permute-start | bytes 221192 | tf_op jit(solution)/shard_map/ppermute | solution.py:374
  13.8 7.1 %collective-permute-start.4 = (bf16[288,128]{1,0:T(8,128)(2,1)S(1)}, bf16[288,128]{1,0:T(8,128)(2,1)S(1)}, u32[]{:S(2)}, u32[]{:S(2)}) collective-permute-start(bf16[288,128]{1,0:T(8,128)(2,1)S(1)} %get-tuple-element.33), channel_id=1, source_target_pairs={{0,4},{4,0},{8,12},{12,8},{1,5},{5,1},{9,13},{13,9},{2,6},{6,2},{1... | collective-permute-start | bytes 221192 | tf_op jit(solution)/shard_map/ppermute | solution.py:374
  13.8 9.2 %collective-permute-start.3 = (bf16[288,128]{1,0:T(8,128)(2,1)S(1)}, bf16[288,128]{1,0:T(8,128)(2,1)S(1)}, u32[]{:S(2)}, u32[]{:S(2)}) collective-permute-start(bf16[288,128]{1,0:T(8,128)(2,1)S(1)} %get-tuple-element.32), channel_id=1, source_target_pairs={{0,12},{4,8},{8,4},{12,0},{1,13},{5,9},{9,5},{13,1},{2,14},{6,10},... | collective-permute-start | bytes 221192 | tf_op jit(solution)/shard_map/ppermute | solution.py:374
